TPU v7x, 128 devices: a whole 4x4x4 slice. The times are simulated.
128 devices in a mesh: ctx: 16 (over x_hi, z, core), head: 8 (over x_lo, y).
Axes of the slice: x: 4 (x_hi: 2, x_lo: 2; x = x_hi * 2 + x_lo), y: 4, z: 4, core: 2. Of those that a mesh axis runs over, the one named last changes fastest.
Arguments:
- hidden_in: bfloat16 [6144, 4096], P('ctx', 'head'), may hold values from -6 to 6
- query: bfloat16 [6144, 4096], P('ctx', 'head'), may hold values from -5 to 5
- key: bfloat16 [6144, 1024], P('ctx', 'head'), may hold values from -5 to 5
- value: bfloat16 [6144, 1024], P('ctx', 'head'), may hold values from -6 to 6
- out_weight: bfloat16 [4096, 4096], P('head'), may hold values from -0.09375 to 0.09375
- grad_out: bfloat16 [6144, 4096], P('ctx', 'head'), may hold values from -3 to 3
- span_map: int32 [16, 2], replicated, may hold values from 0 to 31, as said below
- owner_map: int32 [3, 16], replicated, may hold values from 0 to 15, as said below
Outputs:
- key_weight_gradient: float32 [4096, 1024], P('ctx', 'head')
- value_weight_gradient: float32 [4096, 1024], P('ctx', 'head')
- out_weight_grad: float32 [4096, 4096], P('head', 'ctx')
Inputs may be any that keep to these rules, and one draw needn't show every extreme that they name: `span_map`: row i names a span c of the first 16 spans and then the span 32 - 1 - c; the first column is a permutation of 0 to 15. `owner_map`: each row is a permutation of 0 to 16 - 1.
All inputs are finite; a program needn't handle non-finite values.
Results may differ from a plain program's by a relative error of at most 0.0095.
Values may be sent and summed in bfloat16 or wider, within the bound.
No kernel may reach another device: no remote copies, remote signals or barrier semaphores. Data moves between devices by JAX's collectives and lax.ppermute only.
A program may use at most 128 MiB of HBM per device.

v0:
```python
import jax
import jax.numpy as jnp
from jax import lax
from jax.sharding import PartitionSpec as P

MODEL_WIDTH = 4096
HEAD_SIZE = 128


def shifted(value, axis, by):
    peers = lax.axis_size(axis)
    return lax.ppermute(value, axis, [(i, (i + by) % peers) for i in range(peers)])


def row_positions(span_map, first_row, row_count, half_rows):
    span_list = span_map.reshape(-1)
    global_rows = first_row + jnp.arange(row_count, dtype=jnp.int32)
    slot_index = global_rows // half_rows
    slot_match = slot_index[:, None] == jnp.arange(span_list.shape[0], dtype=jnp.int32)[None, :]
    span_ids = jnp.sum(jnp.where(slot_match, span_list[None, :], 0), axis=1)
    return span_ids * half_rows + global_rows % half_rows


def owner_order(owner_map, cycle_size):
    blocks = jnp.arange(cycle_size, dtype=jnp.int32)
    owner_match = owner_map[:, None, :] == blocks[None, :, None]
    return jnp.sum(jnp.where(owner_match, blocks[None, None, :], 0), axis=2)


def head_scores(query_heads, key_rows, own_positions, key_positions):
    kv_local = query_heads.shape[1]
    key_heads = key_rows.reshape(key_rows.shape[0], kv_local, HEAD_SIZE)
    scores = HEAD_SIZE ** (-0.5) * jnp.einsum(
        "tkgd,skd->kgts", query_heads, key_heads, preferred_element_type=jnp.float32
    )
    visible = key_positions[None, :] <= own_positions[:, None]
    return (jnp.where(visible, scores, -1e30), visible)


def per_device(hidden_in, query, key, value, out_weight, grad_out, span_map, owner_map):
    cycle_size = lax.axis_size("ctx")
    device_index = lax.axis_index("ctx")
    tok_rows = query.shape[0]
    half_rows = tok_rows // 2
    kv_local = key.shape[1] // HEAD_SIZE
    query_local = query.shape[1] // HEAD_SIZE
    group_extent = query_local // kv_local
    kv_width = kv_local * HEAD_SIZE
    hidden_full, grad_full = (
        lax.all_gather(hidden_in, "head", axis=1, tiled=True),
        lax.all_gather(grad_out, "head", axis=1, tiled=True),
    )
    d_attn = lax.dot_general(
        grad_full, out_weight, (((1,), (1,)), ((), ())), preferred_element_type=jnp.float32
    ).astype(jnp.bfloat16)
    query_heads = query.reshape(tok_rows, kv_local, group_extent, HEAD_SIZE)
    d_heads = d_attn.reshape(tok_rows, kv_local, group_extent, HEAD_SIZE)
    own_positions = row_positions(span_map, device_index * tok_rows, tok_rows, half_rows)
    stat_shape = (kv_local, group_extent, tok_rows)
    key_piece = lax.all_gather(key, "ctx", axis=0, tiled=True)
    row_top = jnp.full(stat_shape, -1e30, jnp.float32)
    key_positions = row_positions(span_map, jnp.int32(0), key_piece.shape[0], half_rows)
    masked_scores, visible = head_scores(query_heads, key_piece, own_positions, key_positions)
    new_top = jnp.maximum(row_top, jnp.max(masked_scores, axis=3))
    fresh = jnp.sum(jnp.where(visible, jnp.exp(masked_scores - new_top[..., None]), 0.0), axis=3)
    row_lse = new_top + jnp.log(fresh)
    key_piece = lax.all_gather(key, "ctx", axis=0, tiled=True)
    value_piece = lax.all_gather(value, "ctx", axis=0, tiled=True)
    key_positions = row_positions(span_map, jnp.int32(0), key_piece.shape[0], half_rows)
    masked_scores, visible = head_scores(query_heads, key_piece, own_positions, key_positions)
    prob_low = jnp.where(visible, jnp.exp(masked_scores - row_lse[..., None]), 0.0).astype(
        jnp.bfloat16
    )
    value_heads = value_piece.reshape(value_piece.shape[0], kv_local, HEAD_SIZE)
    output_sum = jnp.einsum(
        "kgts,skd->tkgd", prob_low, value_heads, preferred_element_type=jnp.float32
    )
    attn = output_sum.reshape(tok_rows, query_local * HEAD_SIZE).astype(jnp.bfloat16)
    row_delta = jnp.sum(
        (d_attn.astype(jnp.float32) * attn.astype(jnp.float32)).reshape(
            tok_rows, kv_local, group_extent, HEAD_SIZE
        ),
        axis=3,
    )
    row_delta = jnp.transpose(row_delta, (1, 2, 0))

    def gradients(key_rows, value_rows, key_positions):
        piece_rows = key_rows.shape[0]
        masked_scores, visible = head_scores(query_heads, key_rows, own_positions, key_positions)
        prob_rows = jnp.where(visible, jnp.exp(masked_scores - row_lse[..., None]), 0.0)
        prob_low = prob_rows.astype(jnp.bfloat16)
        value_heads = value_rows.reshape(piece_rows, kv_local, HEAD_SIZE)
        d_probs = jnp.einsum(
            "tkgd,skd->kgts", d_heads, value_heads, preferred_element_type=jnp.float32
        )
        d_scores = (prob_rows * (d_probs - row_delta[..., None])).astype(jnp.bfloat16)
        d_key_part = HEAD_SIZE ** (-0.5) * jnp.einsum(
            "kgts,tkgd->skd", d_scores, query_heads, preferred_element_type=jnp.float32
        )
        d_value_part = jnp.einsum(
            "kgts,tkgd->skd", prob_low, d_heads, preferred_element_type=jnp.float32
        )
        return (
            d_key_part.reshape(piece_rows, kv_width),
            d_value_part.reshape(piece_rows, kv_width),
        )

    def single_turn(turn_index, state_now):
        key_rows, value_rows, key_gradient_total, value_gradient_total = state_now
        source_device = (device_index - turn_index) % cycle_size
        key_positions = row_positions(span_map, source_device * tok_rows, tok_rows, half_rows)
        part_key, part_value = gradients(key_rows, value_rows, key_positions)
        key_rows, value_rows = shifted((key_rows, value_rows), "ctx", 1)
        key_gradient_total, value_gradient_total = shifted(
            (key_gradient_total + part_key, value_gradient_total + part_value), "ctx", 1
        )
        return (key_rows, value_rows, key_gradient_total, value_gradient_total)

    zero_rows = jnp.zeros((tok_rows, kv_width), jnp.float32)
    moved_keys, moved_values, key_gradient_total, value_gradient_total = lax.fori_loop(
        0, cycle_size, single_turn, (key, value, zero_rows, zero_rows)
    )
    d_both = jnp.concatenate([key_gradient_total, value_gradient_total], axis=1)
    grad_both = lax.dot_general(
        hidden_full.astype(jnp.float32),
        d_both,
        (((0,), (0,)), ((), ())),
        preferred_element_type=jnp.float32,
        precision=lax.Precision.HIGHEST,
    )
    block_extent = MODEL_WIDTH // cycle_size
    inverse_permutation = owner_order(owner_map, cycle_size)
    ordered_key = jnp.take(
        grad_both[:, :kv_width].reshape(cycle_size, block_extent, kv_width),
        inverse_permutation[0],
        axis=0,
    ).reshape(MODEL_WIDTH, kv_width)
    ordered_value = jnp.take(
        grad_both[:, kv_width:].reshape(cycle_size, block_extent, kv_width),
        inverse_permutation[1],
        axis=0,
    ).reshape(MODEL_WIDTH, kv_width)
    out_grad = lax.dot_general(
        attn, grad_full, (((0,), (0,)), ((), ())), preferred_element_type=jnp.float32
    )
    ordered_out = jnp.take(
        out_grad.reshape(query_local * HEAD_SIZE, cycle_size, block_extent),
        inverse_permutation[2],
        axis=1,
    ).reshape(query_local * HEAD_SIZE, MODEL_WIDTH)
    key_weight_gradient, value_weight_gradient, out_weight_grad = (
        lax.psum_scatter(ordered_key, "ctx", scatter_dimension=0, tiled=True),
        lax.psum_scatter(ordered_value, "ctx", scatter_dimension=0, tiled=True),
        lax.psum_scatter(ordered_out, "ctx", scatter_dimension=1, tiled=True),
    )
    return (key_weight_gradient, value_weight_gradient, out_weight_grad)


def solution(mesh):
    return jax.shard_map(
        per_device,
        mesh=mesh,
        in_specs=(
            P("ctx", "head"),
            P("ctx", "head"),
            P("ctx", "head"),
            P("ctx", "head"),
            P("head", None),
            P("ctx", "head"),
            P(),
            P(),
        ),
        out_specs=(P("ctx", "head"), P("ctx", "head"), P("head", "ctx")),
        check_vma=False,
    )
```

profile of v0, /device:TPU:0, one launch (start us, length us, event | category | flops | bytes accessed | tf_op | source)
XLA Modules:
  0.0 666.7 jit_solution(16358440405091356605)
XLA Ops:
  18.7 2.8 broadcast_compare_fusion.1
  21.5 38.5 %all-gather.5.cloned.1.call-done = bf16[6144,128]{1,0:T(8,128)(2,1)} async-done(((bf16[384,128]{1,0:T(8,128)(2,1)}), bf16[6144,128]{1,0:T(8,128)(2,1)}) %all-gather.5.cloned.1.call-update) | async-done | bytes 1572880 | tf_op jit(solution)/shard_map/all_gather | solution.py:60
  59.9 15.7 %fusion.31 = (f32[4,384]{1,0:T(4,128)S(1)}, f32[6144,384,4]{1,0,2:T(8,128)}) fusion(pred[384,6144]{0,1:T(8,128)(4,1)S(1)} %broadcast_compare_fusion.1, bf16[6144,128]{1,0:T(8,128)(2,1)} %all-gather.5.cloned.1.call-done, bf16[384,512]{1,0:T(8,128)(2,1)S(1)} %copy-done.6), kind=kOutput, calls=%fused_computation.41 | convolution fusion | flops 2444229120 | bytes 42080256 | tf_op jit(solution)/shard_map/tkgd,skd->kgts/dot_general | solution.py:33
  75.6 16.8 %select_reduce_fusion.1 = f32[4,384]{1,0:T(4,128)S(1)} fusion(f32[6144,384,4]{1,0,2:T(8,128)} %get-tuple-element.426, f32[4,384]{1,0:T(4,128)S(1)} %broadcast_maximum_fusion, pred[384,6144]{0,1:T(8,128)(4,1)S(1)} %broadcast_compare_fusion.1), kind=kLoop, calls=%fused_computation.40 | loop fusion | flops 47184384 | bytes 40120320 | tf_op jit(solution)/shard_map/reduce_sum | solution.py:65
  93.0 13.0 %all-gather.9.cloned.1.call-done = bf16[6144,128]{0,1:T(8,128)(2,1)} async-done(((bf16[384,128]{0,1:T(8,128)(2,1)}), bf16[6144,128]{0,1:T(8,128)(2,1)}) %all-gather.9.cloned.1.call-update) | async-done | bytes 1572880 | tf_op jit(solution)/shard_map/all_gather | solution.py:68
  105.9 15.7 %fusion.39 = bf16[4,384,128]{1,2,0:T(8,128)(2,1)S(1)} fusion(f32[6144,384,4]{1,0,2:T(8,128)} %get-tuple-element.426, f32[4,384]{1,0:T(4,128)} %log_add_fusion, pred[384,6144]{0,1:T(8,128)(4,1)S(1)} %broadcast_compare_fusion.1, bf16[6144,128]{0,1:T(8,128)(2,1)} %all-gather.9.cloned.1.call-done), kind=kOutput, calls=%fused_computation.51 | convolution fusion | flops 2463301632 | bytes 42080256 | tf_op jit(solution)/shard_map/kgts,skd->tkgd/dot_general | solution.py:75
  121.8 28.9 %all-gather.7.cloned.1.call-done = bf16[384,4096]{1,0:T(8,128)(2,1)} async-done(((bf16[384,512]{1,0:T(8,128)(2,1)}), bf16[384,4096]{1,0:T(8,128)(2,1)}) %all-gather.7.cloned.1.call-update) | async-done | bytes 3145744 | tf_op jit(solution)/shard_map/all_gather | solution.py:51
  150.8 5.0 convert_multiply_fusion
  156.8 3.4 copy.65
  160.2 6.6 fusion.69
  166.8 7.9 %gather_fusion = f32[16,512,256]{2,1,0:T(8,128)} fusion(f32[512,16,256]{2,0,1:T(8,128)} %fusion.69, s32[1024]{0:T(1024)} %pad_clamp_fusion), kind=kCustom, calls=%fused_computation.2 | custom fusion | bytes 16777280 | tf_op jit(solution)/shard_map/jit(_take)/gather | solution.py:146
  174.7 9.3 %copy.67 = f32[512,16,256]{0,2,1:T(8,128)} copy(f32[512,16,256]{2,0,1:T(8,128)} %bitcast.186) | data formatting | bytes 16777216 | tf_op jit(solution)/shard_map/jit(_take)/gather | solution.py:146
  184.1 5.9 bitcast_select_fusion.2
  191.1 311.8 %while.23 = (s32[]{:T(128)}, bf16[384,128]{1,0:T(8,128)(2,1)S(1)}, bf16[384,128]{1,0:T(8,128)(2,1)S(1)}, f32[384,128]{1,0:T(8,128)}, f32[384,128]{1,0:T(8,128)S(...) while((s32[]{:T(128)}, bf16[384,128]{1,0:T(8,128)(2,1)S(1)}, ...), condition=%wide.wide.region_7.8_spmd, body=%wide.wide.region_5.7_spmd.sunk | while | flops 609036672 | bytes 12704850 | solution.py:120
  192.0 1.7 fusion.106
  193.7 2.5 fusion.107
  200.7 7.6 %collective-permute-done = bf16[384,128]{1,0:T(8,128)(2,1)S(1)} collective-permute-done((bf16[384,128]{1,0:T(8,128)(2,1)}, bf16[384,128]{1,0:T(8,128)(2,1)S(1)}, u32[]{:S(2)}, u32[]{:S(2)}) %collective-permute-start) | collective-permute-done | bytes 98336 | tf_op jit(solution)/shard_map/while/body/eval_jaxpr/ppermute | solution.py:12
  210.3 1.7 fusion.106
  212.0 2.5 fusion.107
  215.7 10.9 %collective-permute-done = bf16[384,128]{1,0:T(8,128)(2,1)S(1)} collective-permute-done((bf16[384,128]{1,0:T(8,128)(2,1)}, bf16[384,128]{1,0:T(8,128)(2,1)S(1)}, u32[]{:S(2)}, u32[]{:S(2)}) %collective-permute-start) | collective-permute-done | bytes 98336 | tf_op jit(solution)/shard_map/while/body/eval_jaxpr/ppermute | solution.py:12
  230.3 2.5 fusion.107
  233.9 15.6 %collective-permute-done = bf16[384,128]{1,0:T(8,128)(2,1)S(1)} collective-permute-done((bf16[384,128]{1,0:T(8,128)(2,1)}, bf16[384,128]{1,0:T(8,128)(2,1)S(1)}, u32[]{:S(2)}, u32[]{:S(2)}) %collective-permute-start) | collective-permute-done | bytes 98336 | tf_op jit(solution)/shard_map/while/body/eval_jaxpr/ppermute | solution.py:12
  249.6 3.2 collective-permute-done.1
  253.7 1.7 fusion.106
  255.4 2.5 fusion.107
  259.0 19.9 %collective-permute-done = bf16[384,128]{1,0:T(8,128)(2,1)S(1)} collective-permute-done((bf16[384,128]{1,0:T(8,128)(2,1)}, bf16[384,128]{1,0:T(8,128)(2,1)S(1)}, u32[]{:S(2)}, u32[]{:S(2)}) %collective-permute-start) | collective-permute-done | bytes 98336 | tf_op jit(solution)/shard_map/while/body/eval_jaxpr/ppermute | solution.py:12
  279.0 2.8 collective-permute-done.1
  284.4 2.5 fusion.107
  288.0 11.0 %collective-permute-done = bf16[384,128]{1,0:T(8,128)(2,1)S(1)} collective-permute-done((bf16[384,128]{1,0:T(8,128)(2,1)}, bf16[384,128]{1,0:T(8,128)(2,1)S(1)}, u32[]{:S(2)}, u32[]{:S(2)}) %collective-permute-start) | collective-permute-done | bytes 98336 | tf_op jit(solution)/shard_map/while/body/eval_jaxpr/ppermute | solution.py:12
  299.0 3.2 collective-permute-done.1
  303.1 1.7 fusion.106
  304.8 2.5 fusion.107
  308.5 10.9 %collective-permute-done = bf16[384,128]{1,0:T(8,128)(2,1)S(1)} collective-permute-done((bf16[384,128]{1,0:T(8,128)(2,1)}, bf16[384,128]{1,0:T(8,128)(2,1)S(1)}, u32[]{:S(2)}, u32[]{:S(2)}) %collective-permute-start) | collective-permute-done | bytes 98336 | tf_op jit(solution)/shard_map/while/body/eval_jaxpr/ppermute | solution.py:12
  323.1 2.5 fusion.107
  326.8 10.9 %collective-permute-done = bf16[384,128]{1,0:T(8,128)(2,1)S(1)} collective-permute-done((bf16[384,128]{1,0:T(8,128)(2,1)}, bf16[384,128]{1,0:T(8,128)(2,1)S(1)}, u32[]{:S(2)}, u32[]{:S(2)}) %collective-permute-start) | collective-permute-done | bytes 98336 | tf_op jit(solution)/shard_map/while/body/eval_jaxpr/ppermute | solution.py:12
  339.6 1.7 fusion.106
  341.3 2.5 fusion.107
  345.0 10.9 %collective-permute-done = bf16[384,128]{1,0:T(8,128)(2,1)S(1)} collective-permute-done((bf16[384,128]{1,0:T(8,128)(2,1)}, bf16[384,128]{1,0:T(8,128)(2,1)S(1)}, u32[]{:S(2)}, u32[]{:S(2)}) %collective-permute-start) | collective-permute-done | bytes 98336 | tf_op jit(solution)/shard_map/while/body/eval_jaxpr/ppermute | solution.py:12
  359.6 2.5 fusion.107
  363.3 10.9 %collective-permute-done = bf16[384,128]{1,0:T(8,128)(2,1)S(1)} collective-permute-done((bf16[384,128]{1,0:T(8,128)(2,1)}, bf16[384,128]{1,0:T(8,128)(2,1)S(1)}, u32[]{:S(2)}, u32[]{:S(2)}) %collective-permute-start) | collective-permute-done | bytes 98336 | tf_op jit(solution)/shard_map/while/body/eval_jaxpr/ppermute | solution.py:12
  376.1 1.7 fusion.106
  377.8 2.5 fusion.107
  381.5 10.9 %collective-permute-done = bf16[384,128]{1,0:T(8,128)(2,1)S(1)} collective-permute-done((bf16[384,128]{1,0:T(8,128)(2,1)}, bf16[384,128]{1,0:T(8,128)(2,1)S(1)}, u32[]{:S(2)}, u32[]{:S(2)}) %collective-permute-start) | collective-permute-done | bytes 98336 | tf_op jit(solution)/shard_map/while/body/eval_jaxpr/ppermute | solution.py:12
  396.1 2.5 fusion.107
  399.7 10.9 %collective-permute-done = bf16[384,128]{1,0:T(8,128)(2,1)S(1)} collective-permute-done((bf16[384,128]{1,0:T(8,128)(2,1)}, bf16[384,128]{1,0:T(8,128)(2,1)S(1)}, u32[]{:S(2)}, u32[]{:S(2)}) %collective-permute-start) | collective-permute-done | bytes 98336 | tf_op jit(solution)/shard_map/while/body/eval_jaxpr/ppermute | solution.py:12
  414.3 2.5 fusion.107
  418.0 10.9 %collective-permute-done = bf16[384,128]{1,0:T(8,128)(2,1)S(1)} collective-permute-done((bf16[384,128]{1,0:T(8,128)(2,1)}, bf16[384,128]{1,0:T(8,128)(2,1)S(1)}, u32[]{:S(2)}, u32[]{:S(2)}) %collective-permute-start) | collective-permute-done | bytes 98336 | tf_op jit(solution)/shard_map/while/body/eval_jaxpr/ppermute | solution.py:12
  432.5 2.5 fusion.107
  436.2 10.9 %collective-permute-done = bf16[384,128]{1,0:T(8,128)(2,1)S(1)} collective-permute-done((bf16[384,128]{1,0:T(8,128)(2,1)}, bf16[384,128]{1,0:T(8,128)(2,1)S(1)}, u32[]{:S(2)}, u32[]{:S(2)}) %collective-permute-start) | collective-permute-done | bytes 98336 | tf_op jit(solution)/shard_map/while/body/eval_jaxpr/ppermute | solution.py:12
  450.8 2.5 fusion.107
  454.5 10.9 %collective-permute-done = bf16[384,128]{1,0:T(8,128)(2,1)S(1)} collective-permute-done((bf16[384,128]{1,0:T(8,128)(2,1)}, bf16[384,128]{1,0:T(8,128)(2,1)S(1)}, u32[]{:S(2)}, u32[]{:S(2)}) %collective-permute-start) | collective-permute-done | bytes 98336 | tf_op jit(solution)/shard_map/while/body/eval_jaxpr/ppermute | solution.py:12
  469.0 2.5 fusion.107
  472.7 10.9 %collective-permute-done = bf16[384,128]{1,0:T(8,128)(2,1)S(1)} collective-permute-done((bf16[384,128]{1,0:T(8,128)(2,1)}, bf16[384,128]{1,0:T(8,128)(2,1)S(1)}, u32[]{:S(2)}, u32[]{:S(2)}) %collective-permute-start) | collective-permute-done | bytes 98336 | tf_op jit(solution)/shard_map/while/body/eval_jaxpr/ppermute | solution.py:12
  487.3 2.5 fusion.107
  491.0 10.9 %collective-permute-done = bf16[384,128]{1,0:T(8,128)(2,1)S(1)} collective-permute-done((bf16[384,128]{1,0:T(8,128)(2,1)}, bf16[384,128]{1,0:T(8,128)(2,1)S(1)}, u32[]{:S(2)}, u32[]{:S(2)}) %collective-permute-start) | collective-permute-done | bytes 98336 | tf_op jit(solution)/shard_map/while/body/eval_jaxpr/ppermute | solution.py:12
  502.9 5.5 convolution_bitcast_fusion.1
  508.4 1.7 fusion.68
  510.1 1.9 copy.73
  512.0 2.4 gather_fusion.2
  517.6 1.8 copy.72
  519.5 2.3 gather_fusion.1
  523.4 2.1 copy.68
  525.4 59.4 %reduce-scatter.6.cloned.1.call-done = f32[256,128]{1,0:T(8,128)} async-done(((f32[4096,128]{1,0:T(8,128)}), f32[256,128]{1,0:T(8,128)}) %reduce-scatter.6.cloned.1.call-update) | async-done | bytes 131088 | tf_op jit(solution)/shard_map/reduce_scatter | solution.py:153
  584.8 75.0 %reduce-scatter.4.cloned.1.call-done = f32[256,128]{1,0:T(8,128)} async-done(((f32[4096,128]{1,0:T(8,128)}), f32[256,128]{1,0:T(8,128)}) %reduce-scatter.4.cloned.1.call-update) | async-done | bytes 131088 | tf_op jit(solution)/shard_map/reduce_scatter | solution.py:152
  (305 shorter events, 86.5 us)
Async XLA Ops:
  7.2 52.7 %all-gather.5.cloned.1.call-start = ((), (), s32[]{:S(2)}) async-start(), calls=%async_computation.3 | async-start | bytes 1671168 | tf_op jit(solution)/shard_map/all_gather | solution.py:60
  9.7 96.2 %all-gather.9.cloned.1.call-start = ((), (), s32[]{:S(2)}) async-start(), calls=%async_computation.5 | async-start | bytes 1671168 | tf_op jit(solution)/shard_map/all_gather | solution.py:68
  10.5 140.2 %all-gather.7.cloned.1.call-start = ((), (), s32[]{:S(2)}) async-start(), calls=%async_computation.4 | async-start | bytes 3538944 | tf_op jit(solution)/shard_map/all_gather | solution.py:51
  11.3 491.7 %all-gather.11.cloned.1.call-start = ((), (), s32[]{:S(2)}) async-start(), calls=%async_computation.6 | async-start | bytes 3538944 | tf_op jit(solution)/shard_map/all_gather | solution.py:50
  11.9 511.5 %reduce-scatter.8.cloned.1.call-start = ((), (), s32[]{:S(2)}) async-start(), calls=%async_computation.9 | async-start | bytes 8912896 | tf_op jit(solution)/shard_map/reduce_scatter | solution.py:154
  190.0 394.8 %reduce-scatter.6.cloned.1.call-start = ((), (), s32[]{:S(2)}) async-start(), calls=%async_computation.8 | async-start | bytes 2228224 | tf_op jit(solution)/shard_map/reduce_scatter | solution.py:153
  196.2 13.1 %collective-permute-start.2 = (f32[384,128]{1,0:T(8,128)}, f32[384,128]{1,0:T(8,128)}, u32[]{:S(2)}, u32[]{:S(2)}) collective-permute-start(f32[384,128]{1,0:T(8,128)} %fusion.107), channel_id=1, source_target_pairs={{0,8},{8,16},{16,24},{24,32},{32,40},{40,48},{48,56},{56,64},{64,7... | collective-permute-start | bytes 589832 | tf_op jit(solution)/shard_map/while/body/eval_jaxpr/ppermute | solution.py:12
  197.4 12.0 %collective-permute-start.3 = (f32[384,128]{1,0:T(8,128)}, f32[384,128]{1,0:T(8,128)S(1)}, u32[]{:S(2)}, u32[]{:S(2)}) collective-permute-start(f32[384,128]{1,0:T(8,128)} %fusion.108), channel_id=1, source_target_pairs={{0,8},{8,16},{16,24},{24,32},{32,40},{40,48},{48,56},{56,64},{64,7... | collective-permute-start | bytes 589832 | tf_op jit(solution)/shard_map/while/body/eval_jaxpr/ppermute | solution.py:12
  214.5 13.1 %collective-permute-start.2 = (f32[384,128]{1,0:T(8,128)}, f32[384,128]{1,0:T(8,128)}, u32[]{:S(2)}, u32[]{:S(2)}) collective-permute-start(f32[384,128]{1,0:T(8,128)} %fusion.107), channel_id=1, source_target_pairs={{0,8},{8,16},{16,24},{24,32},{32,40},{40,48},{48,56},{56,64},{64,7... | collective-permute-start | bytes 589832 | tf_op jit(solution)/shard_map/while/body/eval_jaxpr/ppermute | solution.py:12
  215.7 12.0 %collective-permute-start.3 = (f32[384,128]{1,0:T(8,128)}, f32[384,128]{1,0:T(8,128)S(1)}, u32[]{:S(2)}, u32[]{:S(2)}) collective-permute-start(f32[384,128]{1,0:T(8,128)} %fusion.108), channel_id=1, source_target_pairs={{0,8},{8,16},{16,24},{24,32},{32,40},{40,48},{48,56},{56,64},{64,7... | collective-permute-start | bytes 589832 | tf_op jit(solution)/shard_map/while/body/eval_jaxpr/ppermute | solution.py:12
  215.7 10.9 %collective-permute-start = (bf16[384,128]{1,0:T(8,128)(2,1)}, bf16[384,128]{1,0:T(8,128)(2,1)S(1)}, u32[]{:S(2)}, u32[]{:S(2)}) collective-permute-start(bf16[384,128]{1,0:T(8,128)(2,1)} %copy.87), channel_id=1, source_target_pairs={{0,8},{8,16},{16,24},{24,32},{32,40},{40,48},{48,56},{56,64},{64,7... | collective-permute-start | bytes 294920 | tf_op jit(solution)/shard_map/while/body/eval_jaxpr/ppermute | solution.py:12
  215.7 12.0 %collective-permute-start.1 = (bf16[384,128]{1,0:T(8,128)(2,1)S(1)}, bf16[384,128]{1,0:T(8,128)(2,1)S(1)}, u32[]{:S(2)}, u32[]{:S(2)}) collective-permute-start(bf16[384,128]{1,0:T(8,128)(2,1)S(1)} %copy.88), channel_id=1, source_target_pairs={{0,8},{8,16},{16,24},{24,32},{32,40},{40,48},{48,56},{56,64},{64,7... | collective-permute-start | bytes 294920 | tf_op jit(solution)/shard_map/while/body/eval_jaxpr/ppermute | solution.py:12
  232.8 20.0 %collective-permute-start.2 = (f32[384,128]{1,0:T(8,128)}, f32[384,128]{1,0:T(8,128)}, u32[]{:S(2)}, u32[]{:S(2)}) collective-permute-start(f32[384,128]{1,0:T(8,128)} %fusion.107), channel_id=1, source_target_pairs={{0,8},{8,16},{16,24},{24,32},{32,40},{40,48},{48,56},{56,64},{64,7... | collective-permute-start | bytes 589832 | tf_op jit(solution)/shard_map/while/body/eval_jaxpr/ppermute | solution.py:12
  233.9 18.8 %collective-permute-start.3 = (f32[384,128]{1,0:T(8,128)}, f32[384,128]{1,0:T(8,128)S(1)}, u32[]{:S(2)}, u32[]{:S(2)}) collective-permute-start(f32[384,128]{1,0:T(8,128)} %fusion.108), channel_id=1, source_target_pairs={{0,8},{8,16},{16,24},{24,32},{32,40},{40,48},{48,56},{56,64},{64,7... | collective-permute-start | bytes 589832 | tf_op jit(solution)/shard_map/while/body/eval_jaxpr/ppermute | solution.py:12
  233.9 15.6 %collective-permute-start = (bf16[384,128]{1,0:T(8,128)(2,1)}, bf16[384,128]{1,0:T(8,128)(2,1)S(1)}, u32[]{:S(2)}, u32[]{:S(2)}) collective-permute-start(bf16[384,128]{1,0:T(8,128)(2,1)} %copy.87), channel_id=1, source_target_pairs={{0,8},{8,16},{16,24},{24,32},{32,40},{40,48},{48,56},{56,64},{64,7... | collective-permute-start | bytes 294920 | tf_op jit(solution)/shard_map/while/body/eval_jaxpr/ppermute | solution.py:12
  233.9 18.8 %collective-permute-start.1 = (bf16[384,128]{1,0:T(8,128)(2,1)S(1)}, bf16[384,128]{1,0:T(8,128)(2,1)S(1)}, u32[]{:S(2)}, u32[]{:S(2)}) collective-permute-start(bf16[384,128]{1,0:T(8,128)(2,1)S(1)} %copy.88), channel_id=1, source_target_pairs={{0,8},{8,16},{16,24},{24,32},{32,40},{40,48},{48,56},{56,64},{64,7... | collective-permute-start | bytes 294920 | tf_op jit(solution)/shard_map/while/body/eval_jaxpr/ppermute | solution.py:12
  257.9 23.9 %collective-permute-start.2 = (f32[384,128]{1,0:T(8,128)}, f32[384,128]{1,0:T(8,128)}, u32[]{:S(2)}, u32[]{:S(2)}) collective-permute-start(f32[384,128]{1,0:T(8,128)} %fusion.107), channel_id=1, source_target_pairs={{0,8},{8,16},{16,24},{24,32},{32,40},{40,48},{48,56},{56,64},{64,7... | collective-permute-start | bytes 589832 | tf_op jit(solution)/shard_map/while/body/eval_jaxpr/ppermute | solution.py:12
  259.0 22.7 %collective-permute-start.3 = (f32[384,128]{1,0:T(8,128)}, f32[384,128]{1,0:T(8,128)S(1)}, u32[]{:S(2)}, u32[]{:S(2)}) collective-permute-start(f32[384,128]{1,0:T(8,128)} %fusion.108), channel_id=1, source_target_pairs={{0,8},{8,16},{16,24},{24,32},{32,40},{40,48},{48,56},{56,64},{64,7... | collective-permute-start | bytes 589832 | tf_op jit(solution)/shard_map/while/body/eval_jaxpr/ppermute | solution.py:12
  259.0 19.9 %collective-permute-start = (bf16[384,128]{1,0:T(8,128)(2,1)}, bf16[384,128]{1,0:T(8,128)(2,1)S(1)}, u32[]{:S(2)}, u32[]{:S(2)}) collective-permute-start(bf16[384,128]{1,0:T(8,128)(2,1)} %copy.87), channel_id=1, source_target_pairs={{0,8},{8,16},{16,24},{24,32},{32,40},{40,48},{48,56},{56,64},{64,7... | collective-permute-start | bytes 294920 | tf_op jit(solution)/shard_map/while/body/eval_jaxpr/ppermute | solution.py:12
  259.0 22.7 %collective-permute-start.1 = (bf16[384,128]{1,0:T(8,128)(2,1)S(1)}, bf16[384,128]{1,0:T(8,128)(2,1)S(1)}, u32[]{:S(2)}, u32[]{:S(2)}) collective-permute-start(bf16[384,128]{1,0:T(8,128)(2,1)S(1)} %copy.88), channel_id=1, source_target_pairs={{0,8},{8,16},{16,24},{24,32},{32,40},{40,48},{48,56},{56,64},{64,7... | collective-permute-start | bytes 294920 | tf_op jit(solution)/shard_map/while/body/eval_jaxpr/ppermute | solution.py:12
  286.9 15.4 %collective-permute-start.2 = (f32[384,128]{1,0:T(8,128)}, f32[384,128]{1,0:T(8,128)}, u32[]{:S(2)}, u32[]{:S(2)}) collective-permute-start(f32[384,128]{1,0:T(8,128)} %fusion.107), channel_id=1, source_target_pairs={{0,8},{8,16},{16,24},{24,32},{32,40},{40,48},{48,56},{56,64},{64,7... | collective-permute-start | bytes 589832 | tf_op jit(solution)/shard_map/while/body/eval_jaxpr/ppermute | solution.py:12
  288.0 14.2 %collective-permute-start.3 = (f32[384,128]{1,0:T(8,128)}, f32[384,128]{1,0:T(8,128)S(1)}, u32[]{:S(2)}, u32[]{:S(2)}) collective-permute-start(f32[384,128]{1,0:T(8,128)} %fusion.108), channel_id=1, source_target_pairs={{0,8},{8,16},{16,24},{24,32},{32,40},{40,48},{48,56},{56,64},{64,7... | collective-permute-start | bytes 589832 | tf_op jit(solution)/shard_map/while/body/eval_jaxpr/ppermute | solution.py:12
  288.0 11.0 %collective-permute-start = (bf16[384,128]{1,0:T(8,128)(2,1)}, bf16[384,128]{1,0:T(8,128)(2,1)S(1)}, u32[]{:S(2)}, u32[]{:S(2)}) collective-permute-start(bf16[384,128]{1,0:T(8,128)(2,1)} %copy.87), channel_id=1, source_target_pairs={{0,8},{8,16},{16,24},{24,32},{32,40},{40,48},{48,56},{56,64},{64,7... | collective-permute-start | bytes 294920 | tf_op jit(solution)/shard_map/while/body/eval_jaxpr/ppermute | solution.py:12
  288.0 14.2 %collective-permute-start.1 = (bf16[384,128]{1,0:T(8,128)(2,1)S(1)}, bf16[384,128]{1,0:T(8,128)(2,1)S(1)}, u32[]{:S(2)}, u32[]{:S(2)}) collective-permute-start(bf16[384,128]{1,0:T(8,128)(2,1)S(1)} %copy.88), channel_id=1, source_target_pairs={{0,8},{8,16},{16,24},{24,32},{32,40},{40,48},{48,56},{56,64},{64,7... | collective-permute-start | bytes 294920 | tf_op jit(solution)/shard_map/while/body/eval_jaxpr/ppermute | solution.py:12
  307.3 13.1 %collective-permute-start.2 = (f32[384,128]{1,0:T(8,128)}, f32[384,128]{1,0:T(8,128)}, u32[]{:S(2)}, u32[]{:S(2)}) collective-permute-start(f32[384,128]{1,0:T(8,128)} %fusion.107), channel_id=1, source_target_pairs={{0,8},{8,16},{16,24},{24,32},{32,40},{40,48},{48,56},{56,64},{64,7... | collective-permute-start | bytes 589832 | tf_op jit(solution)/shard_map/while/body/eval_jaxpr/ppermute | solution.py:12
  308.5 12.0 %collective-permute-start.3 = (f32[384,128]{1,0:T(8,128)}, f32[384,128]{1,0:T(8,128)S(1)}, u32[]{:S(2)}, u32[]{:S(2)}) collective-permute-start(f32[384,128]{1,0:T(8,128)} %fusion.108), channel_id=1, source_target_pairs={{0,8},{8,16},{16,24},{24,32},{32,40},{40,48},{48,56},{56,64},{64,7... | collective-permute-start | bytes 589832 | tf_op jit(solution)/shard_map/while/body/eval_jaxpr/ppermute | solution.py:12
  308.5 12.0 %collective-permute-start.1 = (bf16[384,128]{1,0:T(8,128)(2,1)S(1)}, bf16[384,128]{1,0:T(8,128)(2,1)S(1)}, u32[]{:S(2)}, u32[]{:S(2)}) collective-permute-start(bf16[384,128]{1,0:T(8,128)(2,1)S(1)} %copy.88), channel_id=1, source_target_pairs={{0,8},{8,16},{16,24},{24,32},{32,40},{40,48},{48,56},{56,64},{64,7... | collective-permute-start | bytes 294920 | tf_op jit(solution)/shard_map/while/body/eval_jaxpr/ppermute | solution.py:12
  325.6 13.1 %collective-permute-start.2 = (f32[384,128]{1,0:T(8,128)}, f32[384,128]{1,0:T(8,128)}, u32[]{:S(2)}, u32[]{:S(2)}) collective-permute-start(f32[384,128]{1,0:T(8,128)} %fusion.107), channel_id=1, source_target_pairs={{0,8},{8,16},{16,24},{24,32},{32,40},{40,48},{48,56},{56,64},{64,7... | collective-permute-start | bytes 589832 | tf_op jit(solution)/shard_map/while/body/eval_jaxpr/ppermute | solution.py:12
  326.7 12.0 %collective-permute-start.3 = (f32[384,128]{1,0:T(8,128)}, f32[384,128]{1,0:T(8,128)S(1)}, u32[]{:S(2)}, u32[]{:S(2)}) collective-permute-start(f32[384,128]{1,0:T(8,128)} %fusion.108), channel_id=1, source_target_pairs={{0,8},{8,16},{16,24},{24,32},{32,40},{40,48},{48,56},{56,64},{64,7... | collective-permute-start | bytes 589832 | tf_op jit(solution)/shard_map/while/body/eval_jaxpr/ppermute | solution.py:12
  326.7 10.9 %collective-permute-start = (bf16[384,128]{1,0:T(8,128)(2,1)}, bf16[384,128]{1,0:T(8,128)(2,1)S(1)}, u32[]{:S(2)}, u32[]{:S(2)}) collective-permute-start(bf16[384,128]{1,0:T(8,128)(2,1)} %copy.87), channel_id=1, source_target_pairs={{0,8},{8,16},{16,24},{24,32},{32,40},{40,48},{48,56},{56,64},{64,7... | collective-permute-start | bytes 294920 | tf_op jit(solution)/shard_map/while/body/eval_jaxpr/ppermute | solution.py:12
  326.8 12.0 %collective-permute-start.1 = (bf16[384,128]{1,0:T(8,128)(2,1)S(1)}, bf16[384,128]{1,0:T(8,128)(2,1)S(1)}, u32[]{:S(2)}, u32[]{:S(2)}) collective-permute-start(bf16[384,128]{1,0:T(8,128)(2,1)S(1)} %copy.88), channel_id=1, source_target_pairs={{0,8},{8,16},{16,24},{24,32},{32,40},{40,48},{48,56},{56,64},{64,7... | collective-permute-start | bytes 294920 | tf_op jit(solution)/shard_map/while/body/eval_jaxpr/ppermute | solution.py:12
  343.8 13.1 %collective-permute-start.2 = (f32[384,128]{1,0:T(8,128)}, f32[384,128]{1,0:T(8,128)}, u32[]{:S(2)}, u32[]{:S(2)}) collective-permute-start(f32[384,128]{1,0:T(8,128)} %fusion.107), channel_id=1, source_target_pairs={{0,8},{8,16},{16,24},{24,32},{32,40},{40,48},{48,56},{56,64},{64,7... | collective-permute-start | bytes 589832 | tf_op jit(solution)/shard_map/while/body/eval_jaxpr/ppermute | solution.py:12
  345.0 12.0 %collective-permute-start.3 = (f32[384,128]{1,0:T(8,128)}, f32[384,128]{1,0:T(8,128)S(1)}, u32[]{:S(2)}, u32[]{:S(2)}) collective-permute-start(f32[384,128]{1,0:T(8,128)} %fusion.108), channel_id=1, source_target_pairs={{0,8},{8,16},{16,24},{24,32},{32,40},{40,48},{48,56},{56,64},{64,7... | collective-permute-start | bytes 589832 | tf_op jit(solution)/shard_map/while/body/eval_jaxpr/ppermute | solution.py:12
  345.0 10.9 %collective-permute-start = (bf16[384,128]{1,0:T(8,128)(2,1)}, bf16[384,128]{1,0:T(8,128)(2,1)S(1)}, u32[]{:S(2)}, u32[]{:S(2)}) collective-permute-start(bf16[384,128]{1,0:T(8,128)(2,1)} %copy.87), channel_id=1, source_target_pairs={{0,8},{8,16},{16,24},{24,32},{32,40},{40,48},{48,56},{56,64},{64,7... | collective-permute-start | bytes 294920 | tf_op jit(solution)/shard_map/while/body/eval_jaxpr/ppermute | solution.py:12
  345.0 12.0 %collective-permute-start.1 = (bf16[384,128]{1,0:T(8,128)(2,1)S(1)}, bf16[384,128]{1,0:T(8,128)(2,1)S(1)}, u32[]{:S(2)}, u32[]{:S(2)}) collective-permute-start(bf16[384,128]{1,0:T(8,128)(2,1)S(1)} %copy.88), channel_id=1, source_target_pairs={{0,8},{8,16},{16,24},{24,32},{32,40},{40,48},{48,56},{56,64},{64,7... | collective-permute-start | bytes 294920 | tf_op jit(solution)/shard_map/while/body/eval_jaxpr/ppermute | solution.py:12
  362.1 13.1 %collective-permute-start.2 = (f32[384,128]{1,0:T(8,128)}, f32[384,128]{1,0:T(8,128)}, u32[]{:S(2)}, u32[]{:S(2)}) collective-permute-start(f32[384,128]{1,0:T(8,128)} %fusion.107), channel_id=1, source_target_pairs={{0,8},{8,16},{16,24},{24,32},{32,40},{40,48},{48,56},{56,64},{64,7... | collective-permute-start | bytes 589832 | tf_op jit(solution)/shard_map/while/body/eval_jaxpr/ppermute | solution.py:12
  363.2 12.0 %collective-permute-start.3 = (f32[384,128]{1,0:T(8,128)}, f32[384,128]{1,0:T(8,128)S(1)}, u32[]{:S(2)}, u32[]{:S(2)}) collective-permute-start(f32[384,128]{1,0:T(8,128)} %fusion.108), channel_id=1, source_target_pairs={{0,8},{8,16},{16,24},{24,32},{32,40},{40,48},{48,56},{56,64},{64,7... | collective-permute-start | bytes 589832 | tf_op jit(solution)/shard_map/while/body/eval_jaxpr/ppermute | solution.py:12
  363.2 10.9 %collective-permute-start = (bf16[384,128]{1,0:T(8,128)(2,1)}, bf16[384,128]{1,0:T(8,128)(2,1)S(1)}, u32[]{:S(2)}, u32[]{:S(2)}) collective-permute-start(bf16[384,128]{1,0:T(8,128)(2,1)} %copy.87), channel_id=1, source_target_pairs={{0,8},{8,16},{16,24},{24,32},{32,40},{40,48},{48,56},{56,64},{64,7... | collective-permute-start | bytes 294920 | tf_op jit(solution)/shard_map/while/body/eval_jaxpr/ppermute | solution.py:12
  363.2 12.0 %collective-permute-start.1 = (bf16[384,128]{1,0:T(8,128)(2,1)S(1)}, bf16[384,128]{1,0:T(8,128)(2,1)S(1)}, u32[]{:S(2)}, u32[]{:S(2)}) collective-permute-start(bf16[384,128]{1,0:T(8,128)(2,1)S(1)} %copy.88), channel_id=1, source_target_pairs={{0,8},{8,16},{16,24},{24,32},{32,40},{40,48},{48,56},{56,64},{64,7... | collective-permute-start | bytes 294920 | tf_op jit(solution)/shard_map/while/body/eval_jaxpr/ppermute | solution.py:12
  380.3 13.1 %collective-permute-start.2 = (f32[384,128]{1,0:T(8,128)}, f32[384,128]{1,0:T(8,128)}, u32[]{:S(2)}, u32[]{:S(2)}) collective-permute-start(f32[384,128]{1,0:T(8,128)} %fusion.107), channel_id=1, source_target_pairs={{0,8},{8,16},{16,24},{24,32},{32,40},{40,48},{48,56},{56,64},{64,7... | collective-permute-start | bytes 589832 | tf_op jit(solution)/shard_map/while/body/eval_jaxpr/ppermute | solution.py:12
  381.5 12.0 %collective-permute-start.3 = (f32[384,128]{1,0:T(8,128)}, f32[384,128]{1,0:T(8,128)S(1)}, u32[]{:S(2)}, u32[]{:S(2)}) collective-permute-start(f32[384,128]{1,0:T(8,128)} %fusion.108), channel_id=1, source_target_pairs={{0,8},{8,16},{16,24},{24,32},{32,40},{40,48},{48,56},{56,64},{64,7... | collective-permute-start | bytes 589832 | tf_op jit(solution)/shard_map/while/body/eval_jaxpr/ppermute | solution.py:12
  381.5 12.0 %collective-permute-start.1 = (bf16[384,128]{1,0:T(8,128)(2,1)S(1)}, bf16[384,128]{1,0:T(8,128)(2,1)S(1)}, u32[]{:S(2)}, u32[]{:S(2)}) collective-permute-start(bf16[384,128]{1,0:T(8,128)(2,1)S(1)} %copy.88), channel_id=1, source_target_pairs={{0,8},{8,16},{16,24},{24,32},{32,40},{40,48},{48,56},{56,64},{64,7... | collective-permute-start | bytes 294920 | tf_op jit(solution)/shard_map/while/body/eval_jaxpr/ppermute | solution.py:12
  398.6 13.1 %collective-permute-start.2 = (f32[384,128]{1,0:T(8,128)}, f32[384,128]{1,0:T(8,128)}, u32[]{:S(2)}, u32[]{:S(2)}) collective-permute-start(f32[384,128]{1,0:T(8,128)} %fusion.107), channel_id=1, source_target_pairs={{0,8},{8,16},{16,24},{24,32},{32,40},{40,48},{48,56},{56,64},{64,7... | collective-permute-start | bytes 589832 | tf_op jit(solution)/shard_map/while/body/eval_jaxpr/ppermute | solution.py:12
  399.7 12.0 %collective-permute-start.3 = (f32[384,128]{1,0:T(8,128)}, f32[384,128]{1,0:T(8,128)S(1)}, u32[]{:S(2)}, u32[]{:S(2)}) collective-permute-start(f32[384,128]{1,0:T(8,128)} %fusion.108), channel_id=1, source_target_pairs={{0,8},{8,16},{16,24},{24,32},{32,40},{40,48},{48,56},{56,64},{64,7... | collective-permute-start | bytes 589832 | tf_op jit(solution)/shard_map/while/body/eval_jaxpr/ppermute | solution.py:12
  399.7 10.9 %collective-permute-start = (bf16[384,128]{1,0:T(8,128)(2,1)}, bf16[384,128]{1,0:T(8,128)(2,1)S(1)}, u32[]{:S(2)}, u32[]{:S(2)}) collective-permute-start(bf16[384,128]{1,0:T(8,128)(2,1)} %copy.87), channel_id=1, source_target_pairs={{0,8},{8,16},{16,24},{24,32},{32,40},{40,48},{48,56},{56,64},{64,7... | collective-permute-start | bytes 294920 | tf_op jit(solution)/shard_map/while/body/eval_jaxpr/ppermute | solution.py:12
  399.7 12.0 %collective-permute-start.1 = (bf16[384,128]{1,0:T(8,128)(2,1)S(1)}, bf16[384,128]{1,0:T(8,128)(2,1)S(1)}, u32[]{:S(2)}, u32[]{:S(2)}) collective-permute-start(bf16[384,128]{1,0:T(8,128)(2,1)S(1)} %copy.88), channel_id=1, source_target_pairs={{0,8},{8,16},{16,24},{24,32},{32,40},{40,48},{48,56},{56,64},{64,7... | collective-permute-start | bytes 294920 | tf_op jit(solution)/shard_map/while/body/eval_jaxpr/ppermute | solution.py:12
  416.8 13.1 %collective-permute-start.2 = (f32[384,128]{1,0:T(8,128)}, f32[384,128]{1,0:T(8,128)}, u32[]{:S(2)}, u32[]{:S(2)}) collective-permute-start(f32[384,128]{1,0:T(8,128)} %fusion.107), channel_id=1, source_target_pairs={{0,8},{8,16},{16,24},{24,32},{32,40},{40,48},{48,56},{56,64},{64,7... | collective-permute-start | bytes 589832 | tf_op jit(solution)/shard_map/while/body/eval_jaxpr/ppermute | solution.py:12
  418.0 12.0 %collective-permute-start.3 = (f32[384,128]{1,0:T(8,128)}, f32[384,128]{1,0:T(8,128)S(1)}, u32[]{:S(2)}, u32[]{:S(2)}) collective-permute-start(f32[384,128]{1,0:T(8,128)} %fusion.108), channel_id=1, source_target_pairs={{0,8},{8,16},{16,24},{24,32},{32,40},{40,48},{48,56},{56,64},{64,7... | collective-permute-start | bytes 589832 | tf_op jit(solution)/shard_map/while/body/eval_jaxpr/ppermute | solution.py:12
  418.0 12.0 %collective-permute-start.1 = (bf16[384,128]{1,0:T(8,128)(2,1)S(1)}, bf16[384,128]{1,0:T(8,128)(2,1)S(1)}, u32[]{:S(2)}, u32[]{:S(2)}) collective-permute-start(bf16[384,128]{1,0:T(8,128)(2,1)S(1)} %copy.88), channel_id=1, source_target_pairs={{0,8},{8,16},{16,24},{24,32},{32,40},{40,48},{48,56},{56,64},{64,7... | collective-permute-start | bytes 294920 | tf_op jit(solution)/shard_map/while/body/eval_jaxpr/ppermute | solution.py:12
  435.0 13.1 %collective-permute-start.2 = (f32[384,128]{1,0:T(8,128)}, f32[384,128]{1,0:T(8,128)}, u32[]{:S(2)}, u32[]{:S(2)}) collective-permute-start(f32[384,128]{1,0:T(8,128)} %fusion.107), channel_id=1, source_target_pairs={{0,8},{8,16},{16,24},{24,32},{32,40},{40,48},{48,56},{56,64},{64,7... | collective-permute-start | bytes 589832 | tf_op jit(solution)/shard_map/while/body/eval_jaxpr/ppermute | solution.py:12
  436.2 12.0 %collective-permute-start.3 = (f32[384,128]{1,0:T(8,128)}, f32[384,128]{1,0:T(8,128)S(1)}, u32[]{:S(2)}, u32[]{:S(2)}) collective-permute-start(f32[384,128]{1,0:T(8,128)} %fusion.108), channel_id=1, source_target_pairs={{0,8},{8,16},{16,24},{24,32},{32,40},{40,48},{48,56},{56,64},{64,7... | collective-permute-start | bytes 589832 | tf_op jit(solution)/shard_map/while/body/eval_jaxpr/ppermute | solution.py:12
  436.2 10.9 %collective-permute-start = (bf16[384,128]{1,0:T(8,128)(2,1)}, bf16[384,128]{1,0:T(8,128)(2,1)S(1)}, u32[]{:S(2)}, u32[]{:S(2)}) collective-permute-start(bf16[384,128]{1,0:T(8,128)(2,1)} %copy.87), channel_id=1, source_target_pairs={{0,8},{8,16},{16,24},{24,32},{32,40},{40,48},{48,56},{56,64},{64,7... | collective-permute-start | bytes 294920 | tf_op jit(solution)/shard_map/while/body/eval_jaxpr/ppermute | solution.py:12
  436.2 12.0 %collective-permute-start.1 = (bf16[384,128]{1,0:T(8,128)(2,1)S(1)}, bf16[384,128]{1,0:T(8,128)(2,1)S(1)}, u32[]{:S(2)}, u32[]{:S(2)}) collective-permute-start(bf16[384,128]{1,0:T(8,128)(2,1)S(1)} %copy.88), channel_id=1, source_target_pairs={{0,8},{8,16},{16,24},{24,32},{32,40},{40,48},{48,56},{56,64},{64,7... | collective-permute-start | bytes 294920 | tf_op jit(solution)/shard_map/while/body/eval_jaxpr/ppermute | solution.py:12
  453.3 13.1 %collective-permute-start.2 = (f32[384,128]{1,0:T(8,128)}, f32[384,128]{1,0:T(8,128)}, u32[]{:S(2)}, u32[]{:S(2)}) collective-permute-start(f32[384,128]{1,0:T(8,128)} %fusion.107), channel_id=1, source_target_pairs={{0,8},{8,16},{16,24},{24,32},{32,40},{40,48},{48,56},{56,64},{64,7... | collective-permute-start | bytes 589832 | tf_op jit(solution)/shard_map/while/body/eval_jaxpr/ppermute | solution.py:12
  454.5 12.0 %collective-permute-start.3 = (f32[384,128]{1,0:T(8,128)}, f32[384,128]{1,0:T(8,128)S(1)}, u32[]{:S(2)}, u32[]{:S(2)}) collective-permute-start(f32[384,128]{1,0:T(8,128)} %fusion.108), channel_id=1, source_target_pairs={{0,8},{8,16},{16,24},{24,32},{32,40},{40,48},{48,56},{56,64},{64,7... | collective-permute-start | bytes 589832 | tf_op jit(solution)/shard_map/while/body/eval_jaxpr/ppermute | solution.py:12
  454.5 12.0 %collective-permute-start.1 = (bf16[384,128]{1,0:T(8,128)(2,1)S(1)}, bf16[384,128]{1,0:T(8,128)(2,1)S(1)}, u32[]{:S(2)}, u32[]{:S(2)}) collective-permute-start(bf16[384,128]{1,0:T(8,128)(2,1)S(1)} %copy.88), channel_id=1, source_target_pairs={{0,8},{8,16},{16,24},{24,32},{32,40},{40,48},{48,56},{56,64},{64,7... | collective-permute-start | bytes 294920 | tf_op jit(solution)/shard_map/while/body/eval_jaxpr/ppermute | solution.py:12
  471.5 13.1 %collective-permute-start.2 = (f32[384,128]{1,0:T(8,128)}, f32[384,128]{1,0:T(8,128)}, u32[]{:S(2)}, u32[]{:S(2)}) collective-permute-start(f32[384,128]{1,0:T(8,128)} %fusion.107), channel_id=1, source_target_pairs={{0,8},{8,16},{16,24},{24,32},{32,40},{40,48},{48,56},{56,64},{64,7... | collective-permute-start | bytes 589832 | tf_op jit(solution)/shard_map/while/body/eval_jaxpr/ppermute | solution.py:12
  472.7 12.0 %collective-permute-start.3 = (f32[384,128]{1,0:T(8,128)}, f32[384,128]{1,0:T(8,128)S(1)}, u32[]{:S(2)}, u32[]{:S(2)}) collective-permute-start(f32[384,128]{1,0:T(8,128)} %fusion.108), channel_id=1, source_target_pairs={{0,8},{8,16},{16,24},{24,32},{32,40},{40,48},{48,56},{56,64},{64,7... | collective-permute-start | bytes 589832 | tf_op jit(solution)/shard_map/while/body/eval_jaxpr/ppermute | solution.py:12
  472.7 10.9 %collective-permute-start = (bf16[384,128]{1,0:T(8,128)(2,1)}, bf16[384,128]{1,0:T(8,128)(2,1)S(1)}, u32[]{:S(2)}, u32[]{:S(2)}) collective-permute-start(bf16[384,128]{1,0:T(8,128)(2,1)} %copy.87), channel_id=1, source_target_pairs={{0,8},{8,16},{16,24},{24,32},{32,40},{40,48},{48,56},{56,64},{64,7... | collective-permute-start | bytes 294920 | tf_op jit(solution)/shard_map/while/body/eval_jaxpr/ppermute | solution.py:12
  472.7 12.0 %collective-permute-start.1 = (bf16[384,128]{1,0:T(8,128)(2,1)S(1)}, bf16[384,128]{1,0:T(8,128)(2,1)S(1)}, u32[]{:S(2)}, u32[]{:S(2)}) collective-permute-start(bf16[384,128]{1,0:T(8,128)(2,1)S(1)} %copy.88), channel_id=1, source_target_pairs={{0,8},{8,16},{16,24},{24,32},{32,40},{40,48},{48,56},{56,64},{64,7... | collective-permute-start | bytes 294920 | tf_op jit(solution)/shard_map/while/body/eval_jaxpr/ppermute | solution.py:12
  489.8 13.1 %collective-permute-start.2 = (f32[384,128]{1,0:T(8,128)}, f32[384,128]{1,0:T(8,128)}, u32[]{:S(2)}, u32[]{:S(2)}) collective-permute-start(f32[384,128]{1,0:T(8,128)} %fusion.107), channel_id=1, source_target_pairs={{0,8},{8,16},{16,24},{24,32},{32,40},{40,48},{48,56},{56,64},{64,7... | collective-permute-start | bytes 589832 | tf_op jit(solution)/shard_map/while/body/eval_jaxpr/ppermute | solution.py:12
  490.9 12.0 %collective-permute-start.3 = (f32[384,128]{1,0:T(8,128)}, f32[384,128]{1,0:T(8,128)S(1)}, u32[]{:S(2)}, u32[]{:S(2)}) collective-permute-start(f32[384,128]{1,0:T(8,128)} %fusion.108), channel_id=1, source_target_pairs={{0,8},{8,16},{16,24},{24,32},{32,40},{40,48},{48,56},{56,64},{64,7... | collective-permute-start | bytes 589832 | tf_op jit(solution)/shard_map/while/body/eval_jaxpr/ppermute | solution.py:12
  491.0 12.0 %collective-permute-start.1 = (bf16[384,128]{1,0:T(8,128)(2,1)S(1)}, bf16[384,128]{1,0:T(8,128)(2,1)S(1)}, u32[]{:S(2)}, u32[]{:S(2)}) collective-permute-start(bf16[384,128]{1,0:T(8,128)(2,1)S(1)} %copy.88), channel_id=1, source_target_pairs={{0,8},{8,16},{16,24},{24,32},{32,40},{40,48},{48,56},{56,64},{64,7... | collective-permute-start | bytes 294920 | tf_op jit(solution)/shard_map/while/body/eval_jaxpr/ppermute | solution.py:12
  516.1 143.8 %reduce-scatter.4.cloned.1.call-start = ((), (), s32[]{:S(2)}) async-start(), calls=%async_computation.7 | async-start | bytes 2228224 | tf_op jit(solution)/shard_map/reduce_scatter | solution.py:152
  (19 other events, 191.8 us)
Sparse Core Ops, SparseCore 0:
  11.1 48.7 all-gather.4
  62.2 43.7 all-gather.8
  107.6 43.1 all-gather.6
  152.3 43.8 all-gather.10
  200.3 112.1 reduce-scatter.7
  516.2 68.5 reduce-scatter.5
  589.8 70.0 reduce-scatter.3
where the time goes:
time: 668 us; the launch traced here: 667 us
  waiting for transfers between devices  424 us (63%)
  matrix products  134 us (20%)
  local copies, waits for them, and re-layouts  53.4 us (8%)
  other arithmetic  36.9 us (6%)
  between operations  14.3 us (2%)
    ppermute x64, waiting for transfers between devices, shifted(): lax.ppermute(value, axis, [(i, (i + by) % peers) for i in range(peers)])  208 us
    reduce_scatter x1, waiting for transfers between devices, per_device(): lax.psum_scatter(ordered_key, 'ctx', scatter_dimension=0, tiled=True)  75 us
    reduce_scatter x1, waiting for transfers between devices, per_device(): lax.psum_scatter(ordered_value, 'ctx', scatter_dimension=0, tiled=True)  59.4 us
    dot_general x17, matrix products, head_scores(): jnp.einsum('tkgd,skd->kgts', query_heads, key_heads, preferred_element_ty...  42.6 us
    dot_general x16, matrix products, gradients(): jnp.einsum('kgts,tkgd->skd', d_scores, query_heads, preferred_element_typ...  39.9 us
    all_gather x1, waiting for transfers between devices, per_device(): key_piece = lax.all_gather(key, 'ctx', axis=0, tiled=True)  38.5 us
    all_gather x1, waiting for transfers between devices, per_device(): lax.all_gather(grad_out, 'head', axis=1, tiled=True)  28.9 us
    dot_general x16, matrix products, gradients(): jnp.einsum('kgts,tkgd->skd', prob_low, d_heads, preferred_element_type=jn...  18.7 us
  transfers between devices with their start and end apart: 71, of which 37 were waited for; matrix products, arithmetic and copies ran while one was open for 33% of the time, Pallas kernels for 0%

commit v1 on v0

v1 whole, which is shorter than its diff:
```python
import functools

import jax
import jax.numpy as jnp
from jax import lax
from jax.experimental import pallas as pl
from jax.experimental.pallas import tpu as pltpu
from jax.sharding import PartitionSpec as P

MODEL_WIDTH = 4096
HEAD_SIZE = 128
GROUP = 4
SPAN = 192
SLOTS = 32
N_CTX = 16
CHIPS = 8
TOKENS = 384
KEY_BLOCK = 384
KEY_BLOCKS = 16
LANES = GROUP * SPAN
CHUNK = 256
SCALE = HEAD_SIZE ** (-0.5)
EXP2_SCALE = SCALE * 1.4426950408889634
F32 = jnp.float32
BF16 = jnp.bfloat16
VMEM_BYTES = 58 * 1024 * 1024


def ctx_move(value, dx, dz, dc):
    pairs = []
    for i in range(N_CTX):
        x, z, c = i // 8, (i // 2) % 4, i % 2
        pairs.append((i, ((x ^ dx) * 4 + (z + dz) % 4) * 2 + (c ^ dc)))
    return lax.ppermute(value, "ctx", pairs)


def head_move(value, dx, dy):
    pairs = [(i, ((i // 4) ^ dx) * 4 + (i % 4 + dy) % 4) for i in range(8)]
    return lax.ppermute(value, "head", pairs)


def gather_over_head(own):
    across = head_move(own, 1, 0)
    up0 = head_move(own, 0, 1)
    down0 = head_move(own, 0, 3)
    up1 = head_move(across, 0, 1)
    down1 = head_move(across, 0, 3)
    far0 = head_move(up0, 0, 1)
    far1 = head_move(down1, 0, 3)
    return [own, across, up0, down0, up1, down1, far0, far1]


HEAD_STEPS = ((0, 0), (1, 0), (0, 3), (0, 1), (1, 3), (1, 1), (0, 2), (1, 2))


def gather_over_ctx(own):
    pair = jnp.concatenate([own, ctx_move(own, 1, 0, 0)], axis=0)
    mine = [pair] + [ctx_move(pair, 0, step, 0) for step in (1, 3, 2)]
    return mine + [ctx_move(piece, 0, 0, 1) for piece in mine]


CTX_STEPS = tuple((dz, dc) for dc in (0, 1) for dz in (0, 3, 1, 2))


def nt(a, b):
    return lax.dot_general(a, b, (((1,), (1,)), ((), ())), preferred_element_type=F32)


def nn(a, b):
    return lax.dot_general(a, b, (((1,), (0,)), ((), ())), preferred_element_type=F32)


def attention_kernel(ids, spans, q_ref, do_ref, *rest):
    kv_refs, rest = rest[:8], rest[8:]
    attn_ref, own_ref, other_ref, ks, vs, vt, qs, dos, st, tops, slot, acc_k, acc_v = rest
    ctx = ids[0]
    my_x, my_z, my_c = ctx // 8, (ctx // 2) % 4, ctx % 2
    low = spans[ctx, 0]

    for i in range(N_CTX):
        for half in range(2):
            slot[spans[i, half]] = (my_c ^ (i % 2)) * 16 + (i // 2) * 2 + half

    for piece, (dz, dc) in enumerate(CTX_STEPS):
        for dx in range(2):
            source = ((my_x ^ dx) * 4 + (my_z + dz) % 4) * 2 + (my_c ^ dc)
            for half in range(2):
                span = spans[source, half]
                at = pl.ds(pl.multiple_of(span * SPAN, SPAN), SPAN)
                rows = pl.ds((dx * 2 + half) * SPAN, SPAN)
                ks[at, :] = kv_refs[piece][rows, :HEAD_SIZE]
                vs[at, :] = kv_refs[piece][rows, HEAD_SIZE:]
    for half in range(2):
        for h in range(GROUP):
            rows, cols = pl.ds(half * SPAN, SPAN), pl.ds(h * HEAD_SIZE, HEAD_SIZE)
            qs[half, pl.ds(h * SPAN, SPAN), :] = q_ref[rows, cols]
            dos[half, pl.ds(h * SPAN, SPAN), :] = do_ref[rows, cols]

    def key_rows(b):
        return pl.ds(pl.multiple_of(b * KEY_BLOCK, KEY_BLOCK), KEY_BLOCK)

    @pl.loop(0, KEY_BLOCKS)
    def _(b):
        vt[b] = vs[key_rows(b), :].astype(F32).T.astype(BF16)

    lane = lax.broadcasted_iota(jnp.int32, (1, LANES), 1)
    within = lane
    for h in range(1, GROUP):
        within = within - jnp.where(lane >= h * SPAN, SPAN, 0)
    chunks = [pl.ds(at, CHUNK) for at in range(0, LANES, CHUNK)]
    span_of = (low, SLOTS - 1 - low)
    last = (span_of[0] // 2, span_of[1] // 2)

    def tile_index(half, b):
        return b if half == 1 else KEY_BLOCKS - b

    inverse, delta = [], []
    for half in (1, 0):

        def score(b, masked):
            key_block = ks[key_rows(b), :]
            for n, chunk in enumerate(chunks):
                scores = nt(key_block, qs[half, chunk, :])
                if masked:
                    keys = lax.broadcasted_iota(jnp.int32, (KEY_BLOCK, CHUNK), 0) + b * KEY_BLOCK
                    at = span_of[half] * SPAN + within[:, n * CHUNK : (n + 1) * CHUNK]
                    scores = jnp.where(keys > at, -1e30, scores)
                st[tile_index(half, b), :, chunk] = scores
                tops[:, chunk] = jnp.maximum(tops[:, chunk], jnp.max(scores, axis=0, keepdims=True))

        tops[...] = jnp.full((1, LANES), -1e30, F32)

        @pl.loop(0, last[half])
        def _(b):
            score(b, False)

        score(last[half], True)
        top = tops[...]
        acc_v[...] = jnp.zeros((HEAD_SIZE, LANES), F32)
        tops[...] = jnp.zeros((1, LANES), F32)

        @pl.loop(0, last[half] + 1)
        def _(b):
            values_t = vt[b]
            for n, chunk in enumerate(chunks):
                tile = st.at[tile_index(half, b)]
                p = jnp.exp2((tile[:, chunk] - top[:, n * CHUNK : (n + 1) * CHUNK]) * EXP2_SCALE)
                tile[:, chunk] = p
                tops[:, chunk] += jnp.sum(p, axis=0, keepdims=True)
                acc_v[:, chunk] += nn(values_t, p.astype(BF16))

        inv = 1.0 / tops[...]
        attn_t = (acc_v[...] * inv).astype(BF16).astype(F32)
        do_t = dos[half].astype(F32).T
        inverse.insert(0, inv)
        delta.insert(0, jnp.sum(attn_t * do_t, axis=0, keepdims=True))
        attn = attn_t.T.astype(BF16)
        for h in range(GROUP):
            attn_ref[pl.ds(half * SPAN, SPAN), pl.ds(h * HEAD_SIZE, HEAD_SIZE)] = attn[
                h * SPAN : (h + 1) * SPAN
            ]

    def gradients(b, halves):
        value_block = vs[key_rows(b), :]
        d_key = jnp.zeros((KEY_BLOCK, HEAD_SIZE), F32)
        d_value = jnp.zeros((KEY_BLOCK, HEAD_SIZE), F32)
        for half in halves:
            for n, chunk in enumerate(chunks):
                part = slice(n * CHUNK, (n + 1) * CHUNK)
                p = st[tile_index(half, b), :, chunk] * inverse[half][:, part]
                d_p = nt(value_block, dos[half, chunk, :])
                d_s = (p * (d_p - delta[half][:, part])).astype(BF16)
                d_key += nn(d_s, qs[half, chunk, :])
                d_value += nn(p.astype(BF16), dos[half, chunk, :])
        store(b, (d_key * SCALE).astype(BF16), d_value.astype(BF16))

    def store(b, d_key, d_value):
        for n in range(2):
            at = slot[b * 2 + n]
            rows = slice(n * SPAN, (n + 1) * SPAN)

            @pl.when(at < 16)
            def _():
                own_ref[at, :, :HEAD_SIZE] = d_key[rows]
                own_ref[at, :, HEAD_SIZE:] = d_value[rows]

            @pl.when(at >= 16)
            def _():
                other_ref[at - 16, :, :HEAD_SIZE] = d_key[rows]
                other_ref[at - 16, :, HEAD_SIZE:] = d_value[rows]

    @pl.loop(0, last[0] + 1)
    def _(b):
        gradients(b, (0, 1))

    @pl.loop(last[0] + 1, last[1] + 1)
    def _(b):
        gradients(b, (1,))

    @pl.loop(last[1] + 1, KEY_BLOCKS)
    def _(b):
        zero = jnp.zeros((KEY_BLOCK, HEAD_SIZE), BF16)
        store(b, zero, zero)


def smem():
    return pl.BlockSpec(memory_space=pltpu.SMEM)


def vmem():
    return pl.BlockSpec(memory_space=pltpu.VMEM)


def attention(ids, span_map, query, d_attn, kv_pieces):
    part = jax.ShapeDtypeStruct((2 * CHIPS, SPAN, 2 * HEAD_SIZE), BF16)
    return pl.pallas_call(
        attention_kernel,
        out_shape=(jax.ShapeDtypeStruct(query.shape, BF16), part, part),
        in_specs=[smem(), smem()] + [vmem()] * 10,
        out_specs=(vmem(),) * 3,
        scratch_shapes=[
            pltpu.VMEM((KEY_BLOCKS * KEY_BLOCK, HEAD_SIZE), BF16),
            pltpu.VMEM((KEY_BLOCKS * KEY_BLOCK, HEAD_SIZE), BF16),
            pltpu.VMEM((KEY_BLOCKS, HEAD_SIZE, KEY_BLOCK), BF16),
            pltpu.VMEM((2, LANES, HEAD_SIZE), BF16),
            pltpu.VMEM((2, LANES, HEAD_SIZE), BF16),
            pltpu.VMEM((KEY_BLOCKS + 1, KEY_BLOCK, LANES), F32),
            pltpu.VMEM((1, LANES), F32),
            pltpu.SMEM((SLOTS,), jnp.int32),
            pltpu.VMEM((HEAD_SIZE, LANES), F32),
            pltpu.VMEM((HEAD_SIZE, LANES), F32),
        ],
        compiler_params=pltpu.CompilerParams(vmem_limit_bytes=VMEM_BYTES),
        cost_estimate=pl.CostEstimate(
            flops=13_000_000_000, bytes_accessed=8_000_000, transcendentals=5_000_000
        ),
        name="attention",
    )(ids, span_map, query, d_attn, *kv_pieces)


def out_grad_kernel(ids, owners, attn_ref, *rest):
    pieces, (own_ref, other_ref) = rest[:8], rest[8:]
    my_x, my_y, my_c = ids[1] // 4, ids[1] % 4, ids[0] % 2
    attn_t = attn_ref[...].astype(F32).T.astype(BF16)
    for piece, (dx, dy) in zip(pieces, HEAD_STEPS):
        source = (my_x ^ dx) * 4 + (my_y + dy) % 4
        for half in range(2):
            owner = owners[2, source * 2 + half]
            block = nn(attn_t, piece[:, pl.ds(half * 256, 256)]).astype(BF16)

            @pl.when(owner % 2 == my_c)
            def _():
                own_ref[owner // 2] = block

            @pl.when(owner % 2 != my_c)
            def _():
                other_ref[owner // 2] = block


def out_gradient(ids, owner_map, attn, pieces):
    part = jax.ShapeDtypeStruct((CHIPS, 512, 256), BF16)
    return pl.pallas_call(
        out_grad_kernel,
        out_shape=(part, part),
        in_specs=[smem(), smem()] + [vmem()] * 9,
        out_specs=(vmem(),) * 2,
        compiler_params=pltpu.CompilerParams(vmem_limit_bytes=VMEM_BYTES),
        cost_estimate=pl.CostEstimate(
            flops=1_600_000_000, bytes_accessed=8_000_000, transcendentals=0
        ),
        name="out_gradient",
    )(ids, owner_map, attn, *pieces)


def kv_grad_kernel(ids, owners, parts_ref, hidden_ref, own_ref, other_ref):
    my_c = ids[0] % 2
    total = jnp.sum(parts_ref[...].astype(F32), axis=0)
    high = total.astype(BF16)
    rest = (total - high.astype(F32)).astype(BF16)

    for source in range(8):
        for half in range(2):
            columns = hidden_ref[source, :, pl.ds(half * 256, 256)].astype(F32).T.astype(BF16)
            block = (nn(columns, high) + nn(columns, rest)).astype(BF16)
            for n in range(2):
                owner = owners[n, source * 2 + half]
                lanes = slice(n * HEAD_SIZE, (n + 1) * HEAD_SIZE)

                @pl.when(owner % 2 == my_c)
                def _():
                    own_ref[owner // 2, :, lanes] = block[:, lanes]

                @pl.when(owner % 2 != my_c)
                def _():
                    other_ref[owner // 2, :, lanes] = block[:, lanes]


def kv_gradient(ids, owner_map, parts, hidden):
    part = jax.ShapeDtypeStruct((CHIPS, 256, 2 * HEAD_SIZE), BF16)
    return pl.pallas_call(
        kv_grad_kernel,
        out_shape=(part, part),
        in_specs=[smem(), smem(), vmem(), vmem()],
        out_specs=(vmem(),) * 2,
        compiler_params=pltpu.CompilerParams(vmem_limit_bytes=VMEM_BYTES),
        cost_estimate=pl.CostEstimate(
            flops=1_600_000_000, bytes_accessed=7_000_000, transcendentals=0
        ),
        name="kv_gradient",
    )(ids, owner_map, parts, hidden)


def chip_sum(own, other):
    arrived = ctx_move(other, 0, 0, 1)
    return (own.astype(F32) + arrived.astype(F32)).astype(BF16)


SAME_CORE = [[c + 2 * chip for chip in range(CHIPS)] for c in range(2)]


def exchange(parts):
    return lax.all_to_all(parts, "ctx", 0, 0, tiled=True, axis_index_groups=SAME_CORE)


def per_device(hidden_in, query, key, value, out_weight, grad_out, span_map, owner_map):
    ids = jnp.stack([lax.axis_index("ctx"), lax.axis_index("head")]).astype(jnp.int32)
    grad_pieces = gather_over_head(grad_out)
    kv_pieces = gather_over_ctx(jnp.concatenate([key, value], axis=1))
    my_x, my_y = lax.axis_index("head") // 4, lax.axis_index("head") % 4
    d_attn = jnp.zeros(query.shape, F32)
    for piece, (dx, dy) in zip(grad_pieces, HEAD_STEPS):
        source = (my_x ^ dx) * 4 + (my_y + dy) % 4
        weight = lax.dynamic_slice_in_dim(out_weight, source * 512, 512, 1)
        d_attn = d_attn + nt(piece, weight)
    d_attn = d_attn.astype(BF16)
    hidden_late, _ = lax.optimization_barrier((hidden_in, grad_pieces[-1]))
    hidden = lax.all_gather(hidden_late, "head", axis=0, tiled=False)
    attn, dkv_own, dkv_other = attention(ids, span_map, query, d_attn, kv_pieces)
    dkv = exchange(chip_sum(dkv_own, dkv_other))
    out_own, out_other = out_gradient(ids, owner_map, attn, grad_pieces)
    out_parts = exchange(chip_sum(out_own, out_other))
    kv_own, kv_other = kv_gradient(
        ids, owner_map, dkv.reshape(CHIPS, TOKENS, 2 * HEAD_SIZE), hidden
    )
    kv_parts = exchange(chip_sum(kv_own, kv_other))
    kv_total = jnp.sum(kv_parts.astype(F32), axis=0)
    out_total = jnp.sum(out_parts.astype(F32), axis=0)
    return kv_total[:, :HEAD_SIZE], kv_total[:, HEAD_SIZE:], out_total


def solution(mesh):
    return jax.shard_map(
        per_device,
        mesh=mesh,
        in_specs=(
            P("ctx", "head"),
            P("ctx", "head"),
            P("ctx", "head"),
            P("ctx", "head"),
            P("head", None),
            P("ctx", "head"),
            P(),
            P(),
        ),
        out_specs=(P("ctx", "head"), P("ctx", "head"), P("head", "ctx")),
        check_vma=False,
    )
```

time: 668 us -> 191 us (0.29)
  waiting for transfers between devices: 424 us -> 57 us
  matrix products: 134 us -> 12.9 us
  Pallas kernels: 0 us -> 53.7 us
  local copies, waits for them, and re-layouts: 53.4 us -> 6.83 us
  starting transfers between devices: 3.78 us -> 35.2 us
  other arithmetic: 36.9 us -> 11.1 us
    ppermute x64 -> x18, waiting for transfers between devices: 208 us -> 14.8 us  [the longest x7 8.02 us: head_move(): return lax.ppermute(value, 'head', pairs)]
    reduce_scatter x3 -> x0, waiting for transfers between devices: 134 us -> none  [the longest x1 75 us: per_device(): lax.psum_scatter(ordered_key, 'ctx', scatter_dimension=0, tiled=True)]
    dot_general x53 -> x8, matrix products: 134 us -> 12.9 us  [nt(): lax.dot_general(a, b, (((1,), (1,)), ((), ())), preferred_element_type=F32)]
    all_gather x4 -> x1, waiting for transfers between devices: 80.4 us -> 0.01 us  [per_device(): hidden = lax.all_gather(hidden_late, 'head', axis=0, tiled=False)]
    pallas_call x0 -> x3, Pallas kernels: none -> 53.7 us  [the longest x1 30.7 us: attention(): pl.pallas_call(attention_kernel, out_shape=(jax.ShapeDtypeStruct(query.sh...]
    all_to_all x0 -> x3, waiting for transfers between devices: none -> 42.2 us  [exchange(): lax.all_to_all(parts, 'ctx', 0, 0, tiled=True, axis_index_groups=SAME_CORE)]
    gather x4 -> x0, local copies, waits for them, and re-layouts: 21.9 us -> none  [the longest x2 17.2 us: per_device(): jnp.take(out_grad.reshape(query_local * HEAD_SIZE, cycle_size, block_exte...]
    reduce_sum x21 -> x2, other arithmetic: 19.8 us -> 1.22 us  [the longest x1 1.08 us: per_device(): out_total = jnp.sum(out_parts.astype(F32), axis=0)]
  transfers between devices with their start and end apart: 71 -> 22, of which waited for: 37 -> 9; matrix products, arithmetic and copies ran while one was open for 33% -> 14% of each run, Pallas kernels for 0% -> 28%
where the time goes in v1:
time: 191 us
  waiting for transfers between devices  57 us (30%)
  Pallas kernels  53.7 us (28%)
  starting transfers between devices  35.2 us (18%)
  between operations  14.3 us (7%)
  matrix products  12.9 us (7%)
  other arithmetic  11.1 us (6%)
  local copies, waits for them, and re-layouts  6.83 us (4%)
    all_to_all x3, waiting for transfers between devices, exchange(): lax.all_to_all(parts, 'ctx', 0, 0, tiled=True, axis_index_groups=SAME_CORE)  42.2 us
    pallas_call x1, Pallas kernels, attention(): pl.pallas_call(attention_kernel, out_shape=(jax.ShapeDtypeStruct(query.sh...  30.7 us
    all_to_all x3, starting transfers between devices, exchange(): lax.all_to_all(parts, 'ctx', 0, 0, tiled=True, axis_index_groups=SAME_CORE)  13.8 us
    dot_general x8, matrix products, nt(): lax.dot_general(a, b, (((1,), (1,)), ((), ())), preferred_element_type=F32)  12.9 us
    pallas_call x1, Pallas kernels, kv_gradient(): pl.pallas_call(kv_grad_kernel, out_shape=(part, part), in_specs=[smem(),...  11.8 us
    pallas_call x1, Pallas kernels, out_gradient(): pl.pallas_call(out_grad_kernel, out_shape=(part, part), in_specs=[smem(),...  11.2 us
    ppermute x7, starting transfers between devices, head_move(): return lax.ppermute(value, 'head', pairs)  10.9 us
    ppermute x11, starting transfers between devices, ctx_move(): return lax.ppermute(value, 'ctx', pairs)  10.4 us
  transfers between devices with their start and end apart: 22, of which 9 were waited for; matrix products, arithmetic and copies ran while one was open for 14% of the time, Pallas kernels for 28%

profile of v1, /device:TPU:0, one launch (start us, length us, event | category | flops | bytes accessed | tf_op | source)
XLA Modules:
  0.0 190.9 jit_solution(3162768569616775257)
XLA Ops:
  7.2 0.0 all-gather.3.cloned.1.call-start
  7.2 1.7 collective-permute-start.1
  8.9 1.5 collective-permute-start
  10.4 1.7 collective-permute-start.2
  12.1 0.9 constant_dynamic-update-slice_fusion.1
  13.0 0.9 constant_dynamic-update-slice_fusion
  13.9 2.8 %collective-permute-start.7 = (bf16[384,256]{1,0:T(8,128)(2,1)S(1)}, bf16[384,256]{1,0:T(8,128)(2,1)S(1)}, u32[]{:S(2)}, u32[]{:S(2)}) collective-permute-start(bf16[384,256]{1,0:T(8,128)(2,1)S(1)} %constant_dynamic-update-slice_fusion), channel_id=1, source_target_pairs={{0,64},{8,72},{16,80},{24,88},{32,96},{40,104},{48,112},{56,120},{... | collective-permute-start | bytes 589832 | tf_op jit(solution)/shard_map/ppermute | solution.py:34
  16.7 1.4 copy.19.spans
  18.1 0.7 pad_add_fusion.ids
  18.7 1.5 fusion.15
  20.3 1.0 collective-permute-done.rest_1_
  21.3 1.5 collective-permute-start.4
  22.8 3.3 %collective-permute-done.7 = bf16[384,256]{1,0:T(8,128)(2,1)S(1)} collective-permute-done((bf16[384,256]{1,0:T(8,128)(2,1)S(1)}, bf16[384,256]{1,0:T(8,128)(2,1)S(1)}, u32[]{:S(2)}, u32[]{:S(2)}) %collective-permute-start.7) | collective-permute-done | bytes 196640 | tf_op jit(solution)/shard_map/ppermute | solution.py:34
  26.2 2.0 %collective-permute-start.8 = (bf16[768,256]{1,0:T(8,128)(2,1)S(1)}, bf16[768,256]{1,0:T(8,128)(2,1)}, u32[]{:S(2)}, u32[]{:S(2)}) collective-permute-start(bf16[768,256]{1,0:T(8,128)(2,1)S(1)} %pad_maximum_fusion.rest_0_), channel_id=1, source_target_pairs={{0,16},{8,24},{16,32},{24,40},{32,48},{40,56},{48,0},{56,8},{64,80... | collective-permute-start | bytes 1179656 | tf_op jit(solution)/shard_map/ppermute | solution.py:34
  28.2 2.2 %collective-permute-start.9 = (bf16[768,256]{1,0:T(8,128)(2,1)S(1)}, bf16[768,256]{1,0:T(8,128)(2,1)}, u32[]{:S(2)}, u32[]{:S(2)}) collective-permute-start(bf16[768,256]{1,0:T(8,128)(2,1)S(1)} %pad_maximum_fusion.rest_0_), channel_id=1, source_target_pairs={{0,48},{8,56},{16,0},{24,8},{32,16},{40,24},{48,32},{56,40},{64,11... | collective-permute-start | bytes 1179656 | tf_op jit(solution)/shard_map/ppermute | solution.py:34
  30.4 1.6 convolution_add_fusion.3
  31.9 1.9 collective-permute-start.10
  33.8 0.0 collective-permute-done.2.rest_3_
  33.8 1.6 collective-permute-start.5
  35.4 0.0 collective-permute-done.4.rest_5_
  35.4 1.7 collective-permute-start.6
  37.0 1.4 fusion.11
  38.5 1.6 fusion
  40.1 3.9 %collective-permute-done.6.rest_7_ = bf16[384,512]{1,0:T(8,128)(2,1)S(1)} collective-permute-done((bf16[384,512]{1,0:T(8,128)(2,1)S(1)}, bf16[384,512]{1,0:T(8,128)(2,1)S(1)}, u32[]{:S(2)}, u32[]{:S(2)}) %collective-permute-start.6) | collective-permute-done | bytes 393248 | tf_op jit(solution)/shard_map/ppermute | solution.py:39
  43.9 1.3 collective-permute-start.3
  45.2 1.4 fusion.8
  46.7 0.0 all-gather.3.cloned.1.call-update
  46.7 0.0 collective-permute-done.8.rest_1_
  46.7 0.1 collective-permute-start.11
  46.8 0.5 collective-permute-start.12
  47.3 0.6 collective-permute-done.10.rest_3_
  47.9 0.0 collective-permute-start.13
  47.9 0.0 collective-permute-done.5.rest_6_
  47.9 0.5 collective-permute-start.14
  48.4 1.6 fusion.6
  50.0 3.1 %collective-permute-done.3.rest_4_ = bf16[384,512]{1,0:T(8,128)(2,1)S(1)} collective-permute-done((bf16[384,512]{1,0:T(8,128)(2,1)}, bf16[384,512]{1,0:T(8,128)(2,1)S(1)}, u32[]{:S(2)}, u32[]{:S(2)}) %collective-permute-start.3) | collective-permute-done | bytes 393248 | tf_op jit(solution)/shard_map/ppermute | solution.py:39
  53.1 1.6 fusion.2
  54.7 2.2 %fusion.4.do_ref = bf16[384,512]{1,0:T(8,128)(2,1)} fusion(f32[512,384]{0,1:T(8,128)S(1)} %fusion.2, bf16[384,512]{1,0:T(8,128)(2,1)S(1)} %collective-permute-done.6.rest_7_, bf16[512,4096]{1,0:T(8,128)(2,1)} %param.12, s32[]{:T(128)S(6)} %select_n.72), kind=kOutput, calls=%fused_computation.13 | convolution fusion | flops 201719808 | bytes 2097156 | tf_op jit(solution)/shard_map/dot_general | solution.py:66
  56.9 0.0 collective-permute-done.11.rest_4_
  56.9 0.0 collective-permute-done.12.rest_5_
  57.0 0.7 copy-done.8
  57.7 0.2 copy-done.9
  57.9 0.1 copy-done.10
  58.0 0.8 copy-done.11
  58.8 30.7 %attention.1 = (bf16[384,512]{1,0:T(8,128)(2,1)}, bf16[16,192,256]{2,1,0:T(8,128)(2,1)}, bf16[16,192,256]{2,1,0:T(8,128)(2,1)}) custom-call(s32[2]{0:T(128)} %pad_add_fusion.ids, s32[16,2]{1,0:T(8,128)} %copy.19.spans, bf16[384,512]{1,0:T(8,128)(2,1)} %q_ref.1, bf16[384,512]{1,0:T(8,128)(2,1)} %fusion.4.do_ref, bf16[768,256]{1,0:T(8,128)(2,1)} %copy-done.5, ...), custom_call_target="tpu_custom_call" | custom-call | flops 12999999488 | bytes 8000000 | tf_op jit(solution)/shard_map/attention/pallas_call | solution.py:216
  89.5 0.1 collective-permute-start.15
  89.6 11.2 %out_gradient.1 = (bf16[8,512,256]{2,1,0:T(8,128)(2,1)}, bf16[8,512,256]{2,1,0:T(8,128)(2,1)}) custom-call(s32[2]{0:T(128)} %pad_add_fusion.ids, s32[3,16]{1,0:T(4,128)} %owners.3, bf16[384,512]{1,0:T(8,128)(2,1)} %get-tuple-element.16.attn_ref, bf16[384,512]{1,0:T(8,128)(2,1)} %rest_0_.1, bf16[384,512]{1,0:T(8,128)(2,1)} %collective-permute-done.rest_1_, ...), custom_call_target="tpu_custom_call" | custom-call | flops 1600000000 | bytes 8000000 | tf_op jit(solution)/shard_map/out_gradient/pallas_call | solution.py:262
  100.8 0.4 collective-permute-start.17
  101.2 1.1 copy-done.2
  102.3 3.2 %add_convert_fusion.1 = bf16[16,192,256]{2,1,0:T(8,128)(2,1)} fusion(bf16[16,192,256]{2,1,0:T(8,128)(2,1)} %copy-done.2, bf16[16,192,256]{2,1,0:T(8,128)(2,1)S(1)} %copy-done.1), kind=kLoop, calls=%fused_computation.2 | loop fusion | flops 3145728 | bytes 4718592 | tf_op jit(solution)/shard_map/convert_element_type | solution.py:315
  105.5 4.3 %all-to-all-start = ((bf16[16,192,256]{2,1,0:T(8,128)(2,1)}), bf16[16,192,256]{2,1,0:T(8,128)(2,1)}, u32[]{:S(2)}, u32[]{:S(2)}) async-start(bf16[16,192,256]{2,1,0:T(8,128)(2,1)} %add_convert_fusion.1), calls=%async_computation | async-start | bytes 3145728 | tf_op jit(solution)/shard_map/all_to_all | solution.py:322
  109.9 3.4 %add_convert_fusion = bf16[8,512,256]{2,1,0:T(8,128)(2,1)} fusion(bf16[8,512,256]{2,1,0:T(8,128)(2,1)} %collective-permute-done.17, bf16[8,512,256]{2,1,0:T(8,128)(2,1)S(1)} %copy-done), kind=kLoop, calls=%fused_computation.1 | loop fusion | flops 4194304 | bytes 6291456 | tf_op jit(solution)/shard_map/convert_element_type | solution.py:315
  113.3 17.9 %all-to-all-done = bf16[16,192,256]{2,1,0:T(8,128)(2,1)} async-done(((bf16[16,192,256]{2,1,0:T(8,128)(2,1)}), bf16[16,192,256]{2,1,0:T(8,128)(2,1)}, u32[]{:S(2)}, u32[]{:S(2)}) %all-to-all-start) | async-done | bytes 1572896 | tf_op jit(solution)/shard_map/all_to_all | solution.py:322
  131.2 4.7 %all-to-all-start.2 = ((bf16[8,512,256]{2,1,0:T(8,128)(2,1)}), bf16[8,512,256]{2,1,0:T(8,128)(2,1)S(1)}, u32[]{:S(2)}, u32[]{:S(2)}) async-start(bf16[8,512,256]{2,1,0:T(8,128)(2,1)} %add_convert_fusion), calls=%async_computation.2 | async-start | bytes 4194304 | tf_op jit(solution)/shard_map/all_to_all | solution.py:322
  135.9 0.0 all-gather.3.cloned.1.call-done
  136.0 11.8 %kv_gradient.1 = (bf16[8,256,256]{2,1,0:T(8,128)(2,1)}, bf16[8,256,256]{2,1,0:T(8,128)(2,1)}) custom-call(s32[2]{0:T(128)} %pad_add_fusion.ids, s32[3,16]{1,0:T(4,128)} %owners.3, bf16[8,384,256]{2,1,0:T(8,128)(2,1)} %bitcast.3.parts_ref, bf16[8,384,512]{2,1,0:T(8,128)(2,1)} %bitcast.14), custom_call_target="tpu_custom_call" | custom-call | flops 1600000000 | bytes 7000000 | tf_op jit(solution)/shard_map/kv_gradient/pallas_call | solution.py:300
  147.7 2.9 %collective-permute-done.16 = bf16[8,256,256]{2,1,0:T(8,128)(2,1)S(1)} collective-permute-done((bf16[8,256,256]{2,1,0:T(8,128)(2,1)}, bf16[8,256,256]{2,1,0:T(8,128)(2,1)S(1)}, u32[]{:S(2)}, u32[]{:S(2)}) %collective-permute-start.16) | collective-permute-done | bytes 1048608 | tf_op jit(solution)/shard_map/ppermute | solution.py:34
  150.6 2.5 %add_convert_fusion.2 = bf16[8,256,256]{2,1,0:T(8,128)(2,1)} fusion(bf16[8,256,256]{2,1,0:T(8,128)(2,1)S(1)} %collective-permute-done.16, bf16[8,256,256]{2,1,0:T(8,128)(2,1)} %get-tuple-element.14), kind=kLoop, calls=%fused_computation.4 | loop fusion | flops 2097152 | bytes 3145728 | tf_op jit(solution)/shard_map/convert_element_type | solution.py:315
  153.1 9.5 %all-to-all-done.2 = bf16[8,512,256]{2,1,0:T(8,128)(2,1)S(1)} async-done(((bf16[8,512,256]{2,1,0:T(8,128)(2,1)}), bf16[8,512,256]{2,1,0:T(8,128)(2,1)S(1)}, u32[]{:S(2)}, u32[]{:S(2)}) %all-to-all-start.2) | async-done | bytes 2097184 | tf_op jit(solution)/shard_map/all_to_all | solution.py:322
  162.6 4.8 %all-to-all-start.1 = ((bf16[8,256,256]{2,1,0:T(8,128)(2,1)}), bf16[8,256,256]{2,1,0:T(8,128)(2,1)S(1)}, u32[]{:S(2)}, u32[]{:S(2)}) async-start(bf16[8,256,256]{2,1,0:T(8,128)(2,1)} %add_convert_fusion.2), calls=%async_computation.1 | async-start | bytes 2097152 | tf_op jit(solution)/shard_map/all_to_all | solution.py:322
  167.3 1.1 convert_reduce_fusion
  168.4 14.8 %all-to-all-done.1 = bf16[8,256,256]{2,1,0:T(8,128)(2,1)S(1)} async-done(((bf16[8,256,256]{2,1,0:T(8,128)(2,1)}), bf16[8,256,256]{2,1,0:T(8,128)(2,1)S(1)}, u32[]{:S(2)}, u32[]{:S(2)}) %all-to-all-start.1) | async-done | bytes 1048608 | tf_op jit(solution)/shard_map/all_to_all | solution.py:322
  183.2 0.1 convert_reduce_fusion.1
  183.3 0.7 fusion.25
  (27 shorter events, 0.1 us)
Async XLA Ops:
  7.2 128.8 %all-gather.3.cloned.1.call-start = ((), (), s32[]{:S(2)}) async-start(), calls=%async_computation.3 | async-start | bytes 3538944 | tf_op jit(solution)/shard_map/all_gather | solution.py:337
  7.2 24.7 %collective-permute-start.1 = (bf16[384,512]{1,0:T(8,128)(2,1)}, bf16[384,512]{1,0:T(8,128)(2,1)}, u32[]{:S(2)}, u32[]{:S(2)}) collective-permute-start(bf16[384,512]{1,0:T(8,128)(2,1)} %rest_0_.1), channel_id=1, source_target_pairs={{0,1},{1,2},{2,3},{3,0},{4,5},{5,6},{6,7},{7,4},{8,9},{9,10},{10,1... | collective-permute-start | bytes 1179656 | tf_op jit(solution)/shard_map/ppermute | solution.py:39
  8.9 12.4 %collective-permute-start = (bf16[384,512]{1,0:T(8,128)(2,1)}, bf16[384,512]{1,0:T(8,128)(2,1)}, u32[]{:S(2)}, u32[]{:S(2)}) collective-permute-start(bf16[384,512]{1,0:T(8,128)(2,1)} %rest_0_.1), channel_id=1, source_target_pairs={{0,4},{1,5},{2,6},{3,7},{4,0},{5,1},{6,2},{7,3},{8,12},{9,13},{10,... | collective-permute-start | bytes 1179656 | tf_op jit(solution)/shard_map/ppermute | solution.py:39
  10.4 23.4 %collective-permute-start.2 = (bf16[384,512]{1,0:T(8,128)(2,1)}, bf16[384,512]{1,0:T(8,128)(2,1)S(1)}, u32[]{:S(2)}, u32[]{:S(2)}) collective-permute-start(bf16[384,512]{1,0:T(8,128)(2,1)} %rest_0_.1), channel_id=1, source_target_pairs={{0,3},{1,0},{2,1},{3,2},{4,7},{5,4},{6,5},{7,6},{8,11},{9,8},{10,9... | collective-permute-start | bytes 1179656 | tf_op jit(solution)/shard_map/ppermute | solution.py:39
  13.9 12.2 %collective-permute-start.7 = (bf16[384,256]{1,0:T(8,128)(2,1)S(1)}, bf16[384,256]{1,0:T(8,128)(2,1)S(1)}, u32[]{:S(2)}, u32[]{:S(2)}) collective-permute-start(bf16[384,256]{1,0:T(8,128)(2,1)S(1)} %constant_dynamic-update-slice_fusion), channel_id=1, source_target_pairs={{0,64},{8,72},{16,80},{24,88},{32,96},{40,104},{48,112},{56,120},{... | collective-permute-start | bytes 589832 | tf_op jit(solution)/shard_map/ppermute | solution.py:34
  21.3 14.1 %collective-permute-start.4 = (bf16[384,512]{1,0:T(8,128)(2,1)}, bf16[384,512]{1,0:T(8,128)(2,1)S(1)}, u32[]{:S(2)}, u32[]{:S(2)}) collective-permute-start(bf16[384,512]{1,0:T(8,128)(2,1)} %collective-permute-done.rest_1_), channel_id=1, source_target_pairs={{0,3},{1,0},{2,1},{3,2},{4,7},{5,4},{6,5},{7,6},{8,11},{9,8},{10,9... | collective-permute-start | bytes 1179656 | tf_op jit(solution)/shard_map/ppermute | solution.py:39
  26.2 20.6 %copy-start.5 = (bf16[768,256]{1,0:T(8,128)(2,1)}, bf16[768,256]{1,0:T(8,128)(2,1)S(1)}, u32[]{:S(2)}) copy-start(bf16[768,256]{1,0:T(8,128)(2,1)S(1)} %pad_maximum_fusion.rest_0_) | copy-start | bytes 1179652
  26.2 20.5 %collective-permute-start.8 = (bf16[768,256]{1,0:T(8,128)(2,1)S(1)}, bf16[768,256]{1,0:T(8,128)(2,1)}, u32[]{:S(2)}, u32[]{:S(2)}) collective-permute-start(bf16[768,256]{1,0:T(8,128)(2,1)S(1)} %pad_maximum_fusion.rest_0_), channel_id=1, source_target_pairs={{0,16},{8,24},{16,32},{24,40},{32,48},{40,56},{48,0},{56,8},{64,80... | collective-permute-start | bytes 1179656 | tf_op jit(solution)/shard_map/ppermute | solution.py:34
  28.2 18.7 %collective-permute-start.9 = (bf16[768,256]{1,0:T(8,128)(2,1)S(1)}, bf16[768,256]{1,0:T(8,128)(2,1)}, u32[]{:S(2)}, u32[]{:S(2)}) collective-permute-start(bf16[768,256]{1,0:T(8,128)(2,1)S(1)} %pad_maximum_fusion.rest_0_), channel_id=1, source_target_pairs={{0,48},{8,56},{16,0},{24,8},{32,16},{40,24},{48,32},{56,40},{64,11... | collective-permute-start | bytes 1179656 | tf_op jit(solution)/shard_map/ppermute | solution.py:34
  31.9 16.0 %collective-permute-start.10 = (bf16[768,256]{1,0:T(8,128)(2,1)S(1)}, bf16[768,256]{1,0:T(8,128)(2,1)}, u32[]{:S(2)}, u32[]{:S(2)}) collective-permute-start(bf16[768,256]{1,0:T(8,128)(2,1)S(1)} %pad_maximum_fusion.rest_0_), channel_id=1, source_target_pairs={{0,32},{8,40},{16,48},{24,56},{32,0},{40,8},{48,16},{56,24},{64,96... | collective-permute-start | bytes 1179656 | tf_op jit(solution)/shard_map/ppermute | solution.py:34
  33.8 12.9 %copy-start.6 = (bf16[384,512]{1,0:T(8,128)(2,1)}, bf16[384,512]{1,0:T(8,128)(2,1)S(1)}, u32[]{:S(2)}) copy-start(bf16[384,512]{1,0:T(8,128)(2,1)S(1)} %collective-permute-done.2.rest_3_) | copy-start | bytes 1179652
  33.8 14.1 %collective-permute-start.5 = (bf16[384,512]{1,0:T(8,128)(2,1)}, bf16[384,512]{1,0:T(8,128)(2,1)}, u32[]{:S(2)}, u32[]{:S(2)}) collective-permute-start(bf16[384,512]{1,0:T(8,128)(2,1)} %collective-permute-done.1.rest_2_), channel_id=1, source_target_pairs={{0,1},{1,2},{2,3},{3,0},{4,5},{5,6},{6,7},{7,4},{8,9},{9,10},{10,1... | collective-permute-start | bytes 1179656 | tf_op jit(solution)/shard_map/ppermute | solution.py:39
  35.4 11.3 %copy-start.7 = (bf16[384,512]{1,0:T(8,128)(2,1)}, bf16[384,512]{1,0:T(8,128)(2,1)S(1)}, u32[]{:S(2)}) copy-start(bf16[384,512]{1,0:T(8,128)(2,1)S(1)} %collective-permute-done.4.rest_5_) | copy-start | bytes 1179652
  35.4 8.5 %collective-permute-start.6 = (bf16[384,512]{1,0:T(8,128)(2,1)S(1)}, bf16[384,512]{1,0:T(8,128)(2,1)S(1)}, u32[]{:S(2)}, u32[]{:S(2)}) collective-permute-start(bf16[384,512]{1,0:T(8,128)(2,1)S(1)} %collective-permute-done.4.rest_5_), channel_id=1, source_target_pairs={{0,3},{1,0},{2,1},{3,2},{4,7},{5,4},{6,5},{7,6},{8,11},{9,8},{10,9... | collective-permute-start | bytes 1179656 | tf_op jit(solution)/shard_map/ppermute | solution.py:39
  43.9 10.8 %copy-start.3 = (bf16[384,512]{1,0:T(8,128)(2,1)}, bf16[384,512]{1,0:T(8,128)(2,1)S(1)}, u32[]{:S(2)}) copy-start(bf16[384,512]{1,0:T(8,128)(2,1)S(1)} %collective-permute-done.6.rest_7_) | copy-start | bytes 1179652
  43.9 9.2 %collective-permute-start.3 = (bf16[384,512]{1,0:T(8,128)(2,1)}, bf16[384,512]{1,0:T(8,128)(2,1)S(1)}, u32[]{:S(2)}, u32[]{:S(2)}) collective-permute-start(bf16[384,512]{1,0:T(8,128)(2,1)} %collective-permute-done.rest_1_), channel_id=1, source_target_pairs={{0,1},{1,2},{2,3},{3,0},{4,5},{5,6},{6,7},{7,4},{8,9},{9,10},{10,1... | collective-permute-start | bytes 1179656 | tf_op jit(solution)/shard_map/ppermute | solution.py:39
  46.7 10.2 %collective-permute-start.11 = (bf16[768,256]{1,0:T(8,128)(2,1)S(1)}, bf16[768,256]{1,0:T(8,128)(2,1)S(1)}, u32[]{:S(2)}, u32[]{:S(2)}) collective-permute-start(bf16[768,256]{1,0:T(8,128)(2,1)S(1)} %pad_maximum_fusion.rest_0_), channel_id=1, source_target_pairs={{0,8},{8,0},{16,24},{24,16},{32,40},{40,32},{48,56},{56,48},{64,72... | collective-permute-start | bytes 1179656 | tf_op jit(solution)/shard_map/ppermute | solution.py:34
  46.8 10.1 %collective-permute-start.12 = (bf16[768,256]{1,0:T(8,128)(2,1)}, bf16[768,256]{1,0:T(8,128)(2,1)S(1)}, u32[]{:S(2)}, u32[]{:S(2)}) collective-permute-start(bf16[768,256]{1,0:T(8,128)(2,1)} %collective-permute-done.8.rest_1_), channel_id=1, source_target_pairs={{0,8},{8,0},{16,24},{24,16},{32,40},{40,32},{48,56},{56,48},{64,72... | collective-permute-start | bytes 1179656 | tf_op jit(solution)/shard_map/ppermute | solution.py:34
  47.9 9.1 %collective-permute-start.13 = (bf16[768,256]{1,0:T(8,128)(2,1)}, bf16[768,256]{1,0:T(8,128)(2,1)S(1)}, u32[]{:S(2)}, u32[]{:S(2)}) collective-permute-start(bf16[768,256]{1,0:T(8,128)(2,1)} %collective-permute-done.9.rest_2_), channel_id=1, source_target_pairs={{0,8},{8,0},{16,24},{24,16},{32,40},{40,32},{48,56},{56,48},{64,72... | collective-permute-start | bytes 1179656 | tf_op jit(solution)/shard_map/ppermute | solution.py:34
  47.9 9.1 %collective-permute-start.14 = (bf16[768,256]{1,0:T(8,128)(2,1)}, bf16[768,256]{1,0:T(8,128)(2,1)S(1)}, u32[]{:S(2)}, u32[]{:S(2)}) collective-permute-start(bf16[768,256]{1,0:T(8,128)(2,1)} %collective-permute-done.10.rest_3_), channel_id=1, source_target_pairs={{0,8},{8,0},{16,24},{24,16},{32,40},{40,32},{48,56},{56,48},{64,72... | collective-permute-start | bytes 1179656 | tf_op jit(solution)/shard_map/ppermute | solution.py:34
  53.1 36.4 %copy-start.4 = (bf16[384,512]{1,0:T(8,128)(2,1)}, bf16[384,512]{1,0:T(8,128)(2,1)S(1)}, u32[]{:S(2)}) copy-start(bf16[384,512]{1,0:T(8,128)(2,1)S(1)} %collective-permute-done.3.rest_4_) | copy-start | bytes 1179652
  56.9 0.8 copy-start.8
  56.9 0.9 copy-start.9
  57.0 1.0 copy-start.10
  58.0 0.8 copy-start.11
  89.5 12.8 %copy-start.1 = (bf16[16,192,256]{2,1,0:T(8,128)(2,1)S(1)}, bf16[16,192,256]{2,1,0:T(8,128)(2,1)}, u32[]{:S(2)}) copy-start(bf16[16,192,256]{2,1,0:T(8,128)(2,1)} %get-tuple-element.11) | copy-start | bytes 4718596
  89.5 11.7 %collective-permute-start.15 = (bf16[16,192,256]{2,1,0:T(8,128)(2,1)}, bf16[16,192,256]{2,1,0:T(8,128)(2,1)S(1)}, u32[]{:S(2)}, u32[]{:S(2)}) collective-permute-start(bf16[16,192,256]{2,1,0:T(8,128)(2,1)} %get-tuple-element.12), channel_id=1, source_target_pairs={{0,8},{8,0},{16,24},{24,16},{32,40},{40,32},{48,56},{56,48},{64,72... | collective-permute-start | bytes 4718600 | tf_op jit(solution)/shard_map/ppermute | solution.py:34
  100.8 9.1 %collective-permute-start.17 = (bf16[8,512,256]{2,1,0:T(8,128)(2,1)}, bf16[8,512,256]{2,1,0:T(8,128)(2,1)}, u32[]{:S(2)}, u32[]{:S(2)}) collective-permute-start(bf16[8,512,256]{2,1,0:T(8,128)(2,1)} %get-tuple-element.18), channel_id=1, source_target_pairs={{0,8},{8,0},{16,24},{24,16},{32,40},{40,32},{48,56},{56,48},{64,72... | collective-permute-start | bytes 6291464 | tf_op jit(solution)/shard_map/ppermute | solution.py:34
  101.2 1.1 copy-start.2
  102.3 7.6 %copy-start = (bf16[8,512,256]{2,1,0:T(8,128)(2,1)S(1)}, bf16[8,512,256]{2,1,0:T(8,128)(2,1)}, u32[]{:S(2)}) copy-start(bf16[8,512,256]{2,1,0:T(8,128)(2,1)} %get-tuple-element.17) | copy-start | bytes 6291460
  105.5 25.7 %all-to-all-start = ((bf16[16,192,256]{2,1,0:T(8,128)(2,1)}), bf16[16,192,256]{2,1,0:T(8,128)(2,1)}, u32[]{:S(2)}, u32[]{:S(2)}) async-start(bf16[16,192,256]{2,1,0:T(8,128)(2,1)} %add_convert_fusion.1), calls=%async_computation | async-start | bytes 3145728 | tf_op jit(solution)/shard_map/all_to_all | solution.py:322
  131.2 31.4 %all-to-all-start.2 = ((bf16[8,512,256]{2,1,0:T(8,128)(2,1)}), bf16[8,512,256]{2,1,0:T(8,128)(2,1)S(1)}, u32[]{:S(2)}, u32[]{:S(2)}) async-start(bf16[8,512,256]{2,1,0:T(8,128)(2,1)} %add_convert_fusion), calls=%async_computation.2 | async-start | bytes 4194304 | tf_op jit(solution)/shard_map/all_to_all | solution.py:322
  147.7 2.9 %collective-permute-start.16 = (bf16[8,256,256]{2,1,0:T(8,128)(2,1)}, bf16[8,256,256]{2,1,0:T(8,128)(2,1)S(1)}, u32[]{:S(2)}, u32[]{:S(2)}) collective-permute-start(bf16[8,256,256]{2,1,0:T(8,128)(2,1)} %get-tuple-element.15), channel_id=1, source_target_pairs={{0,8},{8,0},{16,24},{24,16},{32,40},{40,32},{48,56},{56,48},{64,72... | collective-permute-start | bytes 3145736 | tf_op jit(solution)/shard_map/ppermute | solution.py:34
  162.6 20.6 %all-to-all-start.1 = ((bf16[8,256,256]{2,1,0:T(8,128)(2,1)}), bf16[8,256,256]{2,1,0:T(8,128)(2,1)S(1)}, u32[]{:S(2)}, u32[]{:S(2)}) async-start(bf16[8,256,256]{2,1,0:T(8,128)(2,1)} %add_convert_fusion.2), calls=%async_computation.1 | async-start | bytes 2097152 | tf_op jit(solution)/shard_map/all_to_all | solution.py:322
Sparse Core Ops, SparseCore 0:
  46.8 42.1 all-gather.2

commit v2 on v0

v2 whole, which is shorter than its diff:
```python
import jax
import jax.numpy as jnp
from jax import lax
from jax.experimental import pallas as pl
from jax.experimental.pallas import tpu as pltpu
from jax.sharding import PartitionSpec as P

HEAD_SIZE = 128
GROUP = 4
SPAN = 192
SLOTS = 32
N_CTX = 16
CHIPS = 8
TOKENS = 384
KEY_BLOCK = 384
KEY_BLOCKS = 16
OWN_BLOCKS = 8
ROWS = GROUP * SPAN
FEATURES = 256
SCALE = HEAD_SIZE ** (-0.5)
EXP2_SCALE = SCALE * 1.4426950408889634
F32 = jnp.float32
BF16 = jnp.bfloat16
VMEM_BYTES = 58 * 1024 * 1024


def ctx_move(value, dx, dz, dc):
    pairs = []
    for i in range(N_CTX):
        x, z, c = i // 8, (i // 2) % 4, i % 2
        pairs.append((i, ((x ^ dx) * 4 + (z + dz) % 4) * 2 + (c ^ dc)))
    return lax.ppermute(value, "ctx", pairs)


STEPS = ((0, 0), (1, 0), (0, 3), (0, 1), (1, 3), (1, 1), (0, 2), (1, 2))


def gather_over_ctx(own):
    across = ctx_move(own, 1, 0, 0)
    up0 = ctx_move(own, 0, 1, 0)
    down0 = ctx_move(own, 0, 3, 0)
    up1 = ctx_move(across, 0, 1, 0)
    down1 = ctx_move(across, 0, 3, 0)
    far0 = ctx_move(up0, 0, 1, 0)
    far1 = ctx_move(down1, 0, 3, 0)
    mine = [own, across, up0, down0, up1, down1, far0, far1]
    return mine + [swap(piece) for piece in mine]


def swap(value):
    return ctx_move(value, 0, 0, 1)


def source_of(ids, step, other_core):
    x, z, c = ids[0] // 8, (ids[0] // 2) % 4, ids[0] % 2
    dx, dz = STEPS[step]
    return ((x ^ dx) * 4 + (z + dz) % 4) * 2 + (c ^ other_core)


def nt(a, b):
    return lax.dot_general(a, b, (((1,), (1,)), ((), ())), preferred_element_type=F32)


def nn(a, b):
    return lax.dot_general(a, b, (((1,), (0,)), ((), ())), preferred_element_type=F32)


def key_rows(b):
    return pl.ds(pl.multiple_of(b * KEY_BLOCK, KEY_BLOCK), KEY_BLOCK)


def span_rows(n):
    return pl.ds(pl.multiple_of(n * SPAN, SPAN), SPAN)


def heads_down(value, half):
    rows = value[half * SPAN : (half + 1) * SPAN]
    return jnp.concatenate(
        [rows[:, h * HEAD_SIZE : (h + 1) * HEAD_SIZE] for h in range(GROUP)], axis=0
    )


def row_in_span(shape, dim):
    row = lax.broadcasted_iota(jnp.int32, shape, dim)
    within = row
    for h in range(1, GROUP):
        within = within - jnp.where(row >= h * SPAN, SPAN, 0)
    return within


def forward_kernel(ids, spans, q_ref, *rest):
    kv_refs, (attn_ref, lse_ref, ks, vs, qs, acc, tops, sums) = rest[:16], rest[16:]
    for piece in range(16):
        source = source_of(ids, piece % 8, piece // 8)
        for half in range(2):
            at, rows = span_rows(spans[source, half]), pl.ds(half * SPAN, SPAN)
            ks[at, :] = kv_refs[piece][rows, :HEAD_SIZE]
            vs[at, :] = kv_refs[piece][rows, HEAD_SIZE:]
    for half in range(2):
        qs[half] = heads_down(q_ref[...], half)

    for half in range(2):
        span = spans[ids[0], half]
        last = span // 2

        def step(b, masked):
            s = nt(qs[half], ks[key_rows(b), :])
            if masked:
                seen = span * SPAN + row_in_span((ROWS, 1), 0) - b * KEY_BLOCK
                s = jnp.where(lax.broadcasted_iota(jnp.int32, s.shape, 1) > seen, -1e30, s)
            old = tops[...]
            new = jnp.maximum(old, jnp.max(s, axis=1, keepdims=True))
            shrink = jnp.exp2((old - new) * EXP2_SCALE)
            tops[...] = new
            total, low = 0.0, []
            for k in range(0, KEY_BLOCK, HEAD_SIZE):
                p = jnp.exp2((s[:, k : k + HEAD_SIZE] - new) * EXP2_SCALE)
                total = total + p
                low.append(p.astype(BF16))
            sums[...] = sums[...] * shrink + total
            acc[...] = acc[...] * shrink + nn(jnp.concatenate(low, axis=1), vs[key_rows(b), :])

        tops[...] = jnp.full(tops.shape, -1e30, F32)
        sums[...] = jnp.zeros(sums.shape, F32)
        acc[...] = jnp.zeros(acc.shape, F32)

        @pl.loop(0, last)
        def _(b):
            step(b, False)

        step(last, True)
        total = jnp.sum(sums[...], axis=1, keepdims=True)
        attn = (acc[...] * (1.0 / total)).astype(BF16)
        for h in range(GROUP):
            attn_ref[pl.ds(half * SPAN, SPAN), pl.ds(h * HEAD_SIZE, HEAD_SIZE)] = attn[
                h * SPAN : (h + 1) * SPAN
            ]
        lse_ref[half] = (tops[...] * EXP2_SCALE + jnp.log2(total)).T[:8]


def smem():
    return pl.BlockSpec(memory_space=pltpu.SMEM)


def vmem():
    return pl.BlockSpec(memory_space=pltpu.VMEM)


def call(kernel, inputs, outputs, scratch, flops, name):
    bytes_moved = sum(x.size * x.dtype.itemsize for x in list(inputs) + list(outputs))
    return pl.pallas_call(
        kernel,
        out_shape=outputs,
        in_specs=[smem(), smem()] + [vmem()] * (len(inputs) - 2),
        out_specs=(vmem(),) * len(outputs),
        scratch_shapes=scratch,
        compiler_params=pltpu.CompilerParams(vmem_limit_bytes=VMEM_BYTES),
        cost_estimate=pl.CostEstimate(flops=flops, bytes_accessed=bytes_moved, transcendentals=0),
        name=name,
    )(*inputs)


def forward(ids, span_map, query, kv_pieces):
    keys = pltpu.VMEM((KEY_BLOCKS * KEY_BLOCK, HEAD_SIZE), BF16)
    rows = pltpu.VMEM((ROWS, HEAD_SIZE), F32)
    return call(
        forward_kernel,
        (ids, span_map, query, *kv_pieces),
        (
            jax.ShapeDtypeStruct(query.shape, BF16),
            jax.ShapeDtypeStruct((2, 8, ROWS), F32),
        ),
        [keys, keys, pltpu.VMEM((2, ROWS, HEAD_SIZE), BF16), rows, rows, rows],
        10_000_000_000,
        "forward",
    )


def backward_kernel(ids, spans, *rest):
    (q_own, q_other, do_own, do_other, attn_own, attn_other, lse_own, lse_other), rest = (
        rest[:8],
        rest[8:],
    )
    kv_refs, (part_ref, ks, vs, qs, dos, lse, delta, acc_k, acc_v, slot, rank, seen, order) = (
        rest[:8],
        rest[8:],
    )
    core = ids[0] % 2
    for s in range(SLOTS):
        slot[s] = 0
    for chip in range(CHIPS):
        for half in range(2):
            slot[spans[chip * 2 + core, half]] = chip * 2 + half + 1
    count = jnp.int32(0)
    for s in range(SLOTS):
        order[count] = s
        rank[s] = count
        count = count + jnp.minimum(slot[s], 1)
        seen[s] = count

    for piece in range(8):
        source = source_of(ids, piece, 0)
        for half in range(2):
            at, rows = span_rows(rank[spans[source, half]]), pl.ds(half * SPAN, SPAN)
            ks[at, :] = kv_refs[piece][rows, :HEAD_SIZE]
            vs[at, :] = kv_refs[piece][rows, HEAD_SIZE:]
    sides = ((q_own, do_own, attn_own, lse_own), (q_other, do_other, attn_other, lse_other))
    for side, (q_ref, do_ref, attn_ref, lse_ref) in enumerate(sides):
        product = do_ref[...].astype(F32) * attn_ref[...].astype(F32)
        for half in range(2):
            qs[side * 2 + half] = heads_down(q_ref[...], half)
            dos[side * 2 + half] = heads_down(do_ref[...], half)
            lse[side * 2 + half] = lse_ref[half, :1]
            delta[side * 2 + half] = jnp.sum(heads_down(product, half).T, axis=0, keepdims=True)

    def tile(b, group, span, masked):
        s = nt(ks[key_rows(b), :], qs[group])
        if masked:
            row = lax.broadcasted_iota(jnp.int32, (KEY_BLOCK, 1), 0)
            at = jnp.where(row < SPAN, order[b * 2] * SPAN, (order[b * 2 + 1] - 1) * SPAN) + row
            s = jnp.where(at > span * SPAN + row_in_span((1, ROWS), 1), -1e30, s)
        p = jnp.exp2(s * EXP2_SCALE - lse[group])
        d_p = nt(vs[key_rows(b), :], dos[group])
        d_s = (p * (d_p - delta[group])).astype(BF16)
        acc_k[...] += nn(d_s, qs[group])
        acc_v[...] += nn(p.astype(BF16), dos[group])

    @pl.loop(0, OWN_BLOCKS)
    def _(b):
        acc_k[...] = jnp.zeros(acc_k.shape, F32)
        acc_v[...] = jnp.zeros(acc_v.shape, F32)

        @pl.loop(0, 4)
        def _(group):
            span = spans[ids[0] ^ (group // 2), group % 2]
            last = (seen[span] + 1) // 2 - 1

            @pl.when(b < last)
            def _():
                tile(b, group, span, False)

            @pl.when(b == last)
            def _():
                tile(b, group, span, True)

        d_key = (acc_k[...] * SCALE).astype(BF16)
        d_value = acc_v[...].astype(BF16)
        for n in range(2):
            at = slot[order[b * 2 + n]] - 1
            part_ref[at, :, :HEAD_SIZE] = d_key[n * SPAN : (n + 1) * SPAN]
            part_ref[at, :, HEAD_SIZE:] = d_value[n * SPAN : (n + 1) * SPAN]


def backward(ids, span_map, sides, kv_pieces):
    keys = pltpu.VMEM((OWN_BLOCKS * KEY_BLOCK, HEAD_SIZE), BF16)
    rows = pltpu.VMEM((4, ROWS, HEAD_SIZE), BF16)
    stats = pltpu.VMEM((4, 1, ROWS), F32)
    sums = pltpu.VMEM((KEY_BLOCK, HEAD_SIZE), F32)
    table = pltpu.SMEM((SLOTS,), jnp.int32)
    (part,) = call(
        backward_kernel,
        (ids, span_map, *sides, *kv_pieces),
        (jax.ShapeDtypeStruct((2 * CHIPS, SPAN, 2 * HEAD_SIZE), BF16),),
        [keys, keys, rows, rows, stats, stats, sums, sums, table, table, table, table],
        12_000_000_000,
        "backward",
    )
    return part


def blocks_by_owner(owners, n, found):
    for b in range(N_CTX):
        found[owners[n, b]] = b


def feature_block(ref, b):
    return ref[:, pl.ds(pl.multiple_of(b * FEATURES, FEATURES), FEATURES)]


def out_kernel(columns, ids, owners, attn_ref, grad_ref, own_ref, other_ref, found):
    core = ids[0] % 2
    blocks_by_owner(owners, 2, found)
    attn_t = attn_ref[:, columns].astype(F32).T.astype(BF16)
    for out_ref, at in ((other_ref, 1 - core), (own_ref, core)):
        for chip in range(CHIPS):
            out_ref[chip] = nn(attn_t, feature_block(grad_ref, found[chip * 2 + at])).astype(BF16)


def out_gradient(ids, owner_map, attn, grad, half):
    part = jax.ShapeDtypeStruct((CHIPS, FEATURES, FEATURES), BF16)
    columns = slice(half * FEATURES, (half + 1) * FEATURES)

    def kernel(*refs):
        out_kernel(columns, *refs)

    return call(
        kernel,
        (ids, owner_map, attn, grad),
        (part, part),
        [pltpu.SMEM((N_CTX,), jnp.int32)],
        800_000_000,
        f"out_gradient_{half}",
    )


def kv_kernel(ids, owners, parts_ref, hidden_ref, own_ref, other_ref, found_k, found_v):
    core = ids[0] % 2
    blocks_by_owner(owners, 0, found_k)
    blocks_by_owner(owners, 1, found_v)
    total = jnp.sum(parts_ref[...].astype(F32), axis=0)
    both = []
    for n in range(2):
        t = total[:, n * HEAD_SIZE : (n + 1) * HEAD_SIZE].T
        high = t.astype(BF16)
        both.append(jnp.concatenate([high, (t - high.astype(F32)).astype(BF16)], axis=0))
    for out_ref, at in ((other_ref, 1 - core), (own_ref, core)):
        for chip in range(CHIPS):
            for n, found in enumerate((found_k, found_v)):
                block = nn(both[n], feature_block(hidden_ref, found[chip * 2 + at]))
                out_ref[chip, n * HEAD_SIZE : (n + 1) * HEAD_SIZE, :] = (
                    block[:HEAD_SIZE] + block[HEAD_SIZE:]
                ).astype(BF16)


def kv_gradient(ids, owner_map, parts, hidden):
    part = jax.ShapeDtypeStruct((CHIPS, 2 * HEAD_SIZE, FEATURES), BF16)
    found = pltpu.SMEM((N_CTX,), jnp.int32)
    return call(
        kv_kernel,
        (ids, owner_map, parts, hidden),
        (part, part),
        [found, found],
        1_600_000_000,
        "kv_gradient",
    )


SAME_CORE = [[c + 2 * chip for chip in range(CHIPS)] for c in range(2)]


def exchange(parts):
    return lax.all_to_all(parts, "ctx", 0, 0, tiled=True, axis_index_groups=SAME_CORE)


def chip_sum(own, other):
    return (own.astype(F32) + swap(other).astype(F32)).astype(BF16)


def after(value, *earlier):
    return lax.optimization_barrier((value, *earlier))[0]


def per_device(hidden_in, query, key, value, out_weight, grad_out, span_map, owner_map):
    ids = jnp.stack([lax.axis_index("ctx"), lax.axis_index("head")]).astype(jnp.int32)
    grad = lax.all_gather(grad_out, "head", axis=1, tiled=True)
    hidden = lax.all_gather(after(hidden_in, grad), "head", axis=1, tiled=True)
    kv_pieces = gather_over_ctx(jnp.concatenate([key, value], axis=1))
    query_other = swap(query)
    attn, lse = forward(ids, span_map, query, kv_pieces)
    d_attn = nt(grad, out_weight).astype(BF16)
    out_first = exchange(chip_sum(*out_gradient(ids, owner_map, attn, grad, 0)))
    sides = (query, query_other, d_attn, swap(d_attn), attn, swap(attn), lse, swap(lse))
    dkv = backward(ids, span_map, sides, kv_pieces[:8])
    attn_late = after(attn, dkv)
    dkv = exchange(dkv).reshape(CHIPS, TOKENS, 2 * HEAD_SIZE)
    out_second = chip_sum(*out_gradient(ids, owner_map, attn_late, grad, 1))
    out_second = exchange(after(out_second, dkv))
    kv_total = exchange(chip_sum(*kv_gradient(ids, owner_map, dkv, hidden)))
    kv_total = jnp.sum(kv_total.astype(F32), axis=0)
    out_total = jnp.concatenate(
        [jnp.sum(part.astype(F32), axis=0) for part in (out_first, out_second)], axis=0
    )
    return kv_total[:HEAD_SIZE].T, kv_total[HEAD_SIZE:].T, out_total


def solution(mesh):
    return jax.shard_map(
        per_device,
        mesh=mesh,
        in_specs=(
            P("ctx", "head"),
            P("ctx", "head"),
            P("ctx", "head"),
            P("ctx", "head"),
            P("head", None),
            P("ctx", "head"),
            P(),
            P(),
        ),
        out_specs=(P("ctx", "head"), P("ctx", "head"), P("head", "ctx")),
        check_vma=False,
    )
```

time: 668 us -> 219 us (0.33)
  waiting for transfers between devices: 424 us -> 100 us
  matrix products: 134 us -> 4.04 us
  Pallas kernels: 0 us -> 50.3 us
  local copies, waits for them, and re-layouts: 53.4 us -> 6.27 us
  starting transfers between devices: 3.78 us -> 35.2 us
  other arithmetic: 36.9 us -> 8.19 us
    ppermute x64 -> x22, waiting for transfers between devices: 208 us -> 9.86 us  [ctx_move(): return lax.ppermute(value, 'ctx', pairs)]
    reduce_scatter x3 -> x0, waiting for transfers between devices: 134 us -> none  [the longest x1 75 us: per_device(): lax.psum_scatter(ordered_key, 'ctx', scatter_dimension=0, tiled=True)]
    dot_general x53 -> x1, matrix products: 134 us -> 4.04 us  [nt(): lax.dot_general(a, b, (((1,), (1,)), ((), ())), preferred_element_type=F32)]
    pallas_call x0 -> x5, Pallas kernels: none -> 50.3 us  [call(): pl.pallas_call(kernel, out_shape=outputs, in_specs=[smem(), smem()] + [vm...]
    all_to_all x0 -> x4, waiting for transfers between devices: none -> 46.6 us  [exchange(): lax.all_to_all(parts, 'ctx', 0, 0, tiled=True, axis_index_groups=SAME_CORE)]
    all_gather x4 -> x2, waiting for transfers between devices: 80.4 us -> 43.3 us  [the longest x1 43.3 us: per_device(): grad = lax.all_gather(grad_out, 'head', axis=1, tiled=True)]
    gather x4 -> x0, local copies, waits for them, and re-layouts: 21.9 us -> none  [the longest x2 17.2 us: per_device(): jnp.take(out_grad.reshape(query_local * HEAD_SIZE, cycle_size, block_exte...]
    all_to_all x0 -> x4, starting transfers between devices: none -> 19.8 us  [exchange(): lax.all_to_all(parts, 'ctx', 0, 0, tiled=True, axis_index_groups=SAME_CORE)]
  transfers between devices with their start and end apart: 71 -> 28, of which waited for: 37 -> 11; matrix products, arithmetic and copies ran while one was open for 33% -> 7% of each run, Pallas kernels for 0% -> 23%
where the time goes in v2:
time: 219 us
  waiting for transfers between devices  100 us (46%)
  Pallas kernels  50.3 us (23%)
  starting transfers between devices  35.2 us (16%)
  between operations  14.2 us (6%)
  other arithmetic  8.19 us (4%)
  local copies, waits for them, and re-layouts  6.27 us (3%)
  matrix products  4.04 us (2%)
    pallas_call x5, Pallas kernels, call(): pl.pallas_call(kernel, out_shape=outputs, in_specs=[smem(), smem()] + [vm...  50.3 us
    all_to_all x4, waiting for transfers between devices, exchange(): lax.all_to_all(parts, 'ctx', 0, 0, tiled=True, axis_index_groups=SAME_CORE)  46.6 us
    all_gather x1, waiting for transfers between devices, per_device(): grad = lax.all_gather(grad_out, 'head', axis=1, tiled=True)  43.3 us
    all_to_all x4, starting transfers between devices, exchange(): lax.all_to_all(parts, 'ctx', 0, 0, tiled=True, axis_index_groups=SAME_CORE)  19.8 us
    ppermute x22, starting transfers between devices, ctx_move(): return lax.ppermute(value, 'ctx', pairs)  15.4 us
    ppermute x22, waiting for transfers between devices, ctx_move(): return lax.ppermute(value, 'ctx', pairs)  9.86 us
    convert_element_type x3, other arithmetic, chip_sum(): return (own.astype(F32) + swap(other).astype(F32)).astype(BF16)  6.32 us
    unnamed x38, local copies, waits for them, and re-layouts  5.33 us
  transfers between devices with their start and end apart: 28, of which 11 were waited for; matrix products, arithmetic and copies ran while one was open for 7% of the time, Pallas kernels for 23%

profile of v2, /device:TPU:0, one launch (start us, length us, event | category | flops | bytes accessed | tf_op | source)
XLA Modules:
  0.0 218.7 jit_solution(789677081513200297)
XLA Ops:
  7.2 0.0 all-gather.3.cloned.1.call-start
  7.2 0.7 all-gather.3.cloned.1.call-update
  7.9 0.0 all-gather.5.cloned.1.call-start
  7.9 0.9 constant_dynamic-update-slice_fusion.1
  8.9 0.9 constant_dynamic-update-slice_fusion.rest_0_.rest_8_
  9.8 3.2 %collective-permute-start.2 = (bf16[384,256]{1,0:T(8,128)(2,1)S(1)}, bf16[384,256]{1,0:T(8,128)(2,1)S(1)}, u32[]{:S(2)}, u32[]{:S(2)}) collective-permute-start(bf16[384,256]{1,0:T(8,128)(2,1)S(1)} %constant_dynamic-update-slice_fusion.rest_0_.rest_8_), channel_id=1, source_target_pairs={{0,64},{8,72},{16,80},{24,88},{32,96},{40,104},{48,112},{56,120},{... | collective-permute-start | bytes 589832 | tf_op jit(solution)/shard_map/ppermute | solution.py:32
  13.0 43.3 %all-gather.3.cloned.1.call-done.refs_3_ = bf16[384,4096]{1,0:T(8,128)(2,1)} async-done(((bf16[384,512]{1,0:T(8,128)(2,1)}), bf16[384,4096]{1,0:T(8,128)(2,1)}) %all-gather.3.cloned.1.call-update) | async-done | bytes 3145744 | tf_op jit(solution)/shard_map/all_gather | solution.py:355
  56.3 0.0 all-gather.5.cloned.1.call-update
  56.3 1.6 collective-permute-start.3
  57.9 1.7 collective-permute-start.4
  59.6 1.8 collective-permute-start.6
  61.4 0.3 collective-permute-start.5
  61.7 1.5 collective-permute-done.3.rest_2_.rest_10_
  63.3 0.3 collective-permute-start.7
  63.6 0.9 collective-permute-done.4.rest_3_.rest_11_
  64.6 0.5 collective-permute-start.11
  65.1 2.9 %collective-permute-done.6.rest_5_.rest_13_ = bf16[384,256]{1,0:T(8,128)(2,1)} collective-permute-done((bf16[384,256]{1,0:T(8,128)(2,1)S(1)}, bf16[384,256]{1,0:T(8,128)(2,1)}, u32[]{:S(2)}, u32[]{:S(2)}) %collective-permute-start.6) | collective-permute-done | bytes 196640 | tf_op jit(solution)/shard_map/ppermute | solution.py:32
  67.9 2.9 %collective-permute-start.8 = (bf16[384,256]{1,0:T(8,128)(2,1)}, bf16[384,256]{1,0:T(8,128)(2,1)}, u32[]{:S(2)}, u32[]{:S(2)}) collective-permute-start(bf16[384,256]{1,0:T(8,128)(2,1)} %collective-permute-done.6.rest_5_.rest_13_), channel_id=1, source_target_pairs={{0,48},{8,56},{16,0},{24,8},{32,16},{40,24},{48,32},{56,40},{64,11... | collective-permute-start | bytes 589832 | tf_op jit(solution)/shard_map/ppermute | solution.py:32
  70.8 0.0 collective-permute-start.12
  70.8 3.1 %collective-permute-done.7.rest_6_.rest_14_ = bf16[384,256]{1,0:T(8,128)(2,1)} collective-permute-done((bf16[384,256]{1,0:T(8,128)(2,1)S(1)}, bf16[384,256]{1,0:T(8,128)(2,1)}, u32[]{:S(2)}, u32[]{:S(2)}) %collective-permute-start.7) | collective-permute-done | bytes 196640 | tf_op jit(solution)/shard_map/ppermute | solution.py:32
  74.0 0.5 collective-permute-start.13
  74.5 0.0 collective-permute-done.11.rest_10_
  74.5 0.1 collective-permute-start.15
  74.6 0.2 collective-permute-done.8.rest_7_.rest_15_
  74.8 0.2 collective-permute-start.16
  75.0 1.4 copy.14.spans
  76.4 0.6 pad_add_fusion.ids.refs_0_
  77.0 0.3 collective-permute-start
  77.3 0.0 collective-permute-done.14.rest_13_
  77.3 0.0 collective-permute-done.13.rest_12_
  77.3 0.0 collective-permute-done.15.rest_14_
  77.4 15.2 %forward.1 = (bf16[384,512]{1,0:T(8,128)(2,1)}, f32[2,8,768]{2,1,0:T(8,128)}) custom-call(s32[2]{0:T(128)} %pad_add_fusion.ids.refs_0_, s32[16,2]{1,0:T(8,128)} %copy.14.spans, bf16[384,512]{1,0:T(8,128)(2,1)} %rest_0_.1, bf16[384,256]{1,0:T(8,128)(2,1)} %copy-done.5, bf16[384,256]{1,0:T(8,128)(2,1)} %copy-done.10, bf16[384,256]{1,0:T(8,128)(2,1)} %copy-done.11, ...), custom_call_target="tpu_custom_call" | custom-call | flops 10000000000 | bytes 3981448 | tf_op jit(solution)/shard_map/forward/pallas_call | solution.py:151
  92.6 0.2 collective-permute-start.17
  92.8 4.0 %convolution_convert_fusion.rest_2_ = bf16[384,512]{1,0:T(8,128)(2,1)S(1)} fusion(bf16[384,4096]{1,0:T(8,128)(2,1)S(1)} %copy-done, bf16[512,4096]{1,0:T(8,128)(2,1)} %param.12), kind=kOutput, calls=%fused_computation.6 | convolution fusion | flops 1610809344 | bytes 7733248 | tf_op jit(solution)/shard_map/dot_general | solution.py:61
  96.8 0.5 collective-permute-start.1
  97.3 0.3 collective-permute-start.18
  97.6 1.1 collective-permute-done.18.rest_7_
  98.8 0.6 copy-done.16
  99.3 0.1 copy-done.7
  99.5 0.8 copy-done.9
  100.3 20.4 %backward.1 = bf16[16,192,256]{2,1,0:T(8,128)(2,1)} custom-call(s32[2]{0:T(128)} %pad_add_fusion.ids.refs_0_, s32[16,2]{1,0:T(8,128)} %copy.14.spans, bf16[384,512]{1,0:T(8,128)(2,1)} %rest_0_.1, bf16[384,512]{1,0:T(8,128)(2,1)} %copy-done.6, bf16[384,512]{1,0:T(8,128)(2,1)} %copy-done.8, bf16[384,512]{1,0:T(8,128)(2,1)} %copy-done.9, ...), custom_call_target="tpu_custom_call" | custom-call | flops 12000000000 | bytes 5603464 | tf_op jit(solution)/shard_map/backward/pallas_call | solution.py:151
  120.6 6.4 %all-to-all-start = ((bf16[16,192,256]{2,1,0:T(8,128)(2,1)}), bf16[16,192,256]{2,1,0:T(8,128)(2,1)S(1)}, u32[]{:S(2)}, u32[]{:S(2)}) async-start(bf16[16,192,256]{2,1,0:T(8,128)(2,1)} %backward.1), calls=%async_computation | async-start | bytes 3145728 | tf_op jit(solution)/shard_map/all_to_all | solution.py:342
  127.1 4.3 %out_gradient_0.1 = (bf16[8,256,256]{2,1,0:T(8,128)(2,1)}, bf16[8,256,256]{2,1,0:T(8,128)(2,1)}) custom-call(s32[2]{0:T(128)} %pad_add_fusion.ids.refs_0_, s32[3,16]{1,0:T(4,128)} %refs_1_.3, bf16[384,512]{1,0:T(8,128)(2,1)} %get-tuple-element.21.rest_4_.refs_2_, bf16[384,4096]{1,0:T(8,128)(2,1)} %all-gather.3.cloned.1.call-done.refs_3_), custom_call_target="tpu_custom_call" | custom-call | flops 800000000 | bytes 5636296 | tf_op jit(solution)/shard_map/out_gradient_0/pallas_call | solution.py:151
  131.4 0.9 collective-permute-start.20
  132.3 4.4 %out_gradient_1.1 = (bf16[8,256,256]{2,1,0:T(8,128)(2,1)}, bf16[8,256,256]{2,1,0:T(8,128)(2,1)}) custom-call(s32[2]{0:T(128)} %pad_add_fusion.ids.refs_0_, s32[3,16]{1,0:T(4,128)} %refs_1_.3, bf16[384,512]{1,0:T(8,128)(2,1)} %get-tuple-element.21.rest_4_.refs_2_, bf16[384,4096]{1,0:T(8,128)(2,1)} %all-gather.3.cloned.1.call-done.refs_3_), custom_call_target="tpu_custom_call" | custom-call | flops 800000000 | bytes 5636296 | tf_op jit(solution)/shard_map/out_gradient_1/pallas_call | solution.py:151
  136.7 0.1 collective-permute-start.21
  136.7 1.2 add_convert_fusion.1
  138.0 11.2 %all-to-all-done = bf16[16,192,256]{2,1,0:T(8,128)(2,1)S(1)} async-done(((bf16[16,192,256]{2,1,0:T(8,128)(2,1)}), bf16[16,192,256]{2,1,0:T(8,128)(2,1)S(1)}, u32[]{:S(2)}, u32[]{:S(2)}) %all-to-all-start) | async-done | bytes 1572896 | tf_op jit(solution)/shard_map/all_to_all | solution.py:342
  149.2 4.8 %all-to-all-start.2 = ((bf16[8,256,256]{2,1,0:T(8,128)(2,1)}), bf16[8,256,256]{2,1,0:T(8,128)(2,1)S(1)}, u32[]{:S(2)}, u32[]{:S(2)}) async-start(bf16[8,256,256]{2,1,0:T(8,128)(2,1)} %add_convert_fusion.1), calls=%async_computation.2 | async-start | bytes 2097152 | tf_op jit(solution)/shard_map/all_to_all | solution.py:342
  153.9 0.0 all-gather.5.cloned.1.call-done.hidden_ref
  154.0 6.0 %kv_gradient.1 = (bf16[8,256,256]{2,1,0:T(8,128)(2,1)}, bf16[8,256,256]{2,1,0:T(8,128)(2,1)}) custom-call(s32[2]{0:T(128)} %pad_add_fusion.ids.refs_0_, s32[3,16]{1,0:T(4,128)} %refs_1_.3, bf16[8,384,256]{2,1,0:T(8,128)(2,1)} %bitcast.9, bf16[384,4096]{1,0:T(8,128)(2,1)} %all-gather.5.cloned.1.call-done.hidden_ref), custom_call_target="tpu_custom_call" | custom-call | flops 1600000000 | bytes 6815944 | tf_op jit(solution)/shard_map/kv_gradient/pallas_call | solution.py:151
  160.0 2.6 %add_convert_fusion = bf16[8,256,256]{2,1,0:T(8,128)(2,1)} fusion(bf16[8,256,256]{2,1,0:T(8,128)(2,1)} %collective-permute-done.21, bf16[8,256,256]{2,1,0:T(8,128)(2,1)S(1)} %copy-done.2), kind=kLoop, calls=%fused_computation.1 | loop fusion | flops 2097152 | bytes 3145728 | tf_op jit(solution)/shard_map/convert_element_type | solution.py:346
  162.6 7.2 %all-to-all-done.2 = bf16[8,256,256]{2,1,0:T(8,128)(2,1)S(1)} async-done(((bf16[8,256,256]{2,1,0:T(8,128)(2,1)}), bf16[8,256,256]{2,1,0:T(8,128)(2,1)S(1)}, u32[]{:S(2)}, u32[]{:S(2)}) %all-to-all-start.2) | async-done | bytes 1048608 | tf_op jit(solution)/shard_map/all_to_all | solution.py:342
  169.8 4.3 %all-to-all-start.3 = ((bf16[8,256,256]{2,1,0:T(8,128)(2,1)}), bf16[8,256,256]{2,1,0:T(8,128)(2,1)S(1)}, u32[]{:S(2)}, u32[]{:S(2)}) async-start(bf16[8,256,256]{2,1,0:T(8,128)(2,1)} %add_convert_fusion), calls=%async_computation.3 | async-start | bytes 2097152 | tf_op jit(solution)/shard_map/all_to_all | solution.py:342
  174.2 2.5 %add_convert_fusion.2 = bf16[8,256,256]{2,1,0:T(8,128)(2,1)} fusion(bf16[8,256,256]{2,1,0:T(8,128)(2,1)} %collective-permute-done.19, bf16[8,256,256]{2,1,0:T(8,128)(2,1)S(1)} %copy-done.3), kind=kLoop, calls=%fused_computation.5 | loop fusion | flops 2097152 | bytes 3145728 | tf_op jit(solution)/shard_map/convert_element_type | solution.py:346
  176.7 13.4 %all-to-all-done.3 = bf16[8,256,256]{2,1,0:T(8,128)(2,1)S(1)} async-done(((bf16[8,256,256]{2,1,0:T(8,128)(2,1)}), bf16[8,256,256]{2,1,0:T(8,128)(2,1)S(1)}, u32[]{:S(2)}, u32[]{:S(2)}) %all-to-all-start.3) | async-done | bytes 1048608 | tf_op jit(solution)/shard_map/all_to_all | solution.py:342
  190.0 4.2 %all-to-all-start.1 = ((bf16[8,256,256]{2,1,0:T(8,128)(2,1)}), bf16[8,256,256]{2,1,0:T(8,128)(2,1)S(1)}, u32[]{:S(2)}, u32[]{:S(2)}) async-start(bf16[8,256,256]{2,1,0:T(8,128)(2,1)} %add_convert_fusion.2), calls=%async_computation.1 | async-start | bytes 2097152 | tf_op jit(solution)/shard_map/all_to_all | solution.py:342
  194.3 0.1 convert_reduce_fusion.1
  194.4 0.1 convert_reduce_fusion
  194.6 0.8 pad_maximum_fusion
  195.4 14.8 %all-to-all-done.1 = bf16[8,256,256]{2,1,0:T(8,128)(2,1)S(1)} async-done(((bf16[8,256,256]{2,1,0:T(8,128)(2,1)}), bf16[8,256,256]{2,1,0:T(8,128)(2,1)S(1)}, u32[]{:S(2)}, u32[]{:S(2)}) %all-to-all-start.1) | async-done | bytes 1048608 | tf_op jit(solution)/shard_map/all_to_all | solution.py:342
  210.2 0.1 convert_reduce_fusion.2
  210.3 0.8 copy.15
  211.1 0.8 copy.16
  (48 shorter events, 0.1 us)
Async XLA Ops:
  7.2 49.1 %all-gather.3.cloned.1.call-start = ((), (), s32[]{:S(2)}) async-start(), calls=%async_computation.4 | async-start | bytes 3538944 | tf_op jit(solution)/shard_map/all_gather | solution.py:355
  7.9 146.1 %all-gather.5.cloned.1.call-start = ((), (), s32[]{:S(2)}) async-start(), calls=%async_computation.5 | async-start | bytes 3538944 | tf_op jit(solution)/shard_map/all_gather | solution.py:356
  9.8 67.6 %copy-start.5 = (bf16[384,256]{1,0:T(8,128)(2,1)}, bf16[384,256]{1,0:T(8,128)(2,1)S(1)}, u32[]{:S(2)}) copy-start(bf16[384,256]{1,0:T(8,128)(2,1)S(1)} %constant_dynamic-update-slice_fusion.rest_0_.rest_8_) | copy-start | bytes 589828
  9.8 49.8 %collective-permute-start.2 = (bf16[384,256]{1,0:T(8,128)(2,1)S(1)}, bf16[384,256]{1,0:T(8,128)(2,1)S(1)}, u32[]{:S(2)}, u32[]{:S(2)}) collective-permute-start(bf16[384,256]{1,0:T(8,128)(2,1)S(1)} %constant_dynamic-update-slice_fusion.rest_0_.rest_8_), channel_id=1, source_target_pairs={{0,64},{8,72},{16,80},{24,88},{32,96},{40,104},{48,112},{56,120},{... | collective-permute-start | bytes 589832 | tf_op jit(solution)/shard_map/ppermute | solution.py:32
  56.3 7.0 %collective-permute-start.3 = (bf16[384,256]{1,0:T(8,128)(2,1)S(1)}, bf16[384,256]{1,0:T(8,128)(2,1)S(1)}, u32[]{:S(2)}, u32[]{:S(2)}) collective-permute-start(bf16[384,256]{1,0:T(8,128)(2,1)S(1)} %constant_dynamic-update-slice_fusion.rest_0_.rest_8_), channel_id=1, source_target_pairs={{0,16},{8,24},{16,32},{24,40},{32,48},{40,56},{48,0},{56,8},{64,80... | collective-permute-start | bytes 589832 | tf_op jit(solution)/shard_map/ppermute | solution.py:32
  57.9 6.6 %collective-permute-start.4 = (bf16[384,256]{1,0:T(8,128)(2,1)S(1)}, bf16[384,256]{1,0:T(8,128)(2,1)}, u32[]{:S(2)}, u32[]{:S(2)}) collective-permute-start(bf16[384,256]{1,0:T(8,128)(2,1)S(1)} %constant_dynamic-update-slice_fusion.rest_0_.rest_8_), channel_id=1, source_target_pairs={{0,48},{8,56},{16,0},{24,8},{32,16},{40,24},{48,32},{56,40},{64,11... | collective-permute-start | bytes 589832 | tf_op jit(solution)/shard_map/ppermute | solution.py:32
  59.6 4.9 %collective-permute-start.9 = (bf16[384,256]{1,0:T(8,128)(2,1)S(1)}, bf16[384,256]{1,0:T(8,128)(2,1)S(1)}, u32[]{:S(2)}, u32[]{:S(2)}) collective-permute-start(bf16[384,256]{1,0:T(8,128)(2,1)S(1)} %constant_dynamic-update-slice_fusion.rest_0_.rest_8_), channel_id=1, source_target_pairs={{0,8},{8,0},{16,24},{24,16},{32,40},{40,32},{48,56},{56,48},{64,72... | collective-permute-start | bytes 589832 | tf_op jit(solution)/shard_map/ppermute | solution.py:32
  59.6 17.7 %copy-start.10 = (bf16[384,256]{1,0:T(8,128)(2,1)}, bf16[384,256]{1,0:T(8,128)(2,1)S(1)}, u32[]{:S(2)}) copy-start(bf16[384,256]{1,0:T(8,128)(2,1)S(1)} %collective-permute-done.2.rest_1_.rest_9_) | copy-start | bytes 589828
  59.6 8.3 %collective-permute-start.6 = (bf16[384,256]{1,0:T(8,128)(2,1)S(1)}, bf16[384,256]{1,0:T(8,128)(2,1)}, u32[]{:S(2)}, u32[]{:S(2)}) collective-permute-start(bf16[384,256]{1,0:T(8,128)(2,1)S(1)} %collective-permute-done.2.rest_1_.rest_9_), channel_id=1, source_target_pairs={{0,48},{8,56},{16,0},{24,8},{32,16},{40,24},{48,32},{56,40},{64,11... | collective-permute-start | bytes 589832 | tf_op jit(solution)/shard_map/ppermute | solution.py:32
  61.4 9.4 %collective-permute-start.5 = (bf16[384,256]{1,0:T(8,128)(2,1)S(1)}, bf16[384,256]{1,0:T(8,128)(2,1)}, u32[]{:S(2)}, u32[]{:S(2)}) collective-permute-start(bf16[384,256]{1,0:T(8,128)(2,1)S(1)} %collective-permute-done.2.rest_1_.rest_9_), channel_id=1, source_target_pairs={{0,16},{8,24},{16,32},{24,40},{32,48},{40,56},{48,0},{56,8},{64,80... | collective-permute-start | bytes 589832 | tf_op jit(solution)/shard_map/ppermute | solution.py:32
  63.3 13.1 %copy-start.11 = (bf16[384,256]{1,0:T(8,128)(2,1)}, bf16[384,256]{1,0:T(8,128)(2,1)S(1)}, u32[]{:S(2)}) copy-start(bf16[384,256]{1,0:T(8,128)(2,1)S(1)} %collective-permute-done.3.rest_2_.rest_10_) | copy-start | bytes 589828
  63.3 10.7 %collective-permute-start.7 = (bf16[384,256]{1,0:T(8,128)(2,1)S(1)}, bf16[384,256]{1,0:T(8,128)(2,1)}, u32[]{:S(2)}, u32[]{:S(2)}) collective-permute-start(bf16[384,256]{1,0:T(8,128)(2,1)S(1)} %collective-permute-done.3.rest_2_.rest_10_), channel_id=1, source_target_pairs={{0,16},{8,24},{16,32},{24,40},{32,48},{40,56},{48,0},{56,8},{64,80... | collective-permute-start | bytes 589832 | tf_op jit(solution)/shard_map/ppermute | solution.py:32
  64.6 9.4 %collective-permute-start.10 = (bf16[384,256]{1,0:T(8,128)(2,1)S(1)}, bf16[384,256]{1,0:T(8,128)(2,1)S(1)}, u32[]{:S(2)}, u32[]{:S(2)}) collective-permute-start(bf16[384,256]{1,0:T(8,128)(2,1)S(1)} %collective-permute-done.2.rest_1_.rest_9_), channel_id=1, source_target_pairs={{0,8},{8,0},{16,24},{24,16},{32,40},{40,32},{48,56},{56,48},{64,72... | collective-permute-start | bytes 589832 | tf_op jit(solution)/shard_map/ppermute | solution.py:32
  64.6 11.8 %copy-start.12 = (bf16[384,256]{1,0:T(8,128)(2,1)}, bf16[384,256]{1,0:T(8,128)(2,1)S(1)}, u32[]{:S(2)}) copy-start(bf16[384,256]{1,0:T(8,128)(2,1)S(1)} %collective-permute-done.9.rest_8_) | copy-start | bytes 589828
  64.6 9.9 %collective-permute-start.11 = (bf16[384,256]{1,0:T(8,128)(2,1)S(1)}, bf16[384,256]{1,0:T(8,128)(2,1)S(1)}, u32[]{:S(2)}, u32[]{:S(2)}) collective-permute-start(bf16[384,256]{1,0:T(8,128)(2,1)S(1)} %collective-permute-done.3.rest_2_.rest_10_), channel_id=1, source_target_pairs={{0,8},{8,0},{16,24},{24,16},{32,40},{40,32},{48,56},{56,48},{64,72... | collective-permute-start | bytes 589832 | tf_op jit(solution)/shard_map/ppermute | solution.py:32
  67.9 6.9 %collective-permute-start.8 = (bf16[384,256]{1,0:T(8,128)(2,1)}, bf16[384,256]{1,0:T(8,128)(2,1)}, u32[]{:S(2)}, u32[]{:S(2)}) collective-permute-start(bf16[384,256]{1,0:T(8,128)(2,1)} %collective-permute-done.6.rest_5_.rest_13_), channel_id=1, source_target_pairs={{0,48},{8,56},{16,0},{24,8},{32,16},{40,24},{48,32},{56,40},{64,11... | collective-permute-start | bytes 589832 | tf_op jit(solution)/shard_map/ppermute | solution.py:32
  70.8 6.2 %collective-permute-start.12 = (bf16[384,256]{1,0:T(8,128)(2,1)}, bf16[384,256]{1,0:T(8,128)(2,1)}, u32[]{:S(2)}, u32[]{:S(2)}) collective-permute-start(bf16[384,256]{1,0:T(8,128)(2,1)} %collective-permute-done.4.rest_3_.rest_11_), channel_id=1, source_target_pairs={{0,8},{8,0},{16,24},{24,16},{32,40},{40,32},{48,56},{56,48},{64,72... | collective-permute-start | bytes 589832 | tf_op jit(solution)/shard_map/ppermute | solution.py:32
  74.0 3.4 %collective-permute-start.14 = (bf16[384,256]{1,0:T(8,128)(2,1)}, bf16[384,256]{1,0:T(8,128)(2,1)}, u32[]{:S(2)}, u32[]{:S(2)}) collective-permute-start(bf16[384,256]{1,0:T(8,128)(2,1)} %collective-permute-done.6.rest_5_.rest_13_), channel_id=1, source_target_pairs={{0,8},{8,0},{16,24},{24,16},{32,40},{40,32},{48,56},{56,48},{64,72... | collective-permute-start | bytes 589832 | tf_op jit(solution)/shard_map/ppermute | solution.py:32
  74.0 2.4 %copy-start.13 = (bf16[384,256]{1,0:T(8,128)(2,1)}, bf16[384,256]{1,0:T(8,128)(2,1)S(1)}, u32[]{:S(2)}) copy-start(bf16[384,256]{1,0:T(8,128)(2,1)S(1)} %collective-permute-done.10.rest_9_) | copy-start | bytes 589828
  74.0 3.4 %collective-permute-start.13 = (bf16[384,256]{1,0:T(8,128)(2,1)}, bf16[384,256]{1,0:T(8,128)(2,1)}, u32[]{:S(2)}, u32[]{:S(2)}) collective-permute-start(bf16[384,256]{1,0:T(8,128)(2,1)} %collective-permute-done.5.rest_4_.rest_12_), channel_id=1, source_target_pairs={{0,8},{8,0},{16,24},{24,16},{32,40},{40,32},{48,56},{56,48},{64,72... | collective-permute-start | bytes 589832 | tf_op jit(solution)/shard_map/ppermute | solution.py:32
  74.5 1.9 copy-start.14
  74.5 2.9 %collective-permute-start.15 = (bf16[384,256]{1,0:T(8,128)(2,1)}, bf16[384,256]{1,0:T(8,128)(2,1)}, u32[]{:S(2)}, u32[]{:S(2)}) collective-permute-start(bf16[384,256]{1,0:T(8,128)(2,1)} %collective-permute-done.7.rest_6_.rest_14_), channel_id=1, source_target_pairs={{0,8},{8,0},{16,24},{24,16},{32,40},{40,32},{48,56},{56,48},{64,72... | collective-permute-start | bytes 589832 | tf_op jit(solution)/shard_map/ppermute | solution.py:32
  74.8 2.5 %collective-permute-start.16 = (bf16[384,256]{1,0:T(8,128)(2,1)}, bf16[384,256]{1,0:T(8,128)(2,1)}, u32[]{:S(2)}, u32[]{:S(2)}) collective-permute-start(bf16[384,256]{1,0:T(8,128)(2,1)} %collective-permute-done.8.rest_7_.rest_15_), channel_id=1, source_target_pairs={{0,8},{8,0},{16,24},{24,16},{32,40},{40,32},{48,56},{56,48},{64,72... | collective-permute-start | bytes 589832 | tf_op jit(solution)/shard_map/ppermute | solution.py:32
  77.0 15.8 %copy-start = (bf16[384,4096]{1,0:T(8,128)(2,1)S(1)}, bf16[384,4096]{1,0:T(8,128)(2,1)}, u32[]{:S(2)}) copy-start(bf16[384,4096]{1,0:T(8,128)(2,1)} %all-gather.3.cloned.1.call-done.refs_3_) | copy-start | bytes 9437188
  77.0 20.6 %collective-permute-start = (bf16[384,512]{1,0:T(8,128)(2,1)}, bf16[384,512]{1,0:T(8,128)(2,1)S(1)}, u32[]{:S(2)}, u32[]{:S(2)}) collective-permute-start(bf16[384,512]{1,0:T(8,128)(2,1)} %rest_0_.1), channel_id=1, source_target_pairs={{0,8},{8,0},{16,24},{24,16},{32,40},{40,32},{48,56},{56,48},{64,72... | collective-permute-start | bytes 1179656 | tf_op jit(solution)/shard_map/ppermute | solution.py:32
  92.6 4.7 %copy-start.15 = (f32[2,8,768]{2,1,0:T(8,128)S(1)}, f32[2,8,768]{2,1,0:T(8,128)}, u32[]{:S(2)}) copy-start(f32[2,8,768]{2,1,0:T(8,128)} %get-tuple-element.15.rest_6_) | copy-start | bytes 147460
  92.6 6.2 %collective-permute-start.17 = (bf16[384,512]{1,0:T(8,128)(2,1)}, bf16[384,512]{1,0:T(8,128)(2,1)S(1)}, u32[]{:S(2)}, u32[]{:S(2)}) collective-permute-start(bf16[384,512]{1,0:T(8,128)(2,1)} %get-tuple-element.21.rest_4_.refs_2_), channel_id=1, source_target_pairs={{0,8},{8,0},{16,24},{24,16},{32,40},{40,32},{48,56},{56,48},{64,72... | collective-permute-start | bytes 1179656 | tf_op jit(solution)/shard_map/ppermute | solution.py:32
  96.8 1.9 copy-start.8
  96.8 1.9 collective-permute-start.1
  97.3 1.4 collective-permute-start.18
  97.6 1.2 copy-start.6
  98.7 0.6 copy-start.16
  98.7 0.8 copy-start.7
  99.5 0.8 copy-start.9
  120.6 28.6 %all-to-all-start = ((bf16[16,192,256]{2,1,0:T(8,128)(2,1)}), bf16[16,192,256]{2,1,0:T(8,128)(2,1)S(1)}, u32[]{:S(2)}, u32[]{:S(2)}) async-start(bf16[16,192,256]{2,1,0:T(8,128)(2,1)} %backward.1), calls=%async_computation | async-start | bytes 3145728 | tf_op jit(solution)/shard_map/all_to_all | solution.py:342
  131.4 5.4 %copy-start.4 = (bf16[8,256,256]{2,1,0:T(8,128)(2,1)S(1)}, bf16[8,256,256]{2,1,0:T(8,128)(2,1)}, u32[]{:S(2)}) copy-start(bf16[8,256,256]{2,1,0:T(8,128)(2,1)} %get-tuple-element.19) | copy-start | bytes 3145732
  131.4 5.4 %collective-permute-start.20 = (bf16[8,256,256]{2,1,0:T(8,128)(2,1)}, bf16[8,256,256]{2,1,0:T(8,128)(2,1)S(1)}, u32[]{:S(2)}, u32[]{:S(2)}) collective-permute-start(bf16[8,256,256]{2,1,0:T(8,128)(2,1)} %get-tuple-element.20), channel_id=1, source_target_pairs={{0,8},{8,0},{16,24},{24,16},{32,40},{40,32},{48,56},{56,48},{64,72... | collective-permute-start | bytes 3145736 | tf_op jit(solution)/shard_map/ppermute | solution.py:32
  136.7 23.3 %collective-permute-start.21 = (bf16[8,256,256]{2,1,0:T(8,128)(2,1)}, bf16[8,256,256]{2,1,0:T(8,128)(2,1)}, u32[]{:S(2)}, u32[]{:S(2)}) collective-permute-start(bf16[8,256,256]{2,1,0:T(8,128)(2,1)} %get-tuple-element.23), channel_id=1, source_target_pairs={{0,8},{8,0},{16,24},{24,16},{32,40},{40,32},{48,56},{56,48},{64,72... | collective-permute-start | bytes 3145736 | tf_op jit(solution)/shard_map/ppermute | solution.py:32
  149.2 4.8 %copy-start.1 = (bf16[16,192,256]{2,1,0:T(8,128)(2,1)}, bf16[16,192,256]{2,1,0:T(8,128)(2,1)S(1)}, u32[]{:S(2)}) copy-start(bf16[16,192,256]{2,1,0:T(8,128)(2,1)S(1)} %all-to-all-done) | copy-start | bytes 4718596
  149.2 20.6 %all-to-all-start.2 = ((bf16[8,256,256]{2,1,0:T(8,128)(2,1)}), bf16[8,256,256]{2,1,0:T(8,128)(2,1)S(1)}, u32[]{:S(2)}, u32[]{:S(2)}) async-start(bf16[8,256,256]{2,1,0:T(8,128)(2,1)} %add_convert_fusion.1), calls=%async_computation.2 | async-start | bytes 2097152 | tf_op jit(solution)/shard_map/all_to_all | solution.py:342
  154.0 6.0 %copy-start.2 = (bf16[8,256,256]{2,1,0:T(8,128)(2,1)S(1)}, bf16[8,256,256]{2,1,0:T(8,128)(2,1)}, u32[]{:S(2)}) copy-start(bf16[8,256,256]{2,1,0:T(8,128)(2,1)} %get-tuple-element.22) | copy-start | bytes 3145732
  160.0 14.2 %collective-permute-start.19 = (bf16[8,256,256]{2,1,0:T(8,128)(2,1)}, bf16[8,256,256]{2,1,0:T(8,128)(2,1)}, u32[]{:S(2)}, u32[]{:S(2)}) collective-permute-start(bf16[8,256,256]{2,1,0:T(8,128)(2,1)} %get-tuple-element.18), channel_id=1, source_target_pairs={{0,8},{8,0},{16,24},{24,16},{32,40},{40,32},{48,56},{56,48},{64,72... | collective-permute-start | bytes 3145736 | tf_op jit(solution)/shard_map/ppermute | solution.py:32
  160.0 14.2 %copy-start.3 = (bf16[8,256,256]{2,1,0:T(8,128)(2,1)S(1)}, bf16[8,256,256]{2,1,0:T(8,128)(2,1)}, u32[]{:S(2)}) copy-start(bf16[8,256,256]{2,1,0:T(8,128)(2,1)} %get-tuple-element.17) | copy-start | bytes 3145732
  169.8 20.2 %all-to-all-start.3 = ((bf16[8,256,256]{2,1,0:T(8,128)(2,1)}), bf16[8,256,256]{2,1,0:T(8,128)(2,1)S(1)}, u32[]{:S(2)}, u32[]{:S(2)}) async-start(bf16[8,256,256]{2,1,0:T(8,128)(2,1)} %add_convert_fusion), calls=%async_computation.3 | async-start | bytes 2097152 | tf_op jit(solution)/shard_map/all_to_all | solution.py:342
  190.0 20.1 %all-to-all-start.1 = ((bf16[8,256,256]{2,1,0:T(8,128)(2,1)}), bf16[8,256,256]{2,1,0:T(8,128)(2,1)S(1)}, u32[]{:S(2)}, u32[]{:S(2)}) async-start(bf16[8,256,256]{2,1,0:T(8,128)(2,1)} %add_convert_fusion.2), calls=%async_computation.1 | async-start | bytes 2097152 | tf_op jit(solution)/shard_map/all_to_all | solution.py:342
Sparse Core Ops, SparseCore 0:
  9.6 46.6 all-gather.2
  57.9 43.9 all-gather.4

commit v3 on v2

--- a/solution.py
+++ b/solution.py
@@ -17,6 +17,7 @@
 OWN_BLOCKS = 8
 ROWS = GROUP * SPAN
 FEATURES = 256
+HEAD_COLUMNS = 512
 SCALE = HEAD_SIZE ** (-0.5)
 EXP2_SCALE = SCALE * 1.4426950408889634
 F32 = jnp.float32
@@ -147,7 +148,6 @@
 
 
 def call(kernel, inputs, outputs, scratch, flops, name):
-    bytes_moved = sum(x.size * x.dtype.itemsize for x in list(inputs) + list(outputs))
     return pl.pallas_call(
         kernel,
         out_shape=outputs,
@@ -155,7 +155,7 @@
         out_specs=(vmem(),) * len(outputs),
         scratch_shapes=scratch,
         compiler_params=pltpu.CompilerParams(vmem_limit_bytes=VMEM_BYTES),
-        cost_estimate=pl.CostEstimate(flops=flops, bytes_accessed=bytes_moved, transcendentals=0),
+        cost_estimate=pl.CostEstimate(flops=flops, bytes_accessed=1024, transcendentals=0),
         name=name,
     )(*inputs)
 
@@ -171,7 +171,7 @@
             jax.ShapeDtypeStruct((2, 8, ROWS), F32),
         ),
         [keys, keys, pltpu.VMEM((2, ROWS, HEAD_SIZE), BF16), rows, rows, rows],
-        10_000_000_000,
+        1_000_000,
         "forward",
     )
 
@@ -262,7 +262,7 @@
         (ids, span_map, *sides, *kv_pieces),
         (jax.ShapeDtypeStruct((2 * CHIPS, SPAN, 2 * HEAD_SIZE), BF16),),
         [keys, keys, rows, rows, stats, stats, sums, sums, table, table, table, table],
-        12_000_000_000,
+        1_000_000,
         "backward",
     )
     return part
@@ -277,29 +277,24 @@
     return ref[:, pl.ds(pl.multiple_of(b * FEATURES, FEATURES), FEATURES)]
 
 
-def out_kernel(columns, ids, owners, attn_ref, grad_ref, own_ref, other_ref, found):
+def out_kernel(ids, owners, attn_ref, grad_ref, own_ref, other_ref, found):
     core = ids[0] % 2
     blocks_by_owner(owners, 2, found)
-    attn_t = attn_ref[:, columns].astype(F32).T.astype(BF16)
+    attn_t = attn_ref[...].astype(F32).T.astype(BF16)
     for out_ref, at in ((other_ref, 1 - core), (own_ref, core)):
         for chip in range(CHIPS):
             out_ref[chip] = nn(attn_t, feature_block(grad_ref, found[chip * 2 + at])).astype(BF16)
 
 
-def out_gradient(ids, owner_map, attn, grad, half):
-    part = jax.ShapeDtypeStruct((CHIPS, FEATURES, FEATURES), BF16)
-    columns = slice(half * FEATURES, (half + 1) * FEATURES)
-
-    def kernel(*refs):
-        out_kernel(columns, *refs)
-
+def out_gradient(ids, owner_map, attn, grad):
+    part = jax.ShapeDtypeStruct((CHIPS, HEAD_COLUMNS, FEATURES), BF16)
     return call(
-        kernel,
+        out_kernel,
         (ids, owner_map, attn, grad),
         (part, part),
         [pltpu.SMEM((N_CTX,), jnp.int32)],
-        800_000_000,
-        f"out_gradient_{half}",
+        3_200_000_000,
+        "out_gradient",
     )
 
 
@@ -330,7 +325,7 @@
         (ids, owner_map, parts, hidden),
         (part, part),
         [found, found],
-        1_600_000_000,
+        1_000_000,
         "kv_gradient",
     )
 
@@ -353,23 +348,21 @@
 def per_device(hidden_in, query, key, value, out_weight, grad_out, span_map, owner_map):
     ids = jnp.stack([lax.axis_index("ctx"), lax.axis_index("head")]).astype(jnp.int32)
     grad = lax.all_gather(grad_out, "head", axis=1, tiled=True)
-    hidden = lax.all_gather(after(hidden_in, grad), "head", axis=1, tiled=True)
     kv_pieces = gather_over_ctx(jnp.concatenate([key, value], axis=1))
     query_other = swap(query)
-    attn, lse = forward(ids, span_map, query, kv_pieces)
-    d_attn = nt(grad, out_weight).astype(BF16)
-    out_first = exchange(chip_sum(*out_gradient(ids, owner_map, attn, grad, 0)))
+    attn, lse = forward(ids, span_map, after(query, query_other), kv_pieces)
+    hidden = lax.all_gather(after(hidden_in, attn), "head", axis=1, tiled=True)
+    d_attn = nt(after(grad, attn), out_weight).astype(BF16)
     sides = (query, query_other, d_attn, swap(d_attn), attn, swap(attn), lse, swap(lse))
     dkv = backward(ids, span_map, sides, kv_pieces[:8])
     attn_late = after(attn, dkv)
     dkv = exchange(dkv).reshape(CHIPS, TOKENS, 2 * HEAD_SIZE)
-    out_second = chip_sum(*out_gradient(ids, owner_map, attn_late, grad, 1))
-    out_second = exchange(after(out_second, dkv))
-    kv_total = exchange(chip_sum(*kv_gradient(ids, owner_map, dkv, hidden)))
+    out_parts = chip_sum(*out_gradient(ids, owner_map, attn_late, grad))
+    out_parts = exchange(after(out_parts, dkv))
+    kv_total = chip_sum(*kv_gradient(ids, owner_map, dkv, hidden))
+    kv_total = exchange(after(kv_total, out_parts))
     kv_total = jnp.sum(kv_total.astype(F32), axis=0)
-    out_total = jnp.concatenate(
-        [jnp.sum(part.astype(F32), axis=0) for part in (out_first, out_second)], axis=0
-    )
+    out_total = jnp.sum(out_parts.astype(F32), axis=0)
     return kv_total[:HEAD_SIZE].T, kv_total[HEAD_SIZE:].T, out_total
 
 

time: 219 us -> 181 us (0.83)
  waiting for transfers between devices: 100 us -> 65.2 us
  starting transfers between devices: 35.2 us -> 31.5 us
  Pallas kernels: 50.3 us -> 47.2 us
  local copies, waits for them, and re-layouts: 6.27 us -> 8.94 us
    all_gather x1, waiting for transfers between devices: 43.3 us -> 0.01 us  [per_device(): grad = lax.all_gather(grad_out, 'head', axis=1, tiled=True)]
    ppermute x22 -> x21, waiting for transfers between devices: 9.86 us -> 17.2 us  [ctx_move(): return lax.ppermute(value, 'ctx', pairs)]
    all_to_all x4 -> x3, starting transfers between devices: 19.8 us -> 16 us  [exchange(): lax.all_to_all(parts, 'ctx', 0, 0, tiled=True, axis_index_groups=SAME_CORE)]
    pallas_call x5 -> x4, Pallas kernels: 50.3 us -> 47.2 us  [call(): pl.pallas_call(kernel, out_shape=outputs, in_specs=[smem(), smem()] + [vm...]
    unnamed x38 -> x50, local copies, waits for them, and re-layouts: 5.33 us -> 8.01 us
    all_to_all x4 -> x3, waiting for transfers between devices: 46.6 us -> 47.4 us  [exchange(): lax.all_to_all(parts, 'ctx', 0, 0, tiled=True, axis_index_groups=SAME_CORE)]
    convert_element_type x3 -> x2, other arithmetic: 6.32 us -> 6.58 us  [chip_sum(): return (own.astype(F32) + swap(other).astype(F32)).astype(BF16)]
    ppermute x22 -> x21, starting transfers between devices: 15.4 us -> 15.5 us  [ctx_move(): return lax.ppermute(value, 'ctx', pairs)]
  transfers between devices with their start and end apart: 28 -> 26, of which waited for: 11 -> 10; matrix products, arithmetic and copies ran while one was open for 7% -> 9% of each run, Pallas kernels for 23% -> 26%
where the time goes in v3:
time: 181 us
  waiting for transfers between devices  65.2 us (36%)
  Pallas kernels  47.2 us (26%)
  starting transfers between devices  31.5 us (17%)
  between operations  14.3 us (8%)
  local copies, waits for them, and re-layouts  8.94 us (5%)
  other arithmetic  8.38 us (5%)
  matrix products  4.96 us (3%)
    all_to_all x3, waiting for transfers between devices, exchange(): lax.all_to_all(parts, 'ctx', 0, 0, tiled=True, axis_index_groups=SAME_CORE)  47.4 us
    pallas_call x4, Pallas kernels, call(): pl.pallas_call(kernel, out_shape=outputs, in_specs=[smem(), smem()] + [vm...  47.2 us
    ppermute x21, waiting for transfers between devices, ctx_move(): return lax.ppermute(value, 'ctx', pairs)  17.2 us
    all_to_all x3, starting transfers between devices, exchange(): lax.all_to_all(parts, 'ctx', 0, 0, tiled=True, axis_index_groups=SAME_CORE)  16 us
    ppermute x21, starting transfers between devices, ctx_move(): return lax.ppermute(value, 'ctx', pairs)  15.5 us
    unnamed x50, local copies, waits for them, and re-layouts  8.01 us
    convert_element_type x2, other arithmetic, chip_sum(): return (own.astype(F32) + swap(other).astype(F32)).astype(BF16)  6.58 us
    dot_general x1, matrix products, nt(): lax.dot_general(a, b, (((1,), (1,)), ((), ())), preferred_element_type=F32)  4.96 us
  transfers between devices with their start and end apart: 26, of which 10 were waited for; matrix products, arithmetic and copies ran while one was open for 9% of the time, Pallas kernels for 26%

profile of v3, /device:TPU:0, one launch (start us, length us, event | category | flops | bytes accessed | tf_op | source)
XLA Modules:
  0.0 180.5 jit_solution(9177758638395183635)
XLA Ops:
  7.2 0.0 all-gather.3.cloned.1.call-start
  7.2 0.7 all-gather.3.cloned.1.call-update
  7.9 0.0 all-gather.5.cloned.1.call-start
  7.9 0.9 constant_dynamic-update-slice_fusion.1
  8.9 0.9 constant_dynamic-update-slice_fusion.rest_0_.rest_8_
  9.8 3.2 %collective-permute-start.1 = (bf16[384,256]{1,0:T(8,128)(2,1)S(1)}, bf16[384,256]{1,0:T(8,128)(2,1)S(1)}, u32[]{:S(2)}, u32[]{:S(2)}) collective-permute-start(bf16[384,256]{1,0:T(8,128)(2,1)S(1)} %constant_dynamic-update-slice_fusion.rest_0_.rest_8_), channel_id=1, source_target_pairs={{0,64},{8,72},{16,80},{24,88},{32,96},{40,104},{48,112},{56,120},{... | collective-permute-start | bytes 589832 | tf_op jit(solution)/shard_map/ppermute | solution.py:33
  13.0 1.9 %collective-permute-start.2 = (bf16[384,256]{1,0:T(8,128)(2,1)S(1)}, bf16[384,256]{1,0:T(8,128)(2,1)S(1)}, u32[]{:S(2)}, u32[]{:S(2)}) collective-permute-start(bf16[384,256]{1,0:T(8,128)(2,1)S(1)} %constant_dynamic-update-slice_fusion.rest_0_.rest_8_), channel_id=1, source_target_pairs={{0,16},{8,24},{16,32},{24,40},{32,48},{40,56},{48,0},{56,8},{64,80... | collective-permute-start | bytes 589832 | tf_op jit(solution)/shard_map/ppermute | solution.py:33
  14.9 2.1 %collective-permute-start.3 = (bf16[384,256]{1,0:T(8,128)(2,1)S(1)}, bf16[384,256]{1,0:T(8,128)(2,1)S(1)}, u32[]{:S(2)}, u32[]{:S(2)}) collective-permute-start(bf16[384,256]{1,0:T(8,128)(2,1)S(1)} %constant_dynamic-update-slice_fusion.rest_0_.rest_8_), channel_id=1, source_target_pairs={{0,48},{8,56},{16,0},{24,8},{32,16},{40,24},{48,32},{56,40},{64,11... | collective-permute-start | bytes 589832 | tf_op jit(solution)/shard_map/ppermute | solution.py:33
  17.0 0.0 collective-permute-start.8
  17.0 0.9 collective-permute-done.1.rest_1_.rest_9_
  17.9 4.3 %collective-permute-start.5 = (bf16[384,256]{1,0:T(8,128)(2,1)S(1)}, bf16[384,256]{1,0:T(8,128)(2,1)S(1)}, u32[]{:S(2)}, u32[]{:S(2)}) collective-permute-start(bf16[384,256]{1,0:T(8,128)(2,1)S(1)} %collective-permute-done.1.rest_1_.rest_9_), channel_id=1, source_target_pairs={{0,48},{8,56},{16,0},{24,8},{32,16},{40,24},{48,32},{56,40},{64,11... | collective-permute-start | bytes 589832 | tf_op jit(solution)/shard_map/ppermute | solution.py:33
  22.1 0.1 collective-permute-start.4
  22.2 0.0 collective-permute-done.3.rest_3_.rest_11_
  22.3 1.7 collective-permute-start.6
  24.0 1.4 collective-permute-done.5.rest_5_.rest_13_
  25.4 0.0 collective-permute-start.10
  25.4 5.7 %collective-permute-done.4.rest_4_.rest_12_ = bf16[384,256]{1,0:T(8,128)(2,1)S(1)} collective-permute-done((bf16[384,256]{1,0:T(8,128)(2,1)S(1)}, bf16[384,256]{1,0:T(8,128)(2,1)S(1)}, u32[]{:S(2)}, u32[]{:S(2)}) %collective-permute-start.4) | collective-permute-done | bytes 196640 | tf_op jit(solution)/shard_map/ppermute | solution.py:33
  31.1 0.1 collective-permute-start.7
  31.2 3.7 %collective-permute-done.6.rest_6_.rest_14_ = bf16[384,256]{1,0:T(8,128)(2,1)S(1)} collective-permute-done((bf16[384,256]{1,0:T(8,128)(2,1)S(1)}, bf16[384,256]{1,0:T(8,128)(2,1)S(1)}, u32[]{:S(2)}, u32[]{:S(2)}) %collective-permute-start.6) | collective-permute-done | bytes 196640 | tf_op jit(solution)/shard_map/ppermute | solution.py:33
  34.9 0.0 collective-permute-start.11
  34.9 0.0 collective-permute-done.9.rest_9_
  34.9 0.5 collective-permute-start.13
  35.4 0.1 collective-permute-start.12
  35.5 0.0 collective-permute-done.rest_1_
  35.5 0.4 collective-permute-start.14
  35.9 1.3 collective-permute-done.7.rest_7_.rest_15_
  37.2 0.0 collective-permute-start.15
  37.2 1.4 copy.14.spans
  38.6 0.6 pad_add_fusion.ids
  39.2 0.0 collective-permute-done.11.rest_11_
  39.4 0.5 copy-done.16
  39.9 0.1 copy-done.17
  39.9 0.1 copy-done.18
  40.0 0.1 copy-done.19
  40.1 0.7 copy-done.20
  40.8 15.0 %forward.1 = (bf16[384,512]{1,0:T(8,128)(2,1)}, f32[2,8,768]{2,1,0:T(8,128)}) custom-call(s32[2]{0:T(128)} %pad_add_fusion.ids, s32[16,2]{1,0:T(8,128)} %copy.14.spans, bf16[384,512]{1,0:T(8,128)(2,1)} %rest_0_.1, bf16[384,256]{1,0:T(8,128)(2,1)} %copy-done.1, bf16[384,256]{1,0:T(8,128)(2,1)} %copy-done.2, bf16[384,256]{1,0:T(8,128)(2,1)} %copy-done.3, ...), custom_call_target="tpu_custom_call" | custom-call | flops 1000000 | bytes 1024 | tf_op jit(solution)/shard_map/forward/pallas_call | solution.py:151
  55.8 0.0 all-gather.5.cloned.1.call-update
  55.8 0.0 copy-start.21
  55.8 0.5 collective-permute-start.17
  56.4 5.0 %convolution_convert_fusion.rest_2_ = bf16[384,512]{1,0:T(8,128)(2,1)S(1)} fusion(bf16[384,4096]{1,0:T(8,128)(2,1)} %all-gather.3.cloned.1.call-done.grad_ref, bf16[512,4096]{1,0:T(8,128)(2,1)} %param.12), kind=kOutput, calls=%fused_computation.4 | convolution fusion | flops 1610809344 | bytes 7733248 | tf_op jit(solution)/shard_map/dot_general | solution.py:62
  61.3 0.1 collective-permute-start.16
  61.5 0.4 collective-permute-start.18
  61.9 1.3 collective-permute-done.18.rest_7_
  63.2 0.6 copy-done.22
  63.8 0.2 copy-done.10
  64.0 0.8 copy-done.12
  64.8 20.5 %backward.1 = bf16[16,192,256]{2,1,0:T(8,128)(2,1)} custom-call(s32[2]{0:T(128)} %pad_add_fusion.ids, s32[16,2]{1,0:T(8,128)} %copy.14.spans, bf16[384,512]{1,0:T(8,128)(2,1)} %rest_0_.1, bf16[384,512]{1,0:T(8,128)(2,1)} %copy-done.9, bf16[384,512]{1,0:T(8,128)(2,1)} %copy-done.11, bf16[384,512]{1,0:T(8,128)(2,1)} %copy-done.12, ...), custom_call_target="tpu_custom_call" | custom-call | flops 1000000 | bytes 1024 | tf_op jit(solution)/shard_map/backward/pallas_call | solution.py:151
  85.2 5.9 %out_gradient.1 = (bf16[8,512,256]{2,1,0:T(8,128)(2,1)}, bf16[8,512,256]{2,1,0:T(8,128)(2,1)}) custom-call(s32[2]{0:T(128)} %pad_add_fusion.ids, s32[3,16]{1,0:T(4,128)} %owners.3, bf16[384,512]{1,0:T(8,128)(2,1)} %get-tuple-element.22.rest_4_.attn_ref, bf16[384,4096]{1,0:T(8,128)(2,1)} %all-gather.3.cloned.1.call-done.grad_ref), custom_call_target="tpu_custom_call" | custom-call | flops 3200000000 | bytes 1024 | tf_op jit(solution)/shard_map/out_gradient/pallas_call | solution.py:151
  91.1 6.4 %all-to-all-start = ((bf16[16,192,256]{2,1,0:T(8,128)(2,1)}), bf16[16,192,256]{2,1,0:T(8,128)(2,1)S(1)}, u32[]{:S(2)}, u32[]{:S(2)}) async-start(bf16[16,192,256]{2,1,0:T(8,128)(2,1)} %backward.1), calls=%async_computation | async-start | bytes 3145728 | tf_op jit(solution)/shard_map/all_to_all | solution.py:337
  97.5 4.1 %add_convert_fusion = bf16[8,512,256]{2,1,0:T(8,128)(2,1)} fusion(bf16[8,512,256]{2,1,0:T(8,128)(2,1)} %collective-permute-done.20, bf16[8,512,256]{2,1,0:T(8,128)(2,1)} %get-tuple-element.23), kind=kLoop, calls=%fused_computation.1 | loop fusion | flops 4194304 | bytes 6291456 | tf_op jit(solution)/shard_map/convert_element_type | solution.py:341
  101.6 17.4 %all-to-all-done = bf16[16,192,256]{2,1,0:T(8,128)(2,1)S(1)} async-done(((bf16[16,192,256]{2,1,0:T(8,128)(2,1)}), bf16[16,192,256]{2,1,0:T(8,128)(2,1)S(1)}, u32[]{:S(2)}, u32[]{:S(2)}) %all-to-all-start) | async-done | bytes 1572896 | tf_op jit(solution)/shard_map/all_to_all | solution.py:337
  119.0 1.2 copy-done
  120.2 4.8 %all-to-all-start.1 = ((bf16[8,512,256]{2,1,0:T(8,128)(2,1)}), bf16[8,512,256]{2,1,0:T(8,128)(2,1)S(1)}, u32[]{:S(2)}, u32[]{:S(2)}) async-start(bf16[8,512,256]{2,1,0:T(8,128)(2,1)} %add_convert_fusion), calls=%async_computation.1 | async-start | bytes 4194304 | tf_op jit(solution)/shard_map/all_to_all | solution.py:337
  125.0 0.0 all-gather.5.cloned.1.call-done.hidden_ref
  125.0 5.9 %kv_gradient.1 = (bf16[8,256,256]{2,1,0:T(8,128)(2,1)}, bf16[8,256,256]{2,1,0:T(8,128)(2,1)}) custom-call(s32[2]{0:T(128)} %pad_add_fusion.ids, s32[3,16]{1,0:T(4,128)} %owners.3, bf16[8,384,256]{2,1,0:T(8,128)(2,1)} %bitcast.9, bf16[384,4096]{1,0:T(8,128)(2,1)} %all-gather.5.cloned.1.call-done.hidden_ref), custom_call_target="tpu_custom_call" | custom-call | flops 1000000 | bytes 1024 | tf_op jit(solution)/shard_map/kv_gradient/pallas_call | solution.py:151
  130.8 2.9 %collective-permute-done.19 = bf16[8,256,256]{2,1,0:T(8,128)(2,1)S(1)} collective-permute-done((bf16[8,256,256]{2,1,0:T(8,128)(2,1)}, bf16[8,256,256]{2,1,0:T(8,128)(2,1)S(1)}, u32[]{:S(2)}, u32[]{:S(2)}) %collective-permute-start.19) | collective-permute-done | bytes 1048608 | tf_op jit(solution)/shard_map/ppermute | solution.py:33
  133.7 2.5 %add_convert_fusion.1 = bf16[8,256,256]{2,1,0:T(8,128)(2,1)} fusion(bf16[8,256,256]{2,1,0:T(8,128)(2,1)S(1)} %collective-permute-done.19, bf16[8,256,256]{2,1,0:T(8,128)(2,1)} %get-tuple-element.20), kind=kLoop, calls=%fused_computation.3 | loop fusion | flops 2097152 | bytes 3145728 | tf_op jit(solution)/shard_map/convert_element_type | solution.py:341
  136.2 15.2 %all-to-all-done.1 = bf16[8,512,256]{2,1,0:T(8,128)(2,1)S(1)} async-done(((bf16[8,512,256]{2,1,0:T(8,128)(2,1)}), bf16[8,512,256]{2,1,0:T(8,128)(2,1)S(1)}, u32[]{:S(2)}, u32[]{:S(2)}) %all-to-all-start.1) | async-done | bytes 2097184 | tf_op jit(solution)/shard_map/all_to_all | solution.py:337
  151.4 4.8 %all-to-all-start.2 = ((bf16[8,256,256]{2,1,0:T(8,128)(2,1)}), bf16[8,256,256]{2,1,0:T(8,128)(2,1)S(1)}, u32[]{:S(2)}, u32[]{:S(2)}) async-start(bf16[8,256,256]{2,1,0:T(8,128)(2,1)} %add_convert_fusion.1), calls=%async_computation.2 | async-start | bytes 2097152 | tf_op jit(solution)/shard_map/all_to_all | solution.py:337
  156.1 1.1 convert_reduce_fusion
  157.2 14.8 %all-to-all-done.2 = bf16[8,256,256]{2,1,0:T(8,128)(2,1)S(1)} async-done(((bf16[8,256,256]{2,1,0:T(8,128)(2,1)}), bf16[8,256,256]{2,1,0:T(8,128)(2,1)S(1)}, u32[]{:S(2)}, u32[]{:S(2)}) %all-to-all-start.2) | async-done | bytes 1048608 | tf_op jit(solution)/shard_map/all_to_all | solution.py:337
  172.0 0.1 convert_reduce_fusion.1
  172.2 0.8 copy.15
  173.0 0.8 copy.16
  (52 shorter events, 0.1 us)
Async XLA Ops:
  7.2 49.2 %all-gather.3.cloned.1.call-start = ((), (), s32[]{:S(2)}) async-start(), calls=%async_computation.3 | async-start | bytes 3538944 | tf_op jit(solution)/shard_map/all_gather | solution.py:350
  7.9 117.1 %all-gather.5.cloned.1.call-start = ((), (), s32[]{:S(2)}) async-start(), calls=%async_computation.4 | async-start | bytes 3538944 | tf_op jit(solution)/shard_map/all_gather | solution.py:354
  9.8 29.5 %copy-start.1 = (bf16[384,256]{1,0:T(8,128)(2,1)}, bf16[384,256]{1,0:T(8,128)(2,1)S(1)}, u32[]{:S(2)}) copy-start(bf16[384,256]{1,0:T(8,128)(2,1)S(1)} %constant_dynamic-update-slice_fusion.rest_0_.rest_8_) | copy-start | bytes 589828
  9.8 8.1 %collective-permute-start.1 = (bf16[384,256]{1,0:T(8,128)(2,1)S(1)}, bf16[384,256]{1,0:T(8,128)(2,1)S(1)}, u32[]{:S(2)}, u32[]{:S(2)}) collective-permute-start(bf16[384,256]{1,0:T(8,128)(2,1)S(1)} %constant_dynamic-update-slice_fusion.rest_0_.rest_8_), channel_id=1, source_target_pairs={{0,64},{8,72},{16,80},{24,88},{32,96},{40,104},{48,112},{56,120},{... | collective-permute-start | bytes 589832 | tf_op jit(solution)/shard_map/ppermute | solution.py:33
  13.0 9.2 %collective-permute-start.2 = (bf16[384,256]{1,0:T(8,128)(2,1)S(1)}, bf16[384,256]{1,0:T(8,128)(2,1)S(1)}, u32[]{:S(2)}, u32[]{:S(2)}) collective-permute-start(bf16[384,256]{1,0:T(8,128)(2,1)S(1)} %constant_dynamic-update-slice_fusion.rest_0_.rest_8_), channel_id=1, source_target_pairs={{0,16},{8,24},{16,32},{24,40},{32,48},{40,56},{48,0},{56,8},{64,80... | collective-permute-start | bytes 589832 | tf_op jit(solution)/shard_map/ppermute | solution.py:33
  14.9 7.3 %collective-permute-start.3 = (bf16[384,256]{1,0:T(8,128)(2,1)S(1)}, bf16[384,256]{1,0:T(8,128)(2,1)S(1)}, u32[]{:S(2)}, u32[]{:S(2)}) collective-permute-start(bf16[384,256]{1,0:T(8,128)(2,1)S(1)} %constant_dynamic-update-slice_fusion.rest_0_.rest_8_), channel_id=1, source_target_pairs={{0,48},{8,56},{16,0},{24,8},{32,16},{40,24},{48,32},{56,40},{64,11... | collective-permute-start | bytes 589832 | tf_op jit(solution)/shard_map/ppermute | solution.py:33
  17.0 7.0 %collective-permute-start.8 = (bf16[384,256]{1,0:T(8,128)(2,1)S(1)}, bf16[384,256]{1,0:T(8,128)(2,1)S(1)}, u32[]{:S(2)}, u32[]{:S(2)}) collective-permute-start(bf16[384,256]{1,0:T(8,128)(2,1)S(1)} %constant_dynamic-update-slice_fusion.rest_0_.rest_8_), channel_id=1, source_target_pairs={{0,8},{8,0},{16,24},{24,16},{32,40},{40,32},{48,56},{56,48},{64,72... | collective-permute-start | bytes 589832 | tf_op jit(solution)/shard_map/ppermute | solution.py:33
  17.9 21.4 %copy-start.2 = (bf16[384,256]{1,0:T(8,128)(2,1)}, bf16[384,256]{1,0:T(8,128)(2,1)S(1)}, u32[]{:S(2)}) copy-start(bf16[384,256]{1,0:T(8,128)(2,1)S(1)} %collective-permute-done.1.rest_1_.rest_9_) | copy-start | bytes 589828
  17.9 7.5 %collective-permute-start.5 = (bf16[384,256]{1,0:T(8,128)(2,1)S(1)}, bf16[384,256]{1,0:T(8,128)(2,1)S(1)}, u32[]{:S(2)}, u32[]{:S(2)}) collective-permute-start(bf16[384,256]{1,0:T(8,128)(2,1)S(1)} %collective-permute-done.1.rest_1_.rest_9_), channel_id=1, source_target_pairs={{0,48},{8,56},{16,0},{24,8},{32,16},{40,24},{48,32},{56,40},{64,11... | collective-permute-start | bytes 589832 | tf_op jit(solution)/shard_map/ppermute | solution.py:33
  22.1 13.4 %collective-permute-start = (bf16[384,512]{1,0:T(8,128)(2,1)}, bf16[384,512]{1,0:T(8,128)(2,1)S(1)}, u32[]{:S(2)}, u32[]{:S(2)}) collective-permute-start(bf16[384,512]{1,0:T(8,128)(2,1)} %rest_0_.1), channel_id=1, source_target_pairs={{0,8},{8,0},{16,24},{24,16},{32,40},{40,32},{48,56},{56,48},{64,72... | collective-permute-start | bytes 1179656 | tf_op jit(solution)/shard_map/ppermute | solution.py:33
  22.1 17.1 %copy-start.3 = (bf16[384,256]{1,0:T(8,128)(2,1)}, bf16[384,256]{1,0:T(8,128)(2,1)S(1)}, u32[]{:S(2)}) copy-start(bf16[384,256]{1,0:T(8,128)(2,1)S(1)} %collective-permute-done.2.rest_2_.rest_10_) | copy-start | bytes 589828
  22.1 9.0 %collective-permute-start.4 = (bf16[384,256]{1,0:T(8,128)(2,1)S(1)}, bf16[384,256]{1,0:T(8,128)(2,1)S(1)}, u32[]{:S(2)}, u32[]{:S(2)}) collective-permute-start(bf16[384,256]{1,0:T(8,128)(2,1)S(1)} %collective-permute-done.1.rest_1_.rest_9_), channel_id=1, source_target_pairs={{0,16},{8,24},{16,32},{24,40},{32,48},{40,56},{48,0},{56,8},{64,80... | collective-permute-start | bytes 589832 | tf_op jit(solution)/shard_map/ppermute | solution.py:33
  22.2 17.1 %copy-start.4 = (bf16[384,256]{1,0:T(8,128)(2,1)}, bf16[384,256]{1,0:T(8,128)(2,1)S(1)}, u32[]{:S(2)}) copy-start(bf16[384,256]{1,0:T(8,128)(2,1)S(1)} %collective-permute-done.3.rest_3_.rest_11_) | copy-start | bytes 589828
  22.3 12.6 %collective-permute-start.6 = (bf16[384,256]{1,0:T(8,128)(2,1)S(1)}, bf16[384,256]{1,0:T(8,128)(2,1)S(1)}, u32[]{:S(2)}, u32[]{:S(2)}) collective-permute-start(bf16[384,256]{1,0:T(8,128)(2,1)S(1)} %collective-permute-done.2.rest_2_.rest_10_), channel_id=1, source_target_pairs={{0,16},{8,24},{16,32},{24,40},{32,48},{40,56},{48,0},{56,8},{64,80... | collective-permute-start | bytes 589832 | tf_op jit(solution)/shard_map/ppermute | solution.py:33
  24.0 15.3 %copy-start.13 = (bf16[384,256]{1,0:T(8,128)(2,1)}, bf16[384,256]{1,0:T(8,128)(2,1)S(1)}, u32[]{:S(2)}) copy-start(bf16[384,256]{1,0:T(8,128)(2,1)S(1)} %collective-permute-done.8.rest_8_) | copy-start | bytes 589828
  24.0 10.9 %collective-permute-start.9 = (bf16[384,256]{1,0:T(8,128)(2,1)S(1)}, bf16[384,256]{1,0:T(8,128)(2,1)S(1)}, u32[]{:S(2)}, u32[]{:S(2)}) collective-permute-start(bf16[384,256]{1,0:T(8,128)(2,1)S(1)} %collective-permute-done.1.rest_1_.rest_9_), channel_id=1, source_target_pairs={{0,8},{8,0},{16,24},{24,16},{32,40},{40,32},{48,56},{56,48},{64,72... | collective-permute-start | bytes 589832 | tf_op jit(solution)/shard_map/ppermute | solution.py:33
  25.4 13.9 %copy-start.5 = (bf16[384,256]{1,0:T(8,128)(2,1)}, bf16[384,256]{1,0:T(8,128)(2,1)S(1)}, u32[]{:S(2)}) copy-start(bf16[384,256]{1,0:T(8,128)(2,1)S(1)} %collective-permute-done.5.rest_5_.rest_13_) | copy-start | bytes 589828
  25.4 10.0 %collective-permute-start.10 = (bf16[384,256]{1,0:T(8,128)(2,1)S(1)}, bf16[384,256]{1,0:T(8,128)(2,1)S(1)}, u32[]{:S(2)}, u32[]{:S(2)}) collective-permute-start(bf16[384,256]{1,0:T(8,128)(2,1)S(1)} %collective-permute-done.2.rest_2_.rest_10_), channel_id=1, source_target_pairs={{0,8},{8,0},{16,24},{24,16},{32,40},{40,32},{48,56},{56,48},{64,72... | collective-permute-start | bytes 589832 | tf_op jit(solution)/shard_map/ppermute | solution.py:33
  31.1 8.2 %copy-start.6 = (bf16[384,256]{1,0:T(8,128)(2,1)}, bf16[384,256]{1,0:T(8,128)(2,1)S(1)}, u32[]{:S(2)}) copy-start(bf16[384,256]{1,0:T(8,128)(2,1)S(1)} %collective-permute-done.4.rest_4_.rest_12_) | copy-start | bytes 589828
  31.1 6.1 %collective-permute-start.7 = (bf16[384,256]{1,0:T(8,128)(2,1)S(1)}, bf16[384,256]{1,0:T(8,128)(2,1)S(1)}, u32[]{:S(2)}, u32[]{:S(2)}) collective-permute-start(bf16[384,256]{1,0:T(8,128)(2,1)S(1)} %collective-permute-done.5.rest_5_.rest_13_), channel_id=1, source_target_pairs={{0,48},{8,56},{16,0},{24,8},{32,16},{40,24},{48,32},{56,40},{64,11... | collective-permute-start | bytes 589832 | tf_op jit(solution)/shard_map/ppermute | solution.py:33
  34.9 4.5 %copy-start.7 = (bf16[384,256]{1,0:T(8,128)(2,1)}, bf16[384,256]{1,0:T(8,128)(2,1)S(1)}, u32[]{:S(2)}) copy-start(bf16[384,256]{1,0:T(8,128)(2,1)S(1)} %collective-permute-done.6.rest_6_.rest_14_) | copy-start | bytes 589828
  34.9 4.3 %collective-permute-start.11 = (bf16[384,256]{1,0:T(8,128)(2,1)S(1)}, bf16[384,256]{1,0:T(8,128)(2,1)S(1)}, u32[]{:S(2)}, u32[]{:S(2)}) collective-permute-start(bf16[384,256]{1,0:T(8,128)(2,1)S(1)} %collective-permute-done.3.rest_3_.rest_11_), channel_id=1, source_target_pairs={{0,8},{8,0},{16,24},{24,16},{32,40},{40,32},{48,56},{56,48},{64,72... | collective-permute-start | bytes 589832 | tf_op jit(solution)/shard_map/ppermute | solution.py:33
  34.9 4.5 %copy-start.14 = (bf16[384,256]{1,0:T(8,128)(2,1)}, bf16[384,256]{1,0:T(8,128)(2,1)S(1)}, u32[]{:S(2)}) copy-start(bf16[384,256]{1,0:T(8,128)(2,1)S(1)} %collective-permute-done.9.rest_9_) | copy-start | bytes 589828
  34.9 4.3 %collective-permute-start.13 = (bf16[384,256]{1,0:T(8,128)(2,1)S(1)}, bf16[384,256]{1,0:T(8,128)(2,1)S(1)}, u32[]{:S(2)}, u32[]{:S(2)}) collective-permute-start(bf16[384,256]{1,0:T(8,128)(2,1)S(1)} %collective-permute-done.5.rest_5_.rest_13_), channel_id=1, source_target_pairs={{0,8},{8,0},{16,24},{24,16},{32,40},{40,32},{48,56},{56,48},{64,72... | collective-permute-start | bytes 589832 | tf_op jit(solution)/shard_map/ppermute | solution.py:33
  35.4 4.0 %copy-start.15 = (bf16[384,256]{1,0:T(8,128)(2,1)}, bf16[384,256]{1,0:T(8,128)(2,1)S(1)}, u32[]{:S(2)}) copy-start(bf16[384,256]{1,0:T(8,128)(2,1)S(1)} %collective-permute-done.10.rest_10_) | copy-start | bytes 589828
  35.4 3.8 %collective-permute-start.12 = (bf16[384,256]{1,0:T(8,128)(2,1)S(1)}, bf16[384,256]{1,0:T(8,128)(2,1)S(1)}, u32[]{:S(2)}, u32[]{:S(2)}) collective-permute-start(bf16[384,256]{1,0:T(8,128)(2,1)S(1)} %collective-permute-done.4.rest_4_.rest_12_), channel_id=1, source_target_pairs={{0,8},{8,0},{16,24},{24,16},{32,40},{40,32},{48,56},{56,48},{64,72... | collective-permute-start | bytes 589832 | tf_op jit(solution)/shard_map/ppermute | solution.py:33
  35.5 25.8 %copy-start.9 = (bf16[384,512]{1,0:T(8,128)(2,1)}, bf16[384,512]{1,0:T(8,128)(2,1)S(1)}, u32[]{:S(2)}) copy-start(bf16[384,512]{1,0:T(8,128)(2,1)S(1)} %collective-permute-done.rest_1_) | copy-start | bytes 1179652
  35.5 3.7 %collective-permute-start.14 = (bf16[384,256]{1,0:T(8,128)(2,1)S(1)}, bf16[384,256]{1,0:T(8,128)(2,1)S(1)}, u32[]{:S(2)}, u32[]{:S(2)}) collective-permute-start(bf16[384,256]{1,0:T(8,128)(2,1)S(1)} %collective-permute-done.6.rest_6_.rest_14_), channel_id=1, source_target_pairs={{0,8},{8,0},{16,24},{24,16},{32,40},{40,32},{48,56},{56,48},{64,72... | collective-permute-start | bytes 589832 | tf_op jit(solution)/shard_map/ppermute | solution.py:33
  37.2 2.1 %copy-start.8 = (bf16[384,256]{1,0:T(8,128)(2,1)}, bf16[384,256]{1,0:T(8,128)(2,1)S(1)}, u32[]{:S(2)}) copy-start(bf16[384,256]{1,0:T(8,128)(2,1)S(1)} %collective-permute-done.7.rest_7_.rest_15_) | copy-start | bytes 589828
  37.2 2.0 %collective-permute-start.15 = (bf16[384,256]{1,0:T(8,128)(2,1)S(1)}, bf16[384,256]{1,0:T(8,128)(2,1)S(1)}, u32[]{:S(2)}, u32[]{:S(2)}) collective-permute-start(bf16[384,256]{1,0:T(8,128)(2,1)S(1)} %collective-permute-done.7.rest_7_.rest_15_), channel_id=1, source_target_pairs={{0,8},{8,0},{16,24},{24,16},{32,40},{40,32},{48,56},{56,48},{64,72... | collective-permute-start | bytes 589832 | tf_op jit(solution)/shard_map/ppermute | solution.py:33
  39.2 0.7 copy-start.16
  39.2 0.7 copy-start.17
  39.2 0.8 copy-start.18
  39.2 0.8 copy-start.19
  40.1 0.7 copy-start.20
  55.8 5.7 %copy-start.21 = (f32[2,8,768]{2,1,0:T(8,128)S(1)}, f32[2,8,768]{2,1,0:T(8,128)}, u32[]{:S(2)}) copy-start(f32[2,8,768]{2,1,0:T(8,128)} %get-tuple-element.18.rest_6_) | copy-start | bytes 147460
  55.8 7.4 %collective-permute-start.17 = (bf16[384,512]{1,0:T(8,128)(2,1)}, bf16[384,512]{1,0:T(8,128)(2,1)S(1)}, u32[]{:S(2)}, u32[]{:S(2)}) collective-permute-start(bf16[384,512]{1,0:T(8,128)(2,1)} %get-tuple-element.22.rest_4_.attn_ref), channel_id=1, source_target_pairs={{0,8},{8,0},{16,24},{24,16},{32,40},{40,32},{48,56},{56,48},{64,72... | collective-permute-start | bytes 1179656 | tf_op jit(solution)/shard_map/ppermute | solution.py:33
  61.3 1.9 %copy-start.11 = (bf16[384,512]{1,0:T(8,128)(2,1)}, bf16[384,512]{1,0:T(8,128)(2,1)S(1)}, u32[]{:S(2)}) copy-start(bf16[384,512]{1,0:T(8,128)(2,1)S(1)} %convolution_convert_fusion.rest_2_) | copy-start | bytes 1179652
  61.3 1.9 %collective-permute-start.16 = (bf16[384,512]{1,0:T(8,128)(2,1)S(1)}, bf16[384,512]{1,0:T(8,128)(2,1)S(1)}, u32[]{:S(2)}, u32[]{:S(2)}) collective-permute-start(bf16[384,512]{1,0:T(8,128)(2,1)S(1)} %convolution_convert_fusion.rest_2_), channel_id=1, source_target_pairs={{0,8},{8,0},{16,24},{24,16},{32,40},{40,32},{48,56},{56,48},{64,72... | collective-permute-start | bytes 1179656 | tf_op jit(solution)/shard_map/ppermute | solution.py:33
  61.5 1.7 collective-permute-start.18
  63.2 0.6 copy-start.22
  63.2 0.8 copy-start.10
  64.0 0.8 copy-start.12
  91.1 6.4 %collective-permute-start.20 = (bf16[8,512,256]{2,1,0:T(8,128)(2,1)}, bf16[8,512,256]{2,1,0:T(8,128)(2,1)}, u32[]{:S(2)}, u32[]{:S(2)}) collective-permute-start(bf16[8,512,256]{2,1,0:T(8,128)(2,1)} %get-tuple-element.24), channel_id=1, source_target_pairs={{0,8},{8,0},{16,24},{24,16},{32,40},{40,32},{48,56},{56,48},{64,72... | collective-permute-start | bytes 6291464 | tf_op jit(solution)/shard_map/ppermute | solution.py:33
  91.1 27.9 %all-to-all-start = ((bf16[16,192,256]{2,1,0:T(8,128)(2,1)}), bf16[16,192,256]{2,1,0:T(8,128)(2,1)S(1)}, u32[]{:S(2)}, u32[]{:S(2)}) async-start(bf16[16,192,256]{2,1,0:T(8,128)(2,1)} %backward.1), calls=%async_computation | async-start | bytes 3145728 | tf_op jit(solution)/shard_map/all_to_all | solution.py:337
  119.0 1.2 copy-start
  120.2 31.2 %all-to-all-start.1 = ((bf16[8,512,256]{2,1,0:T(8,128)(2,1)}), bf16[8,512,256]{2,1,0:T(8,128)(2,1)S(1)}, u32[]{:S(2)}, u32[]{:S(2)}) async-start(bf16[8,512,256]{2,1,0:T(8,128)(2,1)} %add_convert_fusion), calls=%async_computation.1 | async-start | bytes 4194304 | tf_op jit(solution)/shard_map/all_to_all | solution.py:337
  130.8 2.9 %collective-permute-start.19 = (bf16[8,256,256]{2,1,0:T(8,128)(2,1)}, bf16[8,256,256]{2,1,0:T(8,128)(2,1)S(1)}, u32[]{:S(2)}, u32[]{:S(2)}) collective-permute-start(bf16[8,256,256]{2,1,0:T(8,128)(2,1)} %get-tuple-element.21), channel_id=1, source_target_pairs={{0,8},{8,0},{16,24},{24,16},{32,40},{40,32},{48,56},{56,48},{64,72... | collective-permute-start | bytes 3145736 | tf_op jit(solution)/shard_map/ppermute | solution.py:33
  151.4 20.6 %all-to-all-start.2 = ((bf16[8,256,256]{2,1,0:T(8,128)(2,1)}), bf16[8,256,256]{2,1,0:T(8,128)(2,1)S(1)}, u32[]{:S(2)}, u32[]{:S(2)}) async-start(bf16[8,256,256]{2,1,0:T(8,128)(2,1)} %add_convert_fusion.1), calls=%async_computation.2 | async-start | bytes 2097152 | tf_op jit(solution)/shard_map/all_to_all | solution.py:337
Sparse Core Ops, SparseCore 0:
  9.6 46.6 all-gather.2
  57.9 44.9 all-gather.4

commit v4 on v3

--- a/solution.py
+++ b/solution.py
@@ -14,7 +14,9 @@
 TOKENS = 384
 KEY_BLOCK = 384
 KEY_BLOCKS = 16
+OUT_FLOPS = 8_000_000_000
 OWN_BLOCKS = 8
+WIDE = 3
 ROWS = GROUP * SPAN
 FEATURES = 256
 HEAD_COLUMNS = 512
@@ -213,49 +215,53 @@
             lse[side * 2 + half] = lse_ref[half, :1]
             delta[side * 2 + half] = jnp.sum(heads_down(product, half).T, axis=0, keepdims=True)
 
-    def tile(b, group, span, masked):
-        s = nt(ks[key_rows(b), :], qs[group])
+    acc_k[...] = jnp.zeros(acc_k.shape, F32)
+    acc_v[...] = jnp.zeros(acc_v.shape, F32)
+
+    def tile(first, count, group, span, masked):
+        rows = pl.ds(pl.multiple_of(first, KEY_BLOCK), count)
+        s = nt(ks[rows, :], qs[group])
         if masked:
-            row = lax.broadcasted_iota(jnp.int32, (KEY_BLOCK, 1), 0)
+            b = first // KEY_BLOCK
+            row = lax.broadcasted_iota(jnp.int32, (count, 1), 0)
             at = jnp.where(row < SPAN, order[b * 2] * SPAN, (order[b * 2 + 1] - 1) * SPAN) + row
             s = jnp.where(at > span * SPAN + row_in_span((1, ROWS), 1), -1e30, s)
         p = jnp.exp2(s * EXP2_SCALE - lse[group])
-        d_p = nt(vs[key_rows(b), :], dos[group])
+        d_p = nt(vs[rows, :], dos[group])
         d_s = (p * (d_p - delta[group])).astype(BF16)
-        acc_k[...] += nn(d_s, qs[group])
-        acc_v[...] += nn(p.astype(BF16), dos[group])
-
-    @pl.loop(0, OWN_BLOCKS)
-    def _(b):
-        acc_k[...] = jnp.zeros(acc_k.shape, F32)
-        acc_v[...] = jnp.zeros(acc_v.shape, F32)
-
-        @pl.loop(0, 4)
-        def _(group):
-            span = spans[ids[0] ^ (group // 2), group % 2]
-            last = (seen[span] + 1) // 2 - 1
-
-            @pl.when(b < last)
-            def _():
-                tile(b, group, span, False)
-
-            @pl.when(b == last)
-            def _():
-                tile(b, group, span, True)
-
-        d_key = (acc_k[...] * SCALE).astype(BF16)
-        d_value = acc_v[...].astype(BF16)
-        for n in range(2):
-            at = slot[order[b * 2 + n]] - 1
-            part_ref[at, :, :HEAD_SIZE] = d_key[n * SPAN : (n + 1) * SPAN]
-            part_ref[at, :, HEAD_SIZE:] = d_value[n * SPAN : (n + 1) * SPAN]
+        acc_k[rows, :] += nn(d_s, qs[group])
+        acc_v[rows, :] += nn(p.astype(BF16), dos[group])
+
+    @pl.loop(0, 4)
+    def _(group):
+        span = spans[ids[0] ^ (group // 2), group % 2]
+        last = (seen[span] + 1) // 2 - 1
+        wide = jnp.maximum(last, 0) // WIDE
+
+        @pl.loop(0, wide)
+        def _(n):
+            tile(n * WIDE * KEY_BLOCK, WIDE * KEY_BLOCK, group, span, False)
+
+        @pl.loop(wide * WIDE, last)
+        def _(b):
+            tile(b * KEY_BLOCK, KEY_BLOCK, group, span, False)
+
+        @pl.when(last >= 0)
+        def _():
+            tile(last * KEY_BLOCK, KEY_BLOCK, group, span, True)
+
+    for n in range(2 * CHIPS):
+        at = slot[order[n]] - 1
+        rows = pl.ds(n * SPAN, SPAN)
+        part_ref[at, :, :HEAD_SIZE] = (acc_k[rows, :] * SCALE).astype(BF16)
+        part_ref[at, :, HEAD_SIZE:] = acc_v[rows, :].astype(BF16)
 
 
 def backward(ids, span_map, sides, kv_pieces):
     keys = pltpu.VMEM((OWN_BLOCKS * KEY_BLOCK, HEAD_SIZE), BF16)
     rows = pltpu.VMEM((4, ROWS, HEAD_SIZE), BF16)
     stats = pltpu.VMEM((4, 1, ROWS), F32)
-    sums = pltpu.VMEM((KEY_BLOCK, HEAD_SIZE), F32)
+    sums = pltpu.VMEM((OWN_BLOCKS * KEY_BLOCK, HEAD_SIZE), F32)
     table = pltpu.SMEM((SLOTS,), jnp.int32)
     (part,) = call(
         backward_kernel,
@@ -277,25 +283,29 @@
     return ref[:, pl.ds(pl.multiple_of(b * FEATURES, FEATURES), FEATURES)]
 
 
-def out_kernel(ids, owners, attn_ref, grad_ref, own_ref, other_ref, found):
+def out_kernel(ids, owners, attn_own, attn_other, grad_own, grad_other, out_ref, found):
     core = ids[0] % 2
     blocks_by_owner(owners, 2, found)
-    attn_t = attn_ref[...].astype(F32).T.astype(BF16)
-    for out_ref, at in ((other_ref, 1 - core), (own_ref, core)):
-        for chip in range(CHIPS):
-            out_ref[chip] = nn(attn_t, feature_block(grad_ref, found[chip * 2 + at])).astype(BF16)
-
-
-def out_gradient(ids, owner_map, attn, grad):
+    attn_t = [ref[...].astype(F32).T.astype(BF16) for ref in (attn_own, attn_other)]
+    for chip in range(CHIPS):
+        b = found[chip * 2 + core]
+        block = nn(attn_t[0], feature_block(grad_own, b)) + nn(
+            attn_t[1], feature_block(grad_other, b)
+        )
+        out_ref[chip] = block.astype(BF16)
+
+
+def out_gradient(ids, owner_map, attn, attn_other, grad, grad_other):
     part = jax.ShapeDtypeStruct((CHIPS, HEAD_COLUMNS, FEATURES), BF16)
-    return call(
+    (parts,) = call(
         out_kernel,
-        (ids, owner_map, attn, grad),
-        (part, part),
+        (ids, owner_map, attn, attn_other, grad, grad_other),
+        (part,),
         [pltpu.SMEM((N_CTX,), jnp.int32)],
-        3_200_000_000,
+        OUT_FLOPS,
         "out_gradient",
     )
+    return parts
 
 
 def kv_kernel(ids, owners, parts_ref, hidden_ref, own_ref, other_ref, found_k, found_v):
@@ -353,11 +363,12 @@
     attn, lse = forward(ids, span_map, after(query, query_other), kv_pieces)
     hidden = lax.all_gather(after(hidden_in, attn), "head", axis=1, tiled=True)
     d_attn = nt(after(grad, attn), out_weight).astype(BF16)
-    sides = (query, query_other, d_attn, swap(d_attn), attn, swap(attn), lse, swap(lse))
+    attn_other = swap(attn)
+    sides = (query, query_other, d_attn, swap(d_attn), attn, attn_other, lse, swap(lse))
     dkv = backward(ids, span_map, sides, kv_pieces[:8])
     attn_late = after(attn, dkv)
     dkv = exchange(dkv).reshape(CHIPS, TOKENS, 2 * HEAD_SIZE)
-    out_parts = chip_sum(*out_gradient(ids, owner_map, attn_late, grad))
+    out_parts = out_gradient(ids, owner_map, attn_late, attn_other, grad, swap(grad))
     out_parts = exchange(after(out_parts, dkv))
     kv_total = chip_sum(*kv_gradient(ids, owner_map, dkv, hidden))
     kv_total = exchange(after(kv_total, out_parts))

time: 181 us -> 180 us (level)
  waiting for transfers between devices: 65.2 us -> 70.1 us
  other arithmetic: 8.38 us -> 4.35 us
  Pallas kernels: 47.2 us -> 45.3 us
    all_to_all x3, waiting for transfers between devices: 47.4 us -> 51.7 us  [exchange(): lax.all_to_all(parts, 'ctx', 0, 0, tiled=True, axis_index_groups=SAME_CORE)]
    convert_element_type x2 -> x1, other arithmetic: 6.58 us -> 2.51 us  [chip_sum(): return (own.astype(F32) + swap(other).astype(F32)).astype(BF16)]
    pallas_call x4, Pallas kernels: 47.2 us -> 45.3 us  [call(): pl.pallas_call(kernel, out_shape=outputs, in_specs=[smem(), smem()] + [vm...]
  transfers between devices with their start and end apart: 26 -> 26, of which waited for: 10 -> 11; matrix products, arithmetic and copies ran while one was open for 9% -> 7% of each run, Pallas kernels for 26% -> 25%
where the time goes in v4:
time: 180 us; the launch traced here: 179 us
  waiting for transfers between devices  70.1 us (39%)
  Pallas kernels  45.3 us (25%)
  starting transfers between devices  31.5 us (18%)
  between operations  14.3 us (8%)
  local copies, waits for them, and re-layouts  8.88 us (5%)
  matrix products  4.97 us (3%)
  other arithmetic  4.35 us (2%)
    all_to_all x3, waiting for transfers between devices, exchange(): lax.all_to_all(parts, 'ctx', 0, 0, tiled=True, axis_index_groups=SAME_CORE)  51.7 us
    pallas_call x4, Pallas kernels, call(): pl.pallas_call(kernel, out_shape=outputs, in_specs=[smem(), smem()] + [vm...  45.3 us
    ppermute x21, waiting for transfers between devices, ctx_move(): return lax.ppermute(value, 'ctx', pairs)  17.2 us
    all_to_all x3, starting transfers between devices, exchange(): lax.all_to_all(parts, 'ctx', 0, 0, tiled=True, axis_index_groups=SAME_CORE)  16 us
    ppermute x21, starting transfers between devices, ctx_move(): return lax.ppermute(value, 'ctx', pairs)  15.5 us
    unnamed x50, local copies, waits for them, and re-layouts  7.94 us
    dot_general x1, matrix products, nt(): lax.dot_general(a, b, (((1,), (1,)), ((), ())), preferred_element_type=F32)  4.97 us
  transfers between devices with their start and end apart: 26, of which 11 were waited for; matrix products, arithmetic and copies ran while one was open for 7% of the time, Pallas kernels for 25%

profile of v4, /device:TPU:0, one launch (start us, length us, event | category | flops | bytes accessed | tf_op | source)
XLA Modules:
  0.0 179.4 jit_solution(14538626284335101501)
XLA Ops:
  7.2 0.0 all-gather.3.cloned.1.call-start
  7.2 0.7 all-gather.3.cloned.1.call-update
  7.9 0.0 all-gather.5.cloned.1.call-start
  7.9 0.9 constant_dynamic-update-slice_fusion.1
  8.9 0.9 constant_dynamic-update-slice_fusion.rest_0_.rest_8_
  9.8 3.2 %collective-permute-start.1 = (bf16[384,256]{1,0:T(8,128)(2,1)S(1)}, bf16[384,256]{1,0:T(8,128)(2,1)S(1)}, u32[]{:S(2)}, u32[]{:S(2)}) collective-permute-start(bf16[384,256]{1,0:T(8,128)(2,1)S(1)} %constant_dynamic-update-slice_fusion.rest_0_.rest_8_), channel_id=1, source_target_pairs={{0,64},{8,72},{16,80},{24,88},{32,96},{40,104},{48,112},{56,120},{... | collective-permute-start | bytes 589832 | tf_op jit(solution)/shard_map/ppermute | solution.py:35
  13.0 1.9 %collective-permute-start.2 = (bf16[384,256]{1,0:T(8,128)(2,1)S(1)}, bf16[384,256]{1,0:T(8,128)(2,1)S(1)}, u32[]{:S(2)}, u32[]{:S(2)}) collective-permute-start(bf16[384,256]{1,0:T(8,128)(2,1)S(1)} %constant_dynamic-update-slice_fusion.rest_0_.rest_8_), channel_id=1, source_target_pairs={{0,16},{8,24},{16,32},{24,40},{32,48},{40,56},{48,0},{56,8},{64,80... | collective-permute-start | bytes 589832 | tf_op jit(solution)/shard_map/ppermute | solution.py:35
  14.9 2.1 %collective-permute-start.3 = (bf16[384,256]{1,0:T(8,128)(2,1)S(1)}, bf16[384,256]{1,0:T(8,128)(2,1)S(1)}, u32[]{:S(2)}, u32[]{:S(2)}) collective-permute-start(bf16[384,256]{1,0:T(8,128)(2,1)S(1)} %constant_dynamic-update-slice_fusion.rest_0_.rest_8_), channel_id=1, source_target_pairs={{0,48},{8,56},{16,0},{24,8},{32,16},{40,24},{48,32},{56,40},{64,11... | collective-permute-start | bytes 589832 | tf_op jit(solution)/shard_map/ppermute | solution.py:35
  17.0 0.9 collective-permute-done.1.rest_1_.rest_9_
  17.9 4.3 %collective-permute-start.5 = (bf16[384,256]{1,0:T(8,128)(2,1)S(1)}, bf16[384,256]{1,0:T(8,128)(2,1)S(1)}, u32[]{:S(2)}, u32[]{:S(2)}) collective-permute-start(bf16[384,256]{1,0:T(8,128)(2,1)S(1)} %collective-permute-done.1.rest_1_.rest_9_), channel_id=1, source_target_pairs={{0,48},{8,56},{16,0},{24,8},{32,16},{40,24},{48,32},{56,40},{64,11... | collective-permute-start | bytes 589832 | tf_op jit(solution)/shard_map/ppermute | solution.py:35
  22.1 0.0 collective-permute-start
  22.1 0.0 collective-permute-done.2.rest_2_.rest_10_
  22.1 0.1 collective-permute-start.4
  22.2 0.0 collective-permute-done.3.rest_3_.rest_11_
  22.3 1.7 collective-permute-start.6
  24.0 0.0 collective-permute-done.8.rest_8_
  24.0 1.4 collective-permute-done.5.rest_5_.rest_13_
  25.4 0.0 collective-permute-start.10
  25.4 5.7 %collective-permute-done.4.rest_4_.rest_12_ = bf16[384,256]{1,0:T(8,128)(2,1)S(1)} collective-permute-done((bf16[384,256]{1,0:T(8,128)(2,1)S(1)}, bf16[384,256]{1,0:T(8,128)(2,1)S(1)}, u32[]{:S(2)}, u32[]{:S(2)}) %collective-permute-start.4) | collective-permute-done | bytes 196640 | tf_op jit(solution)/shard_map/ppermute | solution.py:35
  31.1 0.1 collective-permute-start.7
  31.2 3.7 %collective-permute-done.6.rest_6_.rest_14_ = bf16[384,256]{1,0:T(8,128)(2,1)S(1)} collective-permute-done((bf16[384,256]{1,0:T(8,128)(2,1)S(1)}, bf16[384,256]{1,0:T(8,128)(2,1)S(1)}, u32[]{:S(2)}, u32[]{:S(2)}) %collective-permute-start.6) | collective-permute-done | bytes 196640 | tf_op jit(solution)/shard_map/ppermute | solution.py:35
  34.9 0.5 collective-permute-start.13
  35.4 0.1 collective-permute-start.12
  35.5 0.0 collective-permute-done.rest_1_
  35.5 0.4 collective-permute-start.14
  35.9 1.3 collective-permute-done.7.rest_7_.rest_15_
  37.2 1.4 copy.14.spans
  38.6 0.6 pad_add_fusion.ids
  39.2 0.0 collective-permute-done.12.rest_12_
  39.4 0.5 copy-done.16
  39.9 0.1 copy-done.17
  40.0 0.1 copy-done.18
  40.1 0.1 copy-done.19
  40.1 0.7 copy-done.20
  40.8 15.0 %forward.1 = (bf16[384,512]{1,0:T(8,128)(2,1)}, f32[2,8,768]{2,1,0:T(8,128)}) custom-call(s32[2]{0:T(128)} %pad_add_fusion.ids, s32[16,2]{1,0:T(8,128)} %copy.14.spans, bf16[384,512]{1,0:T(8,128)(2,1)} %rest_0_.1, bf16[384,256]{1,0:T(8,128)(2,1)} %copy-done.1, bf16[384,256]{1,0:T(8,128)(2,1)} %copy-done.2, bf16[384,256]{1,0:T(8,128)(2,1)} %copy-done.3, ...), custom_call_target="tpu_custom_call" | custom-call | flops 1000000 | bytes 1024 | tf_op jit(solution)/shard_map/forward/pallas_call | solution.py:153
  55.8 0.0 all-gather.5.cloned.1.call-update
  55.8 0.0 copy-start.21
  55.9 0.4 all-gather.3.cloned.1.call-done.grad_own
  56.3 0.1 collective-permute-start.20
  56.4 0.4 collective-permute-start.17
  56.8 5.0 %convolution_convert_fusion.rest_2_ = bf16[384,512]{1,0:T(8,128)(2,1)S(1)} fusion(bf16[384,4096]{1,0:T(8,128)(2,1)} %all-gather.3.cloned.1.call-done.grad_own, bf16[512,4096]{1,0:T(8,128)(2,1)} %param.12), kind=kOutput, calls=%fused_computation.3 | convolution fusion | flops 1610809344 | bytes 7733248 | tf_op jit(solution)/shard_map/dot_general | solution.py:64
  61.8 0.2 collective-permute-start.16
  62.0 0.4 collective-permute-start.18
  62.4 1.3 collective-permute-done.18.rest_7_
  63.7 0.6 copy-done.22
  64.3 0.1 copy-done.10
  64.4 0.8 copy-done.12
  65.2 17.6 %backward.1 = bf16[16,192,256]{2,1,0:T(8,128)(2,1)} custom-call(s32[2]{0:T(128)} %pad_add_fusion.ids, s32[16,2]{1,0:T(8,128)} %copy.14.spans, bf16[384,512]{1,0:T(8,128)(2,1)} %rest_0_.1, bf16[384,512]{1,0:T(8,128)(2,1)} %copy-done.9, bf16[384,512]{1,0:T(8,128)(2,1)} %copy-done.11, bf16[384,512]{1,0:T(8,128)(2,1)} %copy-done.12, ...), custom_call_target="tpu_custom_call" | custom-call | flops 1000000 | bytes 1024 | tf_op jit(solution)/shard_map/backward/pallas_call | solution.py:153
  82.7 6.5 %all-to-all-start = ((bf16[16,192,256]{2,1,0:T(8,128)(2,1)}), bf16[16,192,256]{2,1,0:T(8,128)(2,1)S(1)}, u32[]{:S(2)}, u32[]{:S(2)}) async-start(bf16[16,192,256]{2,1,0:T(8,128)(2,1)} %backward.1), calls=%async_computation | async-start | bytes 3145728 | tf_op jit(solution)/shard_map/all_to_all | solution.py:347
  89.2 6.9 %out_gradient.1 = bf16[8,512,256]{2,1,0:T(8,128)(2,1)} custom-call(s32[2]{0:T(128)} %pad_add_fusion.ids, s32[3,16]{1,0:T(4,128)} %owners.3, bf16[384,512]{1,0:T(8,128)(2,1)} %get-tuple-element.20.rest_4_.attn_own, bf16[384,512]{1,0:T(8,128)(2,1)} %copy-done.10, bf16[384,4096]{1,0:T(8,128)(2,1)} %all-gather.3.cloned.1.call-done.grad_own, ...), custom_call_target="tpu_custom_call" | custom-call | flops 8000000000 | bytes 1024 | tf_op jit(solution)/shard_map/out_gradient/pallas_call | solution.py:153
  96.1 21.8 %all-to-all-done = bf16[16,192,256]{2,1,0:T(8,128)(2,1)S(1)} async-done(((bf16[16,192,256]{2,1,0:T(8,128)(2,1)}), bf16[16,192,256]{2,1,0:T(8,128)(2,1)S(1)}, u32[]{:S(2)}, u32[]{:S(2)}) %all-to-all-start) | async-done | bytes 1572896 | tf_op jit(solution)/shard_map/all_to_all | solution.py:347
  117.9 1.2 copy-done
  119.1 4.7 %all-to-all-start.1 = ((bf16[8,512,256]{2,1,0:T(8,128)(2,1)}), bf16[8,512,256]{2,1,0:T(8,128)(2,1)S(1)}, u32[]{:S(2)}, u32[]{:S(2)}) async-start(bf16[8,512,256]{2,1,0:T(8,128)(2,1)} %out_gradient.1), calls=%async_computation.1 | async-start | bytes 4194304 | tf_op jit(solution)/shard_map/all_to_all | solution.py:347
  123.8 0.0 all-gather.5.cloned.1.call-done.hidden_ref
  123.8 5.9 %kv_gradient.1 = (bf16[8,256,256]{2,1,0:T(8,128)(2,1)}, bf16[8,256,256]{2,1,0:T(8,128)(2,1)}) custom-call(s32[2]{0:T(128)} %pad_add_fusion.ids, s32[3,16]{1,0:T(4,128)} %owners.3, bf16[8,384,256]{2,1,0:T(8,128)(2,1)} %bitcast.9, bf16[384,4096]{1,0:T(8,128)(2,1)} %all-gather.5.cloned.1.call-done.hidden_ref), custom_call_target="tpu_custom_call" | custom-call | flops 1000000 | bytes 1024 | tf_op jit(solution)/shard_map/kv_gradient/pallas_call | solution.py:153
  129.7 2.9 %collective-permute-done.19 = bf16[8,256,256]{2,1,0:T(8,128)(2,1)S(1)} collective-permute-done((bf16[8,256,256]{2,1,0:T(8,128)(2,1)}, bf16[8,256,256]{2,1,0:T(8,128)(2,1)S(1)}, u32[]{:S(2)}, u32[]{:S(2)}) %collective-permute-start.19) | collective-permute-done | bytes 1048608 | tf_op jit(solution)/shard_map/ppermute | solution.py:35
  132.6 2.5 %add_convert_fusion = bf16[8,256,256]{2,1,0:T(8,128)(2,1)} fusion(bf16[8,256,256]{2,1,0:T(8,128)(2,1)S(1)} %collective-permute-done.19, bf16[8,256,256]{2,1,0:T(8,128)(2,1)} %get-tuple-element.18), kind=kLoop, calls=%fused_computation.2 | loop fusion | flops 2097152 | bytes 3145728 | tf_op jit(solution)/shard_map/convert_element_type | solution.py:351
  135.1 15.1 %all-to-all-done.1 = bf16[8,512,256]{2,1,0:T(8,128)(2,1)S(1)} async-done(((bf16[8,512,256]{2,1,0:T(8,128)(2,1)}), bf16[8,512,256]{2,1,0:T(8,128)(2,1)S(1)}, u32[]{:S(2)}, u32[]{:S(2)}) %all-to-all-start.1) | async-done | bytes 2097184 | tf_op jit(solution)/shard_map/all_to_all | solution.py:347
  150.2 4.8 %all-to-all-start.2 = ((bf16[8,256,256]{2,1,0:T(8,128)(2,1)}), bf16[8,256,256]{2,1,0:T(8,128)(2,1)S(1)}, u32[]{:S(2)}, u32[]{:S(2)}) async-start(bf16[8,256,256]{2,1,0:T(8,128)(2,1)} %add_convert_fusion), calls=%async_computation.2 | async-start | bytes 2097152 | tf_op jit(solution)/shard_map/all_to_all | solution.py:347
  155.0 1.1 convert_reduce_fusion
  156.1 14.8 %all-to-all-done.2 = bf16[8,256,256]{2,1,0:T(8,128)(2,1)S(1)} async-done(((bf16[8,256,256]{2,1,0:T(8,128)(2,1)}), bf16[8,256,256]{2,1,0:T(8,128)(2,1)S(1)}, u32[]{:S(2)}, u32[]{:S(2)}) %all-to-all-start.2) | async-done | bytes 1048608 | tf_op jit(solution)/shard_map/all_to_all | solution.py:347
  170.9 0.1 convert_reduce_fusion.1
  171.0 0.8 copy.15
  171.8 0.8 copy.16
  (51 shorter events, 0.1 us)
Async XLA Ops:
  7.2 49.1 %all-gather.3.cloned.1.call-start = ((), (), s32[]{:S(2)}) async-start(), calls=%async_computation.3 | async-start | bytes 3538944 | tf_op jit(solution)/shard_map/all_gather | solution.py:360
  7.9 115.9 %all-gather.5.cloned.1.call-start = ((), (), s32[]{:S(2)}) async-start(), calls=%async_computation.4 | async-start | bytes 3538944 | tf_op jit(solution)/shard_map/all_gather | solution.py:364
  9.8 29.5 %copy-start.1 = (bf16[384,256]{1,0:T(8,128)(2,1)}, bf16[384,256]{1,0:T(8,128)(2,1)S(1)}, u32[]{:S(2)}) copy-start(bf16[384,256]{1,0:T(8,128)(2,1)S(1)} %constant_dynamic-update-slice_fusion.rest_0_.rest_8_) | copy-start | bytes 589828
  9.8 8.1 %collective-permute-start.1 = (bf16[384,256]{1,0:T(8,128)(2,1)S(1)}, bf16[384,256]{1,0:T(8,128)(2,1)S(1)}, u32[]{:S(2)}, u32[]{:S(2)}) collective-permute-start(bf16[384,256]{1,0:T(8,128)(2,1)S(1)} %constant_dynamic-update-slice_fusion.rest_0_.rest_8_), channel_id=1, source_target_pairs={{0,64},{8,72},{16,80},{24,88},{32,96},{40,104},{48,112},{56,120},{... | collective-permute-start | bytes 589832 | tf_op jit(solution)/shard_map/ppermute | solution.py:35
  13.0 9.2 %collective-permute-start.2 = (bf16[384,256]{1,0:T(8,128)(2,1)S(1)}, bf16[384,256]{1,0:T(8,128)(2,1)S(1)}, u32[]{:S(2)}, u32[]{:S(2)}) collective-permute-start(bf16[384,256]{1,0:T(8,128)(2,1)S(1)} %constant_dynamic-update-slice_fusion.rest_0_.rest_8_), channel_id=1, source_target_pairs={{0,16},{8,24},{16,32},{24,40},{32,48},{40,56},{48,0},{56,8},{64,80... | collective-permute-start | bytes 589832 | tf_op jit(solution)/shard_map/ppermute | solution.py:35
  14.9 7.3 %collective-permute-start.3 = (bf16[384,256]{1,0:T(8,128)(2,1)S(1)}, bf16[384,256]{1,0:T(8,128)(2,1)S(1)}, u32[]{:S(2)}, u32[]{:S(2)}) collective-permute-start(bf16[384,256]{1,0:T(8,128)(2,1)S(1)} %constant_dynamic-update-slice_fusion.rest_0_.rest_8_), channel_id=1, source_target_pairs={{0,48},{8,56},{16,0},{24,8},{32,16},{40,24},{48,32},{56,40},{64,11... | collective-permute-start | bytes 589832 | tf_op jit(solution)/shard_map/ppermute | solution.py:35
  17.0 7.0 %collective-permute-start.8 = (bf16[384,256]{1,0:T(8,128)(2,1)S(1)}, bf16[384,256]{1,0:T(8,128)(2,1)S(1)}, u32[]{:S(2)}, u32[]{:S(2)}) collective-permute-start(bf16[384,256]{1,0:T(8,128)(2,1)S(1)} %constant_dynamic-update-slice_fusion.rest_0_.rest_8_), channel_id=1, source_target_pairs={{0,8},{8,0},{16,24},{24,16},{32,40},{40,32},{48,56},{56,48},{64,72... | collective-permute-start | bytes 589832 | tf_op jit(solution)/shard_map/ppermute | solution.py:35
  17.9 21.4 %copy-start.2 = (bf16[384,256]{1,0:T(8,128)(2,1)}, bf16[384,256]{1,0:T(8,128)(2,1)S(1)}, u32[]{:S(2)}) copy-start(bf16[384,256]{1,0:T(8,128)(2,1)S(1)} %collective-permute-done.1.rest_1_.rest_9_) | copy-start | bytes 589828
  17.9 7.5 %collective-permute-start.5 = (bf16[384,256]{1,0:T(8,128)(2,1)S(1)}, bf16[384,256]{1,0:T(8,128)(2,1)S(1)}, u32[]{:S(2)}, u32[]{:S(2)}) collective-permute-start(bf16[384,256]{1,0:T(8,128)(2,1)S(1)} %collective-permute-done.1.rest_1_.rest_9_), channel_id=1, source_target_pairs={{0,48},{8,56},{16,0},{24,8},{32,16},{40,24},{48,32},{56,40},{64,11... | collective-permute-start | bytes 589832 | tf_op jit(solution)/shard_map/ppermute | solution.py:35
  22.1 13.4 %collective-permute-start = (bf16[384,512]{1,0:T(8,128)(2,1)}, bf16[384,512]{1,0:T(8,128)(2,1)S(1)}, u32[]{:S(2)}, u32[]{:S(2)}) collective-permute-start(bf16[384,512]{1,0:T(8,128)(2,1)} %rest_0_.1), channel_id=1, source_target_pairs={{0,8},{8,0},{16,24},{24,16},{32,40},{40,32},{48,56},{56,48},{64,72... | collective-permute-start | bytes 1179656 | tf_op jit(solution)/shard_map/ppermute | solution.py:35
  22.1 17.2 %copy-start.3 = (bf16[384,256]{1,0:T(8,128)(2,1)}, bf16[384,256]{1,0:T(8,128)(2,1)S(1)}, u32[]{:S(2)}) copy-start(bf16[384,256]{1,0:T(8,128)(2,1)S(1)} %collective-permute-done.2.rest_2_.rest_10_) | copy-start | bytes 589828
  22.1 9.0 %collective-permute-start.4 = (bf16[384,256]{1,0:T(8,128)(2,1)S(1)}, bf16[384,256]{1,0:T(8,128)(2,1)S(1)}, u32[]{:S(2)}, u32[]{:S(2)}) collective-permute-start(bf16[384,256]{1,0:T(8,128)(2,1)S(1)} %collective-permute-done.1.rest_1_.rest_9_), channel_id=1, source_target_pairs={{0,16},{8,24},{16,32},{24,40},{32,48},{40,56},{48,0},{56,8},{64,80... | collective-permute-start | bytes 589832 | tf_op jit(solution)/shard_map/ppermute | solution.py:35
  22.2 17.1 %copy-start.4 = (bf16[384,256]{1,0:T(8,128)(2,1)}, bf16[384,256]{1,0:T(8,128)(2,1)S(1)}, u32[]{:S(2)}) copy-start(bf16[384,256]{1,0:T(8,128)(2,1)S(1)} %collective-permute-done.3.rest_3_.rest_11_) | copy-start | bytes 589828
  22.3 12.6 %collective-permute-start.6 = (bf16[384,256]{1,0:T(8,128)(2,1)S(1)}, bf16[384,256]{1,0:T(8,128)(2,1)S(1)}, u32[]{:S(2)}, u32[]{:S(2)}) collective-permute-start(bf16[384,256]{1,0:T(8,128)(2,1)S(1)} %collective-permute-done.2.rest_2_.rest_10_), channel_id=1, source_target_pairs={{0,16},{8,24},{16,32},{24,40},{32,48},{40,56},{48,0},{56,8},{64,80... | collective-permute-start | bytes 589832 | tf_op jit(solution)/shard_map/ppermute | solution.py:35
  24.0 15.3 %copy-start.13 = (bf16[384,256]{1,0:T(8,128)(2,1)}, bf16[384,256]{1,0:T(8,128)(2,1)S(1)}, u32[]{:S(2)}) copy-start(bf16[384,256]{1,0:T(8,128)(2,1)S(1)} %collective-permute-done.8.rest_8_) | copy-start | bytes 589828
  24.0 10.9 %collective-permute-start.9 = (bf16[384,256]{1,0:T(8,128)(2,1)S(1)}, bf16[384,256]{1,0:T(8,128)(2,1)S(1)}, u32[]{:S(2)}, u32[]{:S(2)}) collective-permute-start(bf16[384,256]{1,0:T(8,128)(2,1)S(1)} %collective-permute-done.1.rest_1_.rest_9_), channel_id=1, source_target_pairs={{0,8},{8,0},{16,24},{24,16},{32,40},{40,32},{48,56},{56,48},{64,72... | collective-permute-start | bytes 589832 | tf_op jit(solution)/shard_map/ppermute | solution.py:35
  25.4 13.9 %copy-start.5 = (bf16[384,256]{1,0:T(8,128)(2,1)}, bf16[384,256]{1,0:T(8,128)(2,1)S(1)}, u32[]{:S(2)}) copy-start(bf16[384,256]{1,0:T(8,128)(2,1)S(1)} %collective-permute-done.5.rest_5_.rest_13_) | copy-start | bytes 589828
  25.4 10.0 %collective-permute-start.10 = (bf16[384,256]{1,0:T(8,128)(2,1)S(1)}, bf16[384,256]{1,0:T(8,128)(2,1)S(1)}, u32[]{:S(2)}, u32[]{:S(2)}) collective-permute-start(bf16[384,256]{1,0:T(8,128)(2,1)S(1)} %collective-permute-done.2.rest_2_.rest_10_), channel_id=1, source_target_pairs={{0,8},{8,0},{16,24},{24,16},{32,40},{40,32},{48,56},{56,48},{64,72... | collective-permute-start | bytes 589832 | tf_op jit(solution)/shard_map/ppermute | solution.py:35
  31.1 8.2 %copy-start.6 = (bf16[384,256]{1,0:T(8,128)(2,1)}, bf16[384,256]{1,0:T(8,128)(2,1)S(1)}, u32[]{:S(2)}) copy-start(bf16[384,256]{1,0:T(8,128)(2,1)S(1)} %collective-permute-done.4.rest_4_.rest_12_) | copy-start | bytes 589828
  31.1 6.1 %collective-permute-start.7 = (bf16[384,256]{1,0:T(8,128)(2,1)S(1)}, bf16[384,256]{1,0:T(8,128)(2,1)S(1)}, u32[]{:S(2)}, u32[]{:S(2)}) collective-permute-start(bf16[384,256]{1,0:T(8,128)(2,1)S(1)} %collective-permute-done.5.rest_5_.rest_13_), channel_id=1, source_target_pairs={{0,48},{8,56},{16,0},{24,8},{32,16},{40,24},{48,32},{56,40},{64,11... | collective-permute-start | bytes 589832 | tf_op jit(solution)/shard_map/ppermute | solution.py:35
  34.9 4.5 %copy-start.7 = (bf16[384,256]{1,0:T(8,128)(2,1)}, bf16[384,256]{1,0:T(8,128)(2,1)S(1)}, u32[]{:S(2)}) copy-start(bf16[384,256]{1,0:T(8,128)(2,1)S(1)} %collective-permute-done.6.rest_6_.rest_14_) | copy-start | bytes 589828
  34.9 4.3 %collective-permute-start.11 = (bf16[384,256]{1,0:T(8,128)(2,1)S(1)}, bf16[384,256]{1,0:T(8,128)(2,1)S(1)}, u32[]{:S(2)}, u32[]{:S(2)}) collective-permute-start(bf16[384,256]{1,0:T(8,128)(2,1)S(1)} %collective-permute-done.3.rest_3_.rest_11_), channel_id=1, source_target_pairs={{0,8},{8,0},{16,24},{24,16},{32,40},{40,32},{48,56},{56,48},{64,72... | collective-permute-start | bytes 589832 | tf_op jit(solution)/shard_map/ppermute | solution.py:35
  34.9 4.5 %copy-start.14 = (bf16[384,256]{1,0:T(8,128)(2,1)}, bf16[384,256]{1,0:T(8,128)(2,1)S(1)}, u32[]{:S(2)}) copy-start(bf16[384,256]{1,0:T(8,128)(2,1)S(1)} %collective-permute-done.9.rest_9_) | copy-start | bytes 589828
  34.9 4.3 %collective-permute-start.13 = (bf16[384,256]{1,0:T(8,128)(2,1)S(1)}, bf16[384,256]{1,0:T(8,128)(2,1)S(1)}, u32[]{:S(2)}, u32[]{:S(2)}) collective-permute-start(bf16[384,256]{1,0:T(8,128)(2,1)S(1)} %collective-permute-done.5.rest_5_.rest_13_), channel_id=1, source_target_pairs={{0,8},{8,0},{16,24},{24,16},{32,40},{40,32},{48,56},{56,48},{64,72... | collective-permute-start | bytes 589832 | tf_op jit(solution)/shard_map/ppermute | solution.py:35
  35.4 4.0 %copy-start.15 = (bf16[384,256]{1,0:T(8,128)(2,1)}, bf16[384,256]{1,0:T(8,128)(2,1)S(1)}, u32[]{:S(2)}) copy-start(bf16[384,256]{1,0:T(8,128)(2,1)S(1)} %collective-permute-done.10.rest_10_) | copy-start | bytes 589828
  35.4 3.8 %collective-permute-start.12 = (bf16[384,256]{1,0:T(8,128)(2,1)S(1)}, bf16[384,256]{1,0:T(8,128)(2,1)S(1)}, u32[]{:S(2)}, u32[]{:S(2)}) collective-permute-start(bf16[384,256]{1,0:T(8,128)(2,1)S(1)} %collective-permute-done.4.rest_4_.rest_12_), channel_id=1, source_target_pairs={{0,8},{8,0},{16,24},{24,16},{32,40},{40,32},{48,56},{56,48},{64,72... | collective-permute-start | bytes 589832 | tf_op jit(solution)/shard_map/ppermute | solution.py:35
  35.5 28.2 %copy-start.9 = (bf16[384,512]{1,0:T(8,128)(2,1)}, bf16[384,512]{1,0:T(8,128)(2,1)S(1)}, u32[]{:S(2)}) copy-start(bf16[384,512]{1,0:T(8,128)(2,1)S(1)} %collective-permute-done.rest_1_) | copy-start | bytes 1179652
  35.5 3.8 %collective-permute-start.14 = (bf16[384,256]{1,0:T(8,128)(2,1)S(1)}, bf16[384,256]{1,0:T(8,128)(2,1)S(1)}, u32[]{:S(2)}, u32[]{:S(2)}) collective-permute-start(bf16[384,256]{1,0:T(8,128)(2,1)S(1)} %collective-permute-done.6.rest_6_.rest_14_), channel_id=1, source_target_pairs={{0,8},{8,0},{16,24},{24,16},{32,40},{40,32},{48,56},{56,48},{64,72... | collective-permute-start | bytes 589832 | tf_op jit(solution)/shard_map/ppermute | solution.py:35
  37.2 2.2 %copy-start.8 = (bf16[384,256]{1,0:T(8,128)(2,1)}, bf16[384,256]{1,0:T(8,128)(2,1)S(1)}, u32[]{:S(2)}) copy-start(bf16[384,256]{1,0:T(8,128)(2,1)S(1)} %collective-permute-done.7.rest_7_.rest_15_) | copy-start | bytes 589828
  37.2 2.1 %collective-permute-start.15 = (bf16[384,256]{1,0:T(8,128)(2,1)S(1)}, bf16[384,256]{1,0:T(8,128)(2,1)S(1)}, u32[]{:S(2)}, u32[]{:S(2)}) collective-permute-start(bf16[384,256]{1,0:T(8,128)(2,1)S(1)} %collective-permute-done.7.rest_7_.rest_15_), channel_id=1, source_target_pairs={{0,8},{8,0},{16,24},{24,16},{32,40},{40,32},{48,56},{56,48},{64,72... | collective-permute-start | bytes 589832 | tf_op jit(solution)/shard_map/ppermute | solution.py:35
  39.2 0.7 copy-start.16
  39.2 0.8 copy-start.17
  39.3 0.8 copy-start.18
  39.3 0.9 copy-start.19
  40.1 0.7 copy-start.20
  55.8 6.2 %copy-start.21 = (f32[2,8,768]{2,1,0:T(8,128)S(1)}, f32[2,8,768]{2,1,0:T(8,128)}, u32[]{:S(2)}) copy-start(f32[2,8,768]{2,1,0:T(8,128)} %get-tuple-element.16.rest_6_) | copy-start | bytes 147460
  56.3 32.9 %collective-permute-start.20 = (bf16[384,4096]{1,0:T(8,128)(2,1)}, bf16[384,4096]{1,0:T(8,128)(2,1)}, u32[]{:S(2)}, u32[]{:S(2)}) collective-permute-start(bf16[384,4096]{1,0:T(8,128)(2,1)} %all-gather.3.cloned.1.call-done.grad_own), channel_id=1, source_target_pairs={{0,8},{8,0},{16,24},{24,16},{32,40},{40,32},{48,56},{56,48},{64,72... | collective-permute-start | bytes 9437192 | tf_op jit(solution)/shard_map/ppermute | solution.py:35
  56.4 7.2 %collective-permute-start.17 = (bf16[384,512]{1,0:T(8,128)(2,1)}, bf16[384,512]{1,0:T(8,128)(2,1)S(1)}, u32[]{:S(2)}, u32[]{:S(2)}) collective-permute-start(bf16[384,512]{1,0:T(8,128)(2,1)} %get-tuple-element.20.rest_4_.attn_own), channel_id=1, source_target_pairs={{0,8},{8,0},{16,24},{24,16},{32,40},{40,32},{48,56},{56,48},{64,72... | collective-permute-start | bytes 1179656 | tf_op jit(solution)/shard_map/ppermute | solution.py:35
  61.8 1.9 %copy-start.11 = (bf16[384,512]{1,0:T(8,128)(2,1)}, bf16[384,512]{1,0:T(8,128)(2,1)S(1)}, u32[]{:S(2)}) copy-start(bf16[384,512]{1,0:T(8,128)(2,1)S(1)} %convolution_convert_fusion.rest_2_) | copy-start | bytes 1179652
  61.8 1.9 %collective-permute-start.16 = (bf16[384,512]{1,0:T(8,128)(2,1)S(1)}, bf16[384,512]{1,0:T(8,128)(2,1)S(1)}, u32[]{:S(2)}, u32[]{:S(2)}) collective-permute-start(bf16[384,512]{1,0:T(8,128)(2,1)S(1)} %convolution_convert_fusion.rest_2_), channel_id=1, source_target_pairs={{0,8},{8,0},{16,24},{24,16},{32,40},{40,32},{48,56},{56,48},{64,72... | collective-permute-start | bytes 1179656 | tf_op jit(solution)/shard_map/ppermute | solution.py:35
  62.0 1.6 collective-permute-start.18
  63.7 0.6 copy-start.22
  63.7 0.8 copy-start.10
  64.4 0.8 copy-start.12
  82.7 35.2 %all-to-all-start = ((bf16[16,192,256]{2,1,0:T(8,128)(2,1)}), bf16[16,192,256]{2,1,0:T(8,128)(2,1)S(1)}, u32[]{:S(2)}, u32[]{:S(2)}) async-start(bf16[16,192,256]{2,1,0:T(8,128)(2,1)} %backward.1), calls=%async_computation | async-start | bytes 3145728 | tf_op jit(solution)/shard_map/all_to_all | solution.py:347
  117.9 1.2 copy-start
  119.1 31.1 %all-to-all-start.1 = ((bf16[8,512,256]{2,1,0:T(8,128)(2,1)}), bf16[8,512,256]{2,1,0:T(8,128)(2,1)S(1)}, u32[]{:S(2)}, u32[]{:S(2)}) async-start(bf16[8,512,256]{2,1,0:T(8,128)(2,1)} %out_gradient.1), calls=%async_computation.1 | async-start | bytes 4194304 | tf_op jit(solution)/shard_map/all_to_all | solution.py:347
  129.7 2.9 %collective-permute-start.19 = (bf16[8,256,256]{2,1,0:T(8,128)(2,1)}, bf16[8,256,256]{2,1,0:T(8,128)(2,1)S(1)}, u32[]{:S(2)}, u32[]{:S(2)}) collective-permute-start(bf16[8,256,256]{2,1,0:T(8,128)(2,1)} %get-tuple-element.19), channel_id=1, source_target_pairs={{0,8},{8,0},{16,24},{24,16},{32,40},{40,32},{48,56},{56,48},{64,72... | collective-permute-start | bytes 3145736 | tf_op jit(solution)/shard_map/ppermute | solution.py:35
  150.2 20.6 %all-to-all-start.2 = ((bf16[8,256,256]{2,1,0:T(8,128)(2,1)}), bf16[8,256,256]{2,1,0:T(8,128)(2,1)S(1)}, u32[]{:S(2)}, u32[]{:S(2)}) async-start(bf16[8,256,256]{2,1,0:T(8,128)(2,1)} %add_convert_fusion), calls=%async_computation.2 | async-start | bytes 2097152 | tf_op jit(solution)/shard_map/all_to_all | solution.py:347
Sparse Core Ops, SparseCore 0:
  9.6 46.6 all-gather.2
  57.9 51.3 all-gather.4

commit v5 on v4

--- a/solution.py
+++ b/solution.py
@@ -54,6 +54,13 @@
     return ctx_move(value, 0, 0, 1)
 
 
+def head_flip(value):
+    return lax.ppermute(value, "head", [(i, i ^ 4) for i in range(8)])
+
+
+SAME_X = [[0, 1, 2, 3], [4, 5, 6, 7]]
+
+
 def source_of(ids, step, other_core):
     x, z, c = ids[0] // 8, (ids[0] // 2) % 4, ids[0] % 2
     dx, dz = STEPS[step]
@@ -279,6 +286,11 @@
         found[owners[n, b]] = b
 
 
+def paired_block(ids, b):
+    x, y, half = b // 8, (b // 2) % 4, b % 2
+    return y * 4 + (x ^ (ids[1] // 4)) * 2 + half
+
+
 def feature_block(ref, b):
     return ref[:, pl.ds(pl.multiple_of(b * FEATURES, FEATURES), FEATURES)]
 
@@ -321,7 +333,7 @@
     for out_ref, at in ((other_ref, 1 - core), (own_ref, core)):
         for chip in range(CHIPS):
             for n, found in enumerate((found_k, found_v)):
-                block = nn(both[n], feature_block(hidden_ref, found[chip * 2 + at]))
+                block = nn(both[n], feature_block(hidden_ref, paired_block(ids, found[chip * 2 + at])))
                 out_ref[chip, n * HEAD_SIZE : (n + 1) * HEAD_SIZE, :] = (
                     block[:HEAD_SIZE] + block[HEAD_SIZE:]
                 ).astype(BF16)
@@ -361,17 +373,20 @@
     kv_pieces = gather_over_ctx(jnp.concatenate([key, value], axis=1))
     query_other = swap(query)
     attn, lse = forward(ids, span_map, after(query, query_other), kv_pieces)
-    hidden = lax.all_gather(after(hidden_in, attn), "head", axis=1, tiled=True)
+    hidden_other = head_flip(after(hidden_in, attn))
     d_attn = nt(after(grad, attn), out_weight).astype(BF16)
     attn_other = swap(attn)
-    sides = (query, query_other, d_attn, swap(d_attn), attn, attn_other, lse, swap(lse))
+    out_parts = out_gradient(
+        ids, owner_map, after(attn, d_attn), attn_other, grad, swap(after(grad, attn))
+    )
+    hidden_pair = jnp.concatenate([hidden_in, after(hidden_other, out_parts)], axis=1)
+    hidden = lax.all_gather(hidden_pair, "head", axis=1, tiled=True, axis_index_groups=SAME_X)
+    query_late = after(query, out_parts, hidden_pair)
+    out_parts = exchange(out_parts)
+    sides = (query_late, query_other, d_attn, swap(d_attn), attn, attn_other, lse, swap(lse))
     dkv = backward(ids, span_map, sides, kv_pieces[:8])
-    attn_late = after(attn, dkv)
-    dkv = exchange(dkv).reshape(CHIPS, TOKENS, 2 * HEAD_SIZE)
-    out_parts = out_gradient(ids, owner_map, attn_late, attn_other, grad, swap(grad))
-    out_parts = exchange(after(out_parts, dkv))
-    kv_total = chip_sum(*kv_gradient(ids, owner_map, dkv, hidden))
-    kv_total = exchange(after(kv_total, out_parts))
+    dkv = exchange(after(dkv, out_parts)).reshape(CHIPS, TOKENS, 2 * HEAD_SIZE)
+    kv_total = exchange(chip_sum(*kv_gradient(ids, owner_map, dkv, hidden)))
     kv_total = jnp.sum(kv_total.astype(F32), axis=0)
     out_total = jnp.sum(out_parts.astype(F32), axis=0)
     return kv_total[:HEAD_SIZE].T, kv_total[HEAD_SIZE:].T, out_total

time: 180 us -> 173 us (0.961)
  waiting for transfers between devices: 70.1 us -> 38.8 us
  blocking collectives: 0 us -> 27.8 us
  starting transfers between devices: 31.5 us -> 26.6 us
    all_to_all x3 -> x2, waiting for transfers between devices: 51.7 us -> 19.5 us  [exchange(): lax.all_to_all(parts, 'ctx', 0, 0, tiled=True, axis_index_groups=SAME_CORE)]
    all_to_all x0 -> x1, blocking collectives: none -> 27.8 us  [exchange(): lax.all_to_all(parts, 'ctx', 0, 0, tiled=True, axis_index_groups=SAME_CORE)]
    all_to_all x3 -> x2, starting transfers between devices: 16 us -> 10.4 us  [exchange(): lax.all_to_all(parts, 'ctx', 0, 0, tiled=True, axis_index_groups=SAME_CORE)]
    unnamed x50 -> x47, local copies, waits for them, and re-layouts: 7.94 us -> 7.55 us
  transfers between devices with their start and end apart: 26 -> 26, of which waited for: 11 -> 10; matrix products, arithmetic and copies ran while one was open for 7% -> 6% of each run, Pallas kernels for 25% -> 23%
where the time goes in v5:
time: 173 us; the launch traced here: 172 us
  Pallas kernels  46.2 us (27%)
  waiting for transfers between devices  38.8 us (22%)
  blocking collectives  27.8 us (16%)
  starting transfers between devices  26.6 us (15%)
  between operations  14.3 us (8%)
  local copies, waits for them, and re-layouts  8.53 us (5%)
  matrix products  5.74 us (3%)
  other arithmetic  4.32 us (2%)
    pallas_call x4, Pallas kernels, call(): pl.pallas_call(kernel, out_shape=outputs, in_specs=[smem(), smem()] + [vm...  46.2 us
    all_to_all x1, blocking collectives, exchange(): lax.all_to_all(parts, 'ctx', 0, 0, tiled=True, axis_index_groups=SAME_CORE)  27.8 us
    all_to_all x2, waiting for transfers between devices, exchange(): lax.all_to_all(parts, 'ctx', 0, 0, tiled=True, axis_index_groups=SAME_CORE)  19.5 us
    ppermute x21, waiting for transfers between devices, ctx_move(): return lax.ppermute(value, 'ctx', pairs)  17.2 us
    ppermute x21, starting transfers between devices, ctx_move(): return lax.ppermute(value, 'ctx', pairs)  15.5 us
    all_to_all x2, starting transfers between devices, exchange(): lax.all_to_all(parts, 'ctx', 0, 0, tiled=True, axis_index_groups=SAME_CORE)  10.4 us
    unnamed x47, local copies, waits for them, and re-layouts  7.55 us
    dot_general x1, matrix products, nt(): lax.dot_general(a, b, (((1,), (1,)), ((), ())), preferred_element_type=F32)  5.74 us
  transfers between devices with their start and end apart: 26, of which 10 were waited for; matrix products, arithmetic and copies ran while one was open for 6% of the time, Pallas kernels for 23%

profile of v5, /device:TPU:0, one launch (start us, length us, event | category | flops | bytes accessed | tf_op | source)
XLA Modules:
  0.0 172.3 jit_solution(6365510375060181836)
XLA Ops:
  7.2 0.0 all-gather.3.cloned.1.call-start
  7.2 0.7 all-gather.3.cloned.1.call-update
  7.9 0.0 all-gather.5.cloned.1.call-start
  8.0 0.9 constant_dynamic-update-slice_fusion.1
  8.9 0.9 constant_dynamic-update-slice_fusion.rest_0_.rest_8_
  9.8 3.2 %collective-permute-start.1 = (bf16[384,256]{1,0:T(8,128)(2,1)S(1)}, bf16[384,256]{1,0:T(8,128)(2,1)S(1)}, u32[]{:S(2)}, u32[]{:S(2)}) collective-permute-start(bf16[384,256]{1,0:T(8,128)(2,1)S(1)} %constant_dynamic-update-slice_fusion.rest_0_.rest_8_), channel_id=1, source_target_pairs={{0,64},{8,72},{16,80},{24,88},{32,96},{40,104},{48,112},{56,120},{... | collective-permute-start | bytes 589832 | tf_op jit(solution)/shard_map/ppermute | solution.py:35
  13.0 1.9 %collective-permute-start.2 = (bf16[384,256]{1,0:T(8,128)(2,1)S(1)}, bf16[384,256]{1,0:T(8,128)(2,1)S(1)}, u32[]{:S(2)}, u32[]{:S(2)}) collective-permute-start(bf16[384,256]{1,0:T(8,128)(2,1)S(1)} %constant_dynamic-update-slice_fusion.rest_0_.rest_8_), channel_id=1, source_target_pairs={{0,16},{8,24},{16,32},{24,40},{32,48},{40,56},{48,0},{56,8},{64,80... | collective-permute-start | bytes 589832 | tf_op jit(solution)/shard_map/ppermute | solution.py:35
  14.9 2.1 %collective-permute-start.3 = (bf16[384,256]{1,0:T(8,128)(2,1)S(1)}, bf16[384,256]{1,0:T(8,128)(2,1)S(1)}, u32[]{:S(2)}, u32[]{:S(2)}) collective-permute-start(bf16[384,256]{1,0:T(8,128)(2,1)S(1)} %constant_dynamic-update-slice_fusion.rest_0_.rest_8_), channel_id=1, source_target_pairs={{0,48},{8,56},{16,0},{24,8},{32,16},{40,24},{48,32},{56,40},{64,11... | collective-permute-start | bytes 589832 | tf_op jit(solution)/shard_map/ppermute | solution.py:35
  17.0 0.0 collective-permute-start.8
  17.0 0.9 collective-permute-done.1.rest_1_.rest_9_
  17.9 4.3 %collective-permute-start.5 = (bf16[384,256]{1,0:T(8,128)(2,1)S(1)}, bf16[384,256]{1,0:T(8,128)(2,1)S(1)}, u32[]{:S(2)}, u32[]{:S(2)}) collective-permute-start(bf16[384,256]{1,0:T(8,128)(2,1)S(1)} %collective-permute-done.1.rest_1_.rest_9_), channel_id=1, source_target_pairs={{0,48},{8,56},{16,0},{24,8},{32,16},{40,24},{48,32},{56,40},{64,11... | collective-permute-start | bytes 589832 | tf_op jit(solution)/shard_map/ppermute | solution.py:35
  22.2 0.1 collective-permute-start.4
  22.2 0.0 collective-permute-done.3.rest_3_.rest_11_
  22.3 1.7 %collective-permute-start.6 = (bf16[384,256]{1,0:T(8,128)(2,1)S(1)}, bf16[384,256]{1,0:T(8,128)(2,1)S(1)}, u32[]{:S(2)}, u32[]{:S(2)}) collective-permute-start(bf16[384,256]{1,0:T(8,128)(2,1)S(1)} %collective-permute-done.2.rest_2_.rest_10_), channel_id=1, source_target_pairs={{0,16},{8,24},{16,32},{24,40},{32,48},{40,56},{48,0},{56,8},{64,80... | collective-permute-start | bytes 589832 | tf_op jit(solution)/shard_map/ppermute | solution.py:35
  24.0 1.4 collective-permute-done.5.rest_5_.rest_13_
  25.4 0.0 collective-permute-start.10
  25.4 5.7 %collective-permute-done.4.rest_4_.rest_12_ = bf16[384,256]{1,0:T(8,128)(2,1)S(1)} collective-permute-done((bf16[384,256]{1,0:T(8,128)(2,1)S(1)}, bf16[384,256]{1,0:T(8,128)(2,1)S(1)}, u32[]{:S(2)}, u32[]{:S(2)}) %collective-permute-start.4) | collective-permute-done | bytes 196640 | tf_op jit(solution)/shard_map/ppermute | solution.py:35
  31.2 0.1 collective-permute-start.7
  31.2 3.7 %collective-permute-done.6.rest_6_.rest_14_ = bf16[384,256]{1,0:T(8,128)(2,1)S(1)} collective-permute-done((bf16[384,256]{1,0:T(8,128)(2,1)S(1)}, bf16[384,256]{1,0:T(8,128)(2,1)S(1)}, u32[]{:S(2)}, u32[]{:S(2)}) %collective-permute-start.6) | collective-permute-done | bytes 196640 | tf_op jit(solution)/shard_map/ppermute | solution.py:35
  34.9 0.0 collective-permute-start.11
  34.9 0.0 collective-permute-done.9.rest_9_
  34.9 0.5 collective-permute-start.13
  35.4 0.1 collective-permute-start.12
  35.5 0.0 collective-permute-done.rest_1_
  35.5 0.4 collective-permute-start.14
  35.9 1.3 collective-permute-done.7.rest_7_.rest_15_
  37.2 1.4 copy.14.spans
  38.6 0.6 pad_add_fusion.ids
  39.2 0.0 collective-permute-done.11.rest_11_
  39.2 0.0 collective-permute-done.13.rest_13_
  39.2 0.0 collective-permute-done.14.rest_14_
  39.4 0.5 copy-done.17
  39.9 0.1 copy-done.18
  40.0 15.0 %forward.1 = (bf16[384,512]{1,0:T(8,128)(2,1)}, f32[2,8,768]{2,1,0:T(8,128)}) custom-call(s32[2]{0:T(128)} %pad_add_fusion.ids, s32[16,2]{1,0:T(8,128)} %copy.14.spans, bf16[384,512]{1,0:T(8,128)(2,1)} %rest_0_, bf16[384,256]{1,0:T(8,128)(2,1)} %copy-done.1, bf16[384,256]{1,0:T(8,128)(2,1)} %copy-done.2, bf16[384,256]{1,0:T(8,128)(2,1)} %copy-done.3, ...), custom_call_target="tpu_custom_call" | custom-call | flops 1000000 | bytes 1024 | tf_op jit(solution)/shard_map/forward/pallas_call | solution.py:160
  55.0 1.3 all-gather.3.cloned.1.call-done.grad_own
  56.3 0.0 collective-permute-start.17
  56.4 0.6 collective-permute-start.16
  56.9 0.6 collective-permute-start.18
  57.5 5.7 %convolution_convert_fusion.rest_2_ = bf16[384,512]{1,0:T(8,128)(2,1)} fusion(bf16[384,4096]{1,0:T(8,128)(2,1)} %all-gather.3.cloned.1.call-done.grad_own, bf16[512,4096]{1,0:T(8,128)(2,1)} %param.12), kind=kOutput, calls=%fused_computation.3 | convolution fusion | flops 1610809344 | bytes 7733248 | tf_op jit(solution)/shard_map/dot_general | solution.py:71
  63.3 0.7 copy-done.10
  64.0 6.9 %out_gradient.1 = bf16[8,512,256]{2,1,0:T(8,128)(2,1)} custom-call(s32[2]{0:T(128)} %pad_add_fusion.ids, s32[3,16]{1,0:T(4,128)} %owners.3, bf16[384,512]{1,0:T(8,128)(2,1)} %get-tuple-element.17.attn_own.rest_4_, bf16[384,512]{1,0:T(8,128)(2,1)} %copy-done.10, bf16[384,4096]{1,0:T(8,128)(2,1)} %all-gather.3.cloned.1.call-done.grad_own, ...), custom_call_target="tpu_custom_call" | custom-call | flops 8000000000 | bytes 1024 | tf_op jit(solution)/shard_map/out_gradient/pallas_call | solution.py:160
  70.9 0.0 collective-permute-done.18
  71.0 0.9 copy-done
  71.9 0.0 all-gather.5.cloned.1.call-update
  71.9 6.9 %all-to-all-start = ((bf16[8,512,256]{2,1,0:T(8,128)(2,1)}), bf16[8,512,256]{2,1,0:T(8,128)(2,1)S(1)}, u32[]{:S(2)}, u32[]{:S(2)}) async-start(bf16[8,512,256]{2,1,0:T(8,128)(2,1)} %out_gradient.1), calls=%async_computation | async-start | bytes 4194304 | tf_op jit(solution)/shard_map/all_to_all | solution.py:359
  78.8 0.1 collective-permute-start.19
  78.9 0.5 collective-permute-start.20
  79.4 1.3 collective-permute-done.20.rest_7_
  80.7 0.0 collective-permute-done.19.rest_3_
  80.7 0.6 copy-done.20
  81.3 0.8 copy-done.12
  82.1 18.4 %backward.1 = bf16[16,192,256]{2,1,0:T(8,128)(2,1)} custom-call(s32[2]{0:T(128)} %pad_add_fusion.ids, s32[16,2]{1,0:T(8,128)} %copy.14.spans, bf16[384,512]{1,0:T(8,128)(2,1)} %rest_0_, bf16[384,512]{1,0:T(8,128)(2,1)} %copy-done.9, bf16[384,512]{1,0:T(8,128)(2,1)} %convolution_convert_fusion.rest_2_, bf16[384,512]{1,0:T(8,128)(2,1)} %copy-done.12, ...), custom_call_target="tpu_custom_call" | custom-call | flops 1000000 | bytes 1024 | tf_op jit(solution)/shard_map/backward/pallas_call | solution.py:160
  100.5 4.9 %all-to-all-done = bf16[8,512,256]{2,1,0:T(8,128)(2,1)S(1)} async-done(((bf16[8,512,256]{2,1,0:T(8,128)(2,1)}), bf16[8,512,256]{2,1,0:T(8,128)(2,1)S(1)}, u32[]{:S(2)}, u32[]{:S(2)}) %all-to-all-start) | async-done | bytes 2097184 | tf_op jit(solution)/shard_map/all_to_all | solution.py:359
  105.3 27.8 %all_to_all.15 = bf16[16,192,256]{2,1,0:T(8,128)(2,1)} all-to-all(bf16[16,192,256]{2,1,0:T(8,128)(2,1)} %backward.1), channel_id=1, replica_groups={{0,16,32,48,64,80,96,112},{8,24,40,56,72,88,104,120},{1,17,33,49,65,81,..., dimensions={0} | all-to-all | bytes 3145728 | tf_op jit(solution)/shard_map/all_to_all | solution.py:359
  133.1 5.9 %kv_gradient.1 = (bf16[8,256,256]{2,1,0:T(8,128)(2,1)}, bf16[8,256,256]{2,1,0:T(8,128)(2,1)}) custom-call(s32[2]{0:T(128)} %pad_add_fusion.ids, s32[3,16]{1,0:T(4,128)} %owners.3, bf16[8,384,256]{2,1,0:T(8,128)(2,1)} %bitcast.9, bf16[384,4096]{1,0:T(8,128)(2,1)} %all-gather.5.cloned.1.call-done.hidden_ref), custom_call_target="tpu_custom_call" | custom-call | flops 1000000 | bytes 1024 | tf_op jit(solution)/shard_map/kv_gradient/pallas_call | solution.py:160
  139.1 0.0 collective-permute-start.21
  139.1 2.9 %collective-permute-done.21 = bf16[8,256,256]{2,1,0:T(8,128)(2,1)S(1)} collective-permute-done((bf16[8,256,256]{2,1,0:T(8,128)(2,1)}, bf16[8,256,256]{2,1,0:T(8,128)(2,1)S(1)}, u32[]{:S(2)}, u32[]{:S(2)}) %collective-permute-start.21) | collective-permute-done | bytes 1048608 | tf_op jit(solution)/shard_map/ppermute | solution.py:35
  141.9 2.5 %add_convert_fusion = bf16[8,256,256]{2,1,0:T(8,128)(2,1)} fusion(bf16[8,256,256]{2,1,0:T(8,128)(2,1)S(1)} %collective-permute-done.21, bf16[8,256,256]{2,1,0:T(8,128)(2,1)} %get-tuple-element.23), kind=kLoop, calls=%fused_computation.2 | loop fusion | flops 2097152 | bytes 3145728 | tf_op jit(solution)/shard_map/convert_element_type | solution.py:363
  144.4 3.6 %all-to-all-start.2 = ((bf16[8,256,256]{2,1,0:T(8,128)(2,1)}), bf16[8,256,256]{2,1,0:T(8,128)(2,1)S(1)}, u32[]{:S(2)}, u32[]{:S(2)}) async-start(bf16[8,256,256]{2,1,0:T(8,128)(2,1)} %add_convert_fusion), calls=%async_computation.2 | async-start | bytes 2097152 | tf_op jit(solution)/shard_map/all_to_all | solution.py:359
  148.0 1.1 convert_reduce_fusion
  149.1 14.7 %all-to-all-done.2 = bf16[8,256,256]{2,1,0:T(8,128)(2,1)S(1)} async-done(((bf16[8,256,256]{2,1,0:T(8,128)(2,1)}), bf16[8,256,256]{2,1,0:T(8,128)(2,1)S(1)}, u32[]{:S(2)}, u32[]{:S(2)}) %all-to-all-start.2) | async-done | bytes 1048608 | tf_op jit(solution)/shard_map/all_to_all | solution.py:359
  163.8 0.1 convert_reduce_fusion.1
  163.9 0.8 copy.15
  164.7 0.8 copy.16
  (50 shorter events, 0.2 us)
Async XLA Ops:
  7.2 49.1 %copy-start.13 = (bf16[384,512]{1,0:T(8,128)(2,1)S(1)}, bf16[384,512]{1,0:T(8,128)(2,1)}, u32[]{:S(2)}) copy-start(bf16[384,512]{1,0:T(8,128)(2,1)} %param.8) | copy-start | bytes 1179652
  7.2 49.1 %all-gather.3.cloned.1.call-start = ((), (), s32[]{:S(2)}) async-start(), calls=%async_computation.3 | async-start | bytes 3538944 | tf_op jit(solution)/shard_map/all_gather | solution.py:372
  7.9 125.2 %all-gather.5.cloned.1.call-start = ((), (), s32[]{:S(2)}) async-start(), calls=%async_computation.4 | async-start | bytes 3932160 | tf_op jit(solution)/shard_map/all_gather | solution.py:383
  9.8 29.5 %copy-start.1 = (bf16[384,256]{1,0:T(8,128)(2,1)}, bf16[384,256]{1,0:T(8,128)(2,1)S(1)}, u32[]{:S(2)}) copy-start(bf16[384,256]{1,0:T(8,128)(2,1)S(1)} %constant_dynamic-update-slice_fusion.rest_0_.rest_8_) | copy-start | bytes 589828
  9.8 8.1 %collective-permute-start.1 = (bf16[384,256]{1,0:T(8,128)(2,1)S(1)}, bf16[384,256]{1,0:T(8,128)(2,1)S(1)}, u32[]{:S(2)}, u32[]{:S(2)}) collective-permute-start(bf16[384,256]{1,0:T(8,128)(2,1)S(1)} %constant_dynamic-update-slice_fusion.rest_0_.rest_8_), channel_id=1, source_target_pairs={{0,64},{8,72},{16,80},{24,88},{32,96},{40,104},{48,112},{56,120},{... | collective-permute-start | bytes 589832 | tf_op jit(solution)/shard_map/ppermute | solution.py:35
  13.0 9.2 %collective-permute-start.2 = (bf16[384,256]{1,0:T(8,128)(2,1)S(1)}, bf16[384,256]{1,0:T(8,128)(2,1)S(1)}, u32[]{:S(2)}, u32[]{:S(2)}) collective-permute-start(bf16[384,256]{1,0:T(8,128)(2,1)S(1)} %constant_dynamic-update-slice_fusion.rest_0_.rest_8_), channel_id=1, source_target_pairs={{0,16},{8,24},{16,32},{24,40},{32,48},{40,56},{48,0},{56,8},{64,80... | collective-permute-start | bytes 589832 | tf_op jit(solution)/shard_map/ppermute | solution.py:35
  14.9 7.3 %collective-permute-start.3 = (bf16[384,256]{1,0:T(8,128)(2,1)S(1)}, bf16[384,256]{1,0:T(8,128)(2,1)S(1)}, u32[]{:S(2)}, u32[]{:S(2)}) collective-permute-start(bf16[384,256]{1,0:T(8,128)(2,1)S(1)} %constant_dynamic-update-slice_fusion.rest_0_.rest_8_), channel_id=1, source_target_pairs={{0,48},{8,56},{16,0},{24,8},{32,16},{40,24},{48,32},{56,40},{64,11... | collective-permute-start | bytes 589832 | tf_op jit(solution)/shard_map/ppermute | solution.py:35
  17.0 7.0 %collective-permute-start.8 = (bf16[384,256]{1,0:T(8,128)(2,1)S(1)}, bf16[384,256]{1,0:T(8,128)(2,1)S(1)}, u32[]{:S(2)}, u32[]{:S(2)}) collective-permute-start(bf16[384,256]{1,0:T(8,128)(2,1)S(1)} %constant_dynamic-update-slice_fusion.rest_0_.rest_8_), channel_id=1, source_target_pairs={{0,8},{8,0},{16,24},{24,16},{32,40},{40,32},{48,56},{56,48},{64,72... | collective-permute-start | bytes 589832 | tf_op jit(solution)/shard_map/ppermute | solution.py:35
  17.9 21.4 %copy-start.2 = (bf16[384,256]{1,0:T(8,128)(2,1)}, bf16[384,256]{1,0:T(8,128)(2,1)S(1)}, u32[]{:S(2)}) copy-start(bf16[384,256]{1,0:T(8,128)(2,1)S(1)} %collective-permute-done.1.rest_1_.rest_9_) | copy-start | bytes 589828
  17.9 7.5 %collective-permute-start.5 = (bf16[384,256]{1,0:T(8,128)(2,1)S(1)}, bf16[384,256]{1,0:T(8,128)(2,1)S(1)}, u32[]{:S(2)}, u32[]{:S(2)}) collective-permute-start(bf16[384,256]{1,0:T(8,128)(2,1)S(1)} %collective-permute-done.1.rest_1_.rest_9_), channel_id=1, source_target_pairs={{0,48},{8,56},{16,0},{24,8},{32,16},{40,24},{48,32},{56,40},{64,11... | collective-permute-start | bytes 589832 | tf_op jit(solution)/shard_map/ppermute | solution.py:35
  22.1 13.4 %collective-permute-start = (bf16[384,512]{1,0:T(8,128)(2,1)}, bf16[384,512]{1,0:T(8,128)(2,1)S(1)}, u32[]{:S(2)}, u32[]{:S(2)}) collective-permute-start(bf16[384,512]{1,0:T(8,128)(2,1)} %rest_0_), channel_id=1, source_target_pairs={{0,8},{8,0},{16,24},{24,16},{32,40},{40,32},{48,56},{56,48},{64,72... | collective-permute-start | bytes 1179656 | tf_op jit(solution)/shard_map/ppermute | solution.py:35
  22.2 17.1 %copy-start.3 = (bf16[384,256]{1,0:T(8,128)(2,1)}, bf16[384,256]{1,0:T(8,128)(2,1)S(1)}, u32[]{:S(2)}) copy-start(bf16[384,256]{1,0:T(8,128)(2,1)S(1)} %collective-permute-done.2.rest_2_.rest_10_) | copy-start | bytes 589828
  22.2 9.0 %collective-permute-start.4 = (bf16[384,256]{1,0:T(8,128)(2,1)S(1)}, bf16[384,256]{1,0:T(8,128)(2,1)S(1)}, u32[]{:S(2)}, u32[]{:S(2)}) collective-permute-start(bf16[384,256]{1,0:T(8,128)(2,1)S(1)} %collective-permute-done.1.rest_1_.rest_9_), channel_id=1, source_target_pairs={{0,16},{8,24},{16,32},{24,40},{32,48},{40,56},{48,0},{56,8},{64,80... | collective-permute-start | bytes 589832 | tf_op jit(solution)/shard_map/ppermute | solution.py:35
  22.3 17.0 %copy-start.4 = (bf16[384,256]{1,0:T(8,128)(2,1)}, bf16[384,256]{1,0:T(8,128)(2,1)S(1)}, u32[]{:S(2)}) copy-start(bf16[384,256]{1,0:T(8,128)(2,1)S(1)} %collective-permute-done.3.rest_3_.rest_11_) | copy-start | bytes 589828
  22.3 12.6 %collective-permute-start.6 = (bf16[384,256]{1,0:T(8,128)(2,1)S(1)}, bf16[384,256]{1,0:T(8,128)(2,1)S(1)}, u32[]{:S(2)}, u32[]{:S(2)}) collective-permute-start(bf16[384,256]{1,0:T(8,128)(2,1)S(1)} %collective-permute-done.2.rest_2_.rest_10_), channel_id=1, source_target_pairs={{0,16},{8,24},{16,32},{24,40},{32,48},{40,56},{48,0},{56,8},{64,80... | collective-permute-start | bytes 589832 | tf_op jit(solution)/shard_map/ppermute | solution.py:35
  24.0 15.3 %copy-start.14 = (bf16[384,256]{1,0:T(8,128)(2,1)}, bf16[384,256]{1,0:T(8,128)(2,1)S(1)}, u32[]{:S(2)}) copy-start(bf16[384,256]{1,0:T(8,128)(2,1)S(1)} %collective-permute-done.8.rest_8_) | copy-start | bytes 589828
  24.0 10.9 %collective-permute-start.9 = (bf16[384,256]{1,0:T(8,128)(2,1)S(1)}, bf16[384,256]{1,0:T(8,128)(2,1)S(1)}, u32[]{:S(2)}, u32[]{:S(2)}) collective-permute-start(bf16[384,256]{1,0:T(8,128)(2,1)S(1)} %collective-permute-done.1.rest_1_.rest_9_), channel_id=1, source_target_pairs={{0,8},{8,0},{16,24},{24,16},{32,40},{40,32},{48,56},{56,48},{64,72... | collective-permute-start | bytes 589832 | tf_op jit(solution)/shard_map/ppermute | solution.py:35
  25.4 13.9 %copy-start.5 = (bf16[384,256]{1,0:T(8,128)(2,1)}, bf16[384,256]{1,0:T(8,128)(2,1)S(1)}, u32[]{:S(2)}) copy-start(bf16[384,256]{1,0:T(8,128)(2,1)S(1)} %collective-permute-done.5.rest_5_.rest_13_) | copy-start | bytes 589828
  25.4 10.0 %collective-permute-start.10 = (bf16[384,256]{1,0:T(8,128)(2,1)S(1)}, bf16[384,256]{1,0:T(8,128)(2,1)S(1)}, u32[]{:S(2)}, u32[]{:S(2)}) collective-permute-start(bf16[384,256]{1,0:T(8,128)(2,1)S(1)} %collective-permute-done.2.rest_2_.rest_10_), channel_id=1, source_target_pairs={{0,8},{8,0},{16,24},{24,16},{32,40},{40,32},{48,56},{56,48},{64,72... | collective-permute-start | bytes 589832 | tf_op jit(solution)/shard_map/ppermute | solution.py:35
  31.1 8.2 %copy-start.6 = (bf16[384,256]{1,0:T(8,128)(2,1)}, bf16[384,256]{1,0:T(8,128)(2,1)S(1)}, u32[]{:S(2)}) copy-start(bf16[384,256]{1,0:T(8,128)(2,1)S(1)} %collective-permute-done.4.rest_4_.rest_12_) | copy-start | bytes 589828
  31.2 6.1 %collective-permute-start.7 = (bf16[384,256]{1,0:T(8,128)(2,1)S(1)}, bf16[384,256]{1,0:T(8,128)(2,1)S(1)}, u32[]{:S(2)}, u32[]{:S(2)}) collective-permute-start(bf16[384,256]{1,0:T(8,128)(2,1)S(1)} %collective-permute-done.5.rest_5_.rest_13_), channel_id=1, source_target_pairs={{0,48},{8,56},{16,0},{24,8},{32,16},{40,24},{48,32},{56,40},{64,11... | collective-permute-start | bytes 589832 | tf_op jit(solution)/shard_map/ppermute | solution.py:35
  34.9 4.4 %copy-start.7 = (bf16[384,256]{1,0:T(8,128)(2,1)}, bf16[384,256]{1,0:T(8,128)(2,1)S(1)}, u32[]{:S(2)}) copy-start(bf16[384,256]{1,0:T(8,128)(2,1)S(1)} %collective-permute-done.6.rest_6_.rest_14_) | copy-start | bytes 589828
  34.9 4.3 %collective-permute-start.11 = (bf16[384,256]{1,0:T(8,128)(2,1)S(1)}, bf16[384,256]{1,0:T(8,128)(2,1)S(1)}, u32[]{:S(2)}, u32[]{:S(2)}) collective-permute-start(bf16[384,256]{1,0:T(8,128)(2,1)S(1)} %collective-permute-done.3.rest_3_.rest_11_), channel_id=1, source_target_pairs={{0,8},{8,0},{16,24},{24,16},{32,40},{40,32},{48,56},{56,48},{64,72... | collective-permute-start | bytes 589832 | tf_op jit(solution)/shard_map/ppermute | solution.py:35
  34.9 4.4 %copy-start.15 = (bf16[384,256]{1,0:T(8,128)(2,1)}, bf16[384,256]{1,0:T(8,128)(2,1)S(1)}, u32[]{:S(2)}) copy-start(bf16[384,256]{1,0:T(8,128)(2,1)S(1)} %collective-permute-done.9.rest_9_) | copy-start | bytes 589828
  34.9 4.3 %collective-permute-start.13 = (bf16[384,256]{1,0:T(8,128)(2,1)S(1)}, bf16[384,256]{1,0:T(8,128)(2,1)S(1)}, u32[]{:S(2)}, u32[]{:S(2)}) collective-permute-start(bf16[384,256]{1,0:T(8,128)(2,1)S(1)} %collective-permute-done.5.rest_5_.rest_13_), channel_id=1, source_target_pairs={{0,8},{8,0},{16,24},{24,16},{32,40},{40,32},{48,56},{56,48},{64,72... | collective-permute-start | bytes 589832 | tf_op jit(solution)/shard_map/ppermute | solution.py:35
  35.4 3.9 %copy-start.16 = (bf16[384,256]{1,0:T(8,128)(2,1)}, bf16[384,256]{1,0:T(8,128)(2,1)S(1)}, u32[]{:S(2)}) copy-start(bf16[384,256]{1,0:T(8,128)(2,1)S(1)} %collective-permute-done.10.rest_10_) | copy-start | bytes 589828
  35.4 3.8 %collective-permute-start.12 = (bf16[384,256]{1,0:T(8,128)(2,1)S(1)}, bf16[384,256]{1,0:T(8,128)(2,1)}, u32[]{:S(2)}, u32[]{:S(2)}) collective-permute-start(bf16[384,256]{1,0:T(8,128)(2,1)S(1)} %collective-permute-done.4.rest_4_.rest_12_), channel_id=1, source_target_pairs={{0,8},{8,0},{16,24},{24,16},{32,40},{40,32},{48,56},{56,48},{64,72... | collective-permute-start | bytes 589832 | tf_op jit(solution)/shard_map/ppermute | solution.py:35
  35.5 35.4 %copy-start.9 = (bf16[384,512]{1,0:T(8,128)(2,1)}, bf16[384,512]{1,0:T(8,128)(2,1)S(1)}, u32[]{:S(2)}) copy-start(bf16[384,512]{1,0:T(8,128)(2,1)S(1)} %collective-permute-done.rest_1_) | copy-start | bytes 1179652
  35.5 3.7 %collective-permute-start.14 = (bf16[384,256]{1,0:T(8,128)(2,1)S(1)}, bf16[384,256]{1,0:T(8,128)(2,1)}, u32[]{:S(2)}, u32[]{:S(2)}) collective-permute-start(bf16[384,256]{1,0:T(8,128)(2,1)S(1)} %collective-permute-done.6.rest_6_.rest_14_), channel_id=1, source_target_pairs={{0,8},{8,0},{16,24},{24,16},{32,40},{40,32},{48,56},{56,48},{64,72... | collective-permute-start | bytes 589832 | tf_op jit(solution)/shard_map/ppermute | solution.py:35
  37.2 2.1 %copy-start.8 = (bf16[384,256]{1,0:T(8,128)(2,1)}, bf16[384,256]{1,0:T(8,128)(2,1)S(1)}, u32[]{:S(2)}) copy-start(bf16[384,256]{1,0:T(8,128)(2,1)S(1)} %collective-permute-done.7.rest_7_.rest_15_) | copy-start | bytes 589828
  37.2 2.0 %collective-permute-start.15 = (bf16[384,256]{1,0:T(8,128)(2,1)S(1)}, bf16[384,256]{1,0:T(8,128)(2,1)}, u32[]{:S(2)}, u32[]{:S(2)}) collective-permute-start(bf16[384,256]{1,0:T(8,128)(2,1)S(1)} %collective-permute-done.7.rest_7_.rest_15_), channel_id=1, source_target_pairs={{0,8},{8,0},{16,24},{24,16},{32,40},{40,32},{48,56},{56,48},{64,72... | collective-permute-start | bytes 589832 | tf_op jit(solution)/shard_map/ppermute | solution.py:35
  39.2 0.7 copy-start.17
  39.2 0.7 copy-start.18
  56.3 7.0 %collective-permute-start.17 = (bf16[384,4096]{1,0:T(8,128)(2,1)}, bf16[384,4096]{1,0:T(8,128)(2,1)}, u32[]{:S(2)}, u32[]{:S(2)}) collective-permute-start(bf16[384,4096]{1,0:T(8,128)(2,1)} %all-gather.3.cloned.1.call-done.grad_own), channel_id=1, source_target_pairs={{0,8},{8,0},{16,24},{24,16},{32,40},{40,32},{48,56},{56,48},{64,72... | collective-permute-start | bytes 9437192 | tf_op jit(solution)/shard_map/ppermute | solution.py:35
  56.4 6.9 %collective-permute-start.16 = (bf16[384,512]{1,0:T(8,128)(2,1)}, bf16[384,512]{1,0:T(8,128)(2,1)S(1)}, u32[]{:S(2)}, u32[]{:S(2)}) collective-permute-start(bf16[384,512]{1,0:T(8,128)(2,1)} %get-tuple-element.17.attn_own.rest_4_), channel_id=1, source_target_pairs={{0,8},{8,0},{16,24},{24,16},{32,40},{40,32},{48,56},{56,48},{64,72... | collective-permute-start | bytes 1179656 | tf_op jit(solution)/shard_map/ppermute | solution.py:35
  56.9 14.0 %collective-permute-start.18 = (bf16[384,512]{1,0:T(8,128)(2,1)S(1)}, bf16[384,512]{1,0:T(8,128)(2,1)S(1)}, u32[]{:S(2)}, u32[]{:S(2)}) collective-permute-start(bf16[384,512]{1,0:T(8,128)(2,1)S(1)} %copy-done.13), channel_id=1, source_target_pairs={{0,4},{1,5},{2,6},{3,7},{4,0},{5,1},{6,2},{7,3},{8,12},{9,13},{10,... | collective-permute-start | bytes 1179656 | tf_op jit(solution)/shard_map/ppermute | solution.py:58
  63.3 0.7 copy-start.10
  70.9 7.9 %copy-start.11 = (bf16[384,512]{1,0:T(8,128)(2,1)S(1)}, bf16[384,512]{1,0:T(8,128)(2,1)}, u32[]{:S(2)}) copy-start(bf16[384,512]{1,0:T(8,128)(2,1)} %convolution_convert_fusion.rest_2_) | copy-start | bytes 1179652
  70.9 8.0 %copy-start.19 = (f32[2,8,768]{2,1,0:T(8,128)S(1)}, f32[2,8,768]{2,1,0:T(8,128)}, u32[]{:S(2)}) copy-start(f32[2,8,768]{2,1,0:T(8,128)} %get-tuple-element.21.rest_6_) | copy-start | bytes 147460
  71.0 0.9 copy-start
  71.9 33.4 %all-to-all-start = ((bf16[8,512,256]{2,1,0:T(8,128)(2,1)}), bf16[8,512,256]{2,1,0:T(8,128)(2,1)S(1)}, u32[]{:S(2)}, u32[]{:S(2)}) async-start(bf16[8,512,256]{2,1,0:T(8,128)(2,1)} %out_gradient.1), calls=%async_computation | async-start | bytes 4194304 | tf_op jit(solution)/shard_map/all_to_all | solution.py:359
  78.8 1.9 %collective-permute-start.19 = (bf16[384,512]{1,0:T(8,128)(2,1)S(1)}, bf16[384,512]{1,0:T(8,128)(2,1)S(1)}, u32[]{:S(2)}, u32[]{:S(2)}) collective-permute-start(bf16[384,512]{1,0:T(8,128)(2,1)S(1)} %copy-done.11), channel_id=1, source_target_pairs={{0,8},{8,0},{16,24},{24,16},{32,40},{40,32},{48,56},{56,48},{64,72... | collective-permute-start | bytes 1179656 | tf_op jit(solution)/shard_map/ppermute | solution.py:35
  78.9 1.8 %collective-permute-start.20 = (f32[2,8,768]{2,1,0:T(8,128)S(1)}, f32[2,8,768]{2,1,0:T(8,128)S(1)}, u32[]{:S(2)}, u32[]{:S(2)}) collective-permute-start(f32[2,8,768]{2,1,0:T(8,128)S(1)} %copy-done.19), channel_id=1, source_target_pairs={{0,8},{8,0},{16,24},{24,16},{32,40},{40,32},{48,56},{56,48},{64,72... | collective-permute-start | bytes 147464 | tf_op jit(solution)/shard_map/ppermute | solution.py:35
  80.7 0.6 copy-start.20
  81.3 0.8 copy-start.12
  139.1 2.9 %collective-permute-start.21 = (bf16[8,256,256]{2,1,0:T(8,128)(2,1)}, bf16[8,256,256]{2,1,0:T(8,128)(2,1)S(1)}, u32[]{:S(2)}, u32[]{:S(2)}) collective-permute-start(bf16[8,256,256]{2,1,0:T(8,128)(2,1)} %get-tuple-element.24), channel_id=1, source_target_pairs={{0,8},{8,0},{16,24},{24,16},{32,40},{40,32},{48,56},{56,48},{64,72... | collective-permute-start | bytes 3145736 | tf_op jit(solution)/shard_map/ppermute | solution.py:35
  144.4 19.3 %all-to-all-start.2 = ((bf16[8,256,256]{2,1,0:T(8,128)(2,1)}), bf16[8,256,256]{2,1,0:T(8,128)(2,1)S(1)}, u32[]{:S(2)}, u32[]{:S(2)}) async-start(bf16[8,256,256]{2,1,0:T(8,128)(2,1)} %add_convert_fusion), calls=%async_computation.2 | async-start | bytes 2097152 | tf_op jit(solution)/shard_map/all_to_all | solution.py:359
Sparse Core Ops, SparseCore 0:
  9.7 46.6 all-gather.2
  72.0 39.9 all-gather.4

commit v6 on v5

--- a/solution.py
+++ b/solution.py
@@ -25,6 +25,7 @@
 F32 = jnp.float32
 BF16 = jnp.bfloat16
 VMEM_BYTES = 58 * 1024 * 1024
+SMALL_VMEM_BYTES = 20 * 1024 * 1024
 
 
 def ctx_move(value, dx, dz, dc):
@@ -156,14 +157,14 @@
     return pl.BlockSpec(memory_space=pltpu.VMEM)
 
 
-def call(kernel, inputs, outputs, scratch, flops, name):
+def call(kernel, inputs, outputs, scratch, flops, name, vmem_bytes=VMEM_BYTES):
     return pl.pallas_call(
         kernel,
         out_shape=outputs,
         in_specs=[smem(), smem()] + [vmem()] * (len(inputs) - 2),
         out_specs=(vmem(),) * len(outputs),
         scratch_shapes=scratch,
-        compiler_params=pltpu.CompilerParams(vmem_limit_bytes=VMEM_BYTES),
+        compiler_params=pltpu.CompilerParams(vmem_limit_bytes=vmem_bytes),
         cost_estimate=pl.CostEstimate(flops=flops, bytes_accessed=1024, transcendentals=0),
         name=name,
     )(*inputs)
@@ -316,6 +317,7 @@
         [pltpu.SMEM((N_CTX,), jnp.int32)],
         OUT_FLOPS,
         "out_gradient",
+        SMALL_VMEM_BYTES,
     )
     return parts
 
@@ -349,6 +351,7 @@
         [found, found],
         1_000_000,
         "kv_gradient",
+        SMALL_VMEM_BYTES,
     )
 
 

time: 173 us -> 167 us (0.965)
  Pallas kernels: 46.2 us -> 40.5 us
    pallas_call x4, Pallas kernels: 46.2 us -> 40.5 us  [call(): pl.pallas_call(kernel, out_shape=outputs, in_specs=[smem(), smem()] + [vm...]
    unnamed x47 -> x61, local copies, waits for them, and re-layouts: 7.55 us -> 8.69 us
  transfers between devices with their start and end apart: 26 -> 26, of which waited for: 10 -> 12; matrix products, arithmetic and copies ran while one was open for 6% -> 7% of each run, Pallas kernels for 23% -> 22%
where the time goes in v6:
time: 167 us
  Pallas kernels  40.5 us (24%)
  waiting for transfers between devices  38.1 us (23%)
  blocking collectives  27.7 us (17%)
  starting transfers between devices  26.4 us (16%)
  between operations  14.4 us (9%)
  local copies, waits for them, and re-layouts  9.66 us (6%)
  matrix products  4.97 us (3%)
  other arithmetic  4.78 us (3%)
    pallas_call x4, Pallas kernels, call(): pl.pallas_call(kernel, out_shape=outputs, in_specs=[smem(), smem()] + [vm...  40.5 us
    all_to_all x1, blocking collectives, exchange(): lax.all_to_all(parts, 'ctx', 0, 0, tiled=True, axis_index_groups=SAME_CORE)  27.7 us
    all_to_all x2, waiting for transfers between devices, exchange(): lax.all_to_all(parts, 'ctx', 0, 0, tiled=True, axis_index_groups=SAME_CORE)  17.9 us
    ppermute x21, waiting for transfers between devices, ctx_move(): return lax.ppermute(value, 'ctx', pairs)  17.1 us
    ppermute x21, starting transfers between devices, ctx_move(): return lax.ppermute(value, 'ctx', pairs)  15.6 us
    all_to_all x2, starting transfers between devices, exchange(): lax.all_to_all(parts, 'ctx', 0, 0, tiled=True, axis_index_groups=SAME_CORE)  10.1 us
    unnamed x61, local copies, waits for them, and re-layouts  8.69 us
    dot_general x1, matrix products, nt(): lax.dot_general(a, b, (((1,), (1,)), ((), ())), preferred_element_type=F32)  4.97 us
  transfers between devices with their start and end apart: 26, of which 12 were waited for; matrix products, arithmetic and copies ran while one was open for 7% of the time, Pallas kernels for 22%

profile of v6, /device:TPU:0, one launch (start us, length us, event | category | flops | bytes accessed | tf_op | source)
XLA Modules:
  0.0 166.5 jit_solution(10973551311630684036)
XLA Ops:
  7.2 0.0 all-gather.3.cloned.1.call-start
  7.2 0.7 all-gather.3.cloned.1.call-update
  7.9 0.0 all-gather.5.cloned.1.call-start
  8.0 0.9 constant_dynamic-update-slice_fusion.1
  8.9 0.9 constant_dynamic-update-slice_fusion.rest_0_.rest_8_
  9.8 3.2 %collective-permute-start.1 = (bf16[384,256]{1,0:T(8,128)(2,1)S(1)}, bf16[384,256]{1,0:T(8,128)(2,1)S(1)}, u32[]{:S(2)}, u32[]{:S(2)}) collective-permute-start(bf16[384,256]{1,0:T(8,128)(2,1)S(1)} %constant_dynamic-update-slice_fusion.rest_0_.rest_8_), channel_id=1, source_target_pairs={{0,64},{8,72},{16,80},{24,88},{32,96},{40,104},{48,112},{56,120},{... | collective-permute-start | bytes 589832 | tf_op jit(solution)/shard_map/ppermute | solution.py:36
  13.0 1.9 %collective-permute-start.2 = (bf16[384,256]{1,0:T(8,128)(2,1)S(1)}, bf16[384,256]{1,0:T(8,128)(2,1)S(1)}, u32[]{:S(2)}, u32[]{:S(2)}) collective-permute-start(bf16[384,256]{1,0:T(8,128)(2,1)S(1)} %constant_dynamic-update-slice_fusion.rest_0_.rest_8_), channel_id=1, source_target_pairs={{0,16},{8,24},{16,32},{24,40},{32,48},{40,56},{48,0},{56,8},{64,80... | collective-permute-start | bytes 589832 | tf_op jit(solution)/shard_map/ppermute | solution.py:36
  14.9 2.1 %collective-permute-start.3 = (bf16[384,256]{1,0:T(8,128)(2,1)S(1)}, bf16[384,256]{1,0:T(8,128)(2,1)S(1)}, u32[]{:S(2)}, u32[]{:S(2)}) collective-permute-start(bf16[384,256]{1,0:T(8,128)(2,1)S(1)} %constant_dynamic-update-slice_fusion.rest_0_.rest_8_), channel_id=1, source_target_pairs={{0,48},{8,56},{16,0},{24,8},{32,16},{40,24},{48,32},{56,40},{64,11... | collective-permute-start | bytes 589832 | tf_op jit(solution)/shard_map/ppermute | solution.py:36
  17.0 0.0 collective-permute-start.8
  17.0 0.9 collective-permute-done.1.rest_1_.rest_9_
  17.9 4.3 %collective-permute-start.5 = (bf16[384,256]{1,0:T(8,128)(2,1)S(1)}, bf16[384,256]{1,0:T(8,128)(2,1)S(1)}, u32[]{:S(2)}, u32[]{:S(2)}) collective-permute-start(bf16[384,256]{1,0:T(8,128)(2,1)S(1)} %collective-permute-done.1.rest_1_.rest_9_), channel_id=1, source_target_pairs={{0,48},{8,56},{16,0},{24,8},{32,16},{40,24},{48,32},{56,40},{64,11... | collective-permute-start | bytes 589832 | tf_op jit(solution)/shard_map/ppermute | solution.py:36
  22.2 0.0 collective-permute-done.2.rest_2_.rest_10_
  22.2 0.1 collective-permute-start.4
  22.2 0.0 collective-permute-done.3.rest_3_.rest_11_
  22.3 1.7 %collective-permute-start.6 = (bf16[384,256]{1,0:T(8,128)(2,1)S(1)}, bf16[384,256]{1,0:T(8,128)(2,1)S(1)}, u32[]{:S(2)}, u32[]{:S(2)}) collective-permute-start(bf16[384,256]{1,0:T(8,128)(2,1)S(1)} %collective-permute-done.2.rest_2_.rest_10_), channel_id=1, source_target_pairs={{0,16},{8,24},{16,32},{24,40},{32,48},{40,56},{48,0},{56,8},{64,80... | collective-permute-start | bytes 589832 | tf_op jit(solution)/shard_map/ppermute | solution.py:36
  24.0 1.4 collective-permute-done.5.rest_5_.rest_13_
  25.4 0.0 collective-permute-start.10
  25.4 5.7 %collective-permute-done.4.rest_4_.rest_12_ = bf16[384,256]{1,0:T(8,128)(2,1)S(1)} collective-permute-done((bf16[384,256]{1,0:T(8,128)(2,1)S(1)}, bf16[384,256]{1,0:T(8,128)(2,1)S(1)}, u32[]{:S(2)}, u32[]{:S(2)}) %collective-permute-start.4) | collective-permute-done | bytes 196640 | tf_op jit(solution)/shard_map/ppermute | solution.py:36
  31.2 0.1 collective-permute-start.7
  31.2 3.7 %collective-permute-done.6.rest_6_.rest_14_ = bf16[384,256]{1,0:T(8,128)(2,1)S(1)} collective-permute-done((bf16[384,256]{1,0:T(8,128)(2,1)S(1)}, bf16[384,256]{1,0:T(8,128)(2,1)S(1)}, u32[]{:S(2)}, u32[]{:S(2)}) %collective-permute-start.6) | collective-permute-done | bytes 196640 | tf_op jit(solution)/shard_map/ppermute | solution.py:36
  34.9 0.0 collective-permute-start.11
  34.9 0.5 collective-permute-start.13
  35.4 0.1 collective-permute-start.12
  35.5 0.0 collective-permute-done.rest_1_
  35.5 0.4 collective-permute-start.14
  35.9 1.3 collective-permute-done.7.rest_7_.rest_15_
  37.2 1.4 copy.14.spans
  38.6 0.6 pad_add_fusion.ids
  39.3 0.0 collective-permute-done.12.rest_12_
  39.3 0.0 collective-permute-done.15.rest_15_
  39.4 0.5 copy-done.23
  39.9 0.1 copy-done.24
  40.0 0.1 copy-done.25
  40.0 15.0 %forward.1 = (bf16[384,512]{1,0:T(8,128)(2,1)}, f32[2,8,768]{2,1,0:T(8,128)}) custom-call(s32[2]{0:T(128)} %pad_add_fusion.ids, s32[16,2]{1,0:T(8,128)} %copy.14.spans, bf16[384,512]{1,0:T(8,128)(2,1)} %rest_0_, bf16[384,256]{1,0:T(8,128)(2,1)} %copy-done.8, bf16[384,256]{1,0:T(8,128)(2,1)} %copy-done.9, bf16[384,256]{1,0:T(8,128)(2,1)} %copy-done.10, ...), custom_call_target="tpu_custom_call" | custom-call | flops 1000000 | bytes 1024 | tf_op jit(solution)/shard_map/forward/pallas_call | solution.py:161
  55.1 1.2 all-gather.3.cloned.1.call-done.grad_own
  56.4 0.0 copy-start.5
  56.4 0.6 collective-permute-start.16
  57.0 0.6 collective-permute-start.18
  57.6 5.0 %convolution_convert_fusion.rest_2_ = bf16[384,512]{1,0:T(8,128)(2,1)S(1)} fusion(bf16[384,4096]{1,0:T(8,128)(2,1)} %all-gather.3.cloned.1.call-done.grad_own, bf16[512,4096]{1,0:T(8,128)(2,1)} %param.12), kind=kOutput, calls=%fused_computation.3 | convolution fusion | flops 1610809344 | bytes 7733248 | tf_op jit(solution)/shard_map/dot_general | solution.py:72
  62.6 0.2 collective-permute-done.16.attn_other.rest_5_
  62.8 4.3 %out_gradient.1 = bf16[8,512,256]{2,1,0:T(8,128)(2,1)} custom-call(s32[2]{0:T(128)S(1)} %copy-done.3, s32[3,16]{1,0:T(4,128)S(1)} %copy-done.5, bf16[384,512]{1,0:T(8,128)(2,1)S(1)} %copy-done.1, bf16[384,512]{1,0:T(8,128)(2,1)S(1)} %collective-permute-done.16.attn_other.rest_5_, bf16[384,4096]{1,0:T(8,128)(2,1)S(1)} %copy-done.6, ...), custom_call_target="tpu_custom_call" | custom-call | flops 8000000000 | bytes 1024 | tf_op jit(solution)/shard_map/out_gradient/pallas_call | solution.py:161
  67.1 1.2 collective-permute-done.18
  68.3 0.9 copy-done.7
  69.2 0.0 all-gather.5.cloned.1.call-update
  69.2 6.6 %all-to-all-start = ((bf16[8,512,256]{2,1,0:T(8,128)(2,1)}), bf16[8,512,256]{2,1,0:T(8,128)(2,1)}, u32[]{:S(2)}, u32[]{:S(2)}) async-start(bf16[8,512,256]{2,1,0:T(8,128)(2,1)} %out_gradient.1), calls=%async_computation | async-start | bytes 4194304 | tf_op jit(solution)/shard_map/all_to_all | solution.py:362
  75.8 0.1 collective-permute-start.19
  75.9 0.5 collective-permute-start.20
  76.4 1.3 collective-permute-done.20.rest_7_
  77.7 0.6 copy-done.27
  78.3 0.7 copy-done.18
  79.0 18.1 %backward.1 = bf16[16,192,256]{2,1,0:T(8,128)(2,1)} custom-call(s32[2]{0:T(128)} %pad_add_fusion.ids, s32[16,2]{1,0:T(8,128)} %copy.14.spans, bf16[384,512]{1,0:T(8,128)(2,1)} %rest_0_, bf16[384,512]{1,0:T(8,128)(2,1)} %copy-done.16, bf16[384,512]{1,0:T(8,128)(2,1)} %copy-done.17, bf16[384,512]{1,0:T(8,128)(2,1)} %copy-done.18, ...), custom_call_target="tpu_custom_call" | custom-call | flops 1000000 | bytes 1024 | tf_op jit(solution)/shard_map/backward/pallas_call | solution.py:161
  97.1 4.8 %all-to-all-done = bf16[8,512,256]{2,1,0:T(8,128)(2,1)} async-done(((bf16[8,512,256]{2,1,0:T(8,128)(2,1)}), bf16[8,512,256]{2,1,0:T(8,128)(2,1)}, u32[]{:S(2)}, u32[]{:S(2)}) %all-to-all-start) | async-done | bytes 2097184 | tf_op jit(solution)/shard_map/all_to_all | solution.py:362
  101.9 27.7 %all_to_all.15 = bf16[16,192,256]{2,1,0:T(8,128)(2,1)S(1)} all-to-all(bf16[16,192,256]{2,1,0:T(8,128)(2,1)} %backward.1), channel_id=1, replica_groups={{0,16,32,48,64,80,96,112},{8,24,40,56,72,88,104,120},{1,17,33,49,65,81,..., dimensions={0} | all-to-all | bytes 3145728 | tf_op jit(solution)/shard_map/all_to_all | solution.py:362
  129.6 1.9 %copy-done = bf16[384,4096]{1,0:T(8,128)(2,1)S(1)} copy-done((bf16[384,4096]{1,0:T(8,128)(2,1)S(1)}, bf16[384,4096]{1,0:T(8,128)(2,1)}, u32[]{:S(2)}) %copy-start) | copy-done | bytes 3145752
  131.5 3.1 %kv_gradient.1 = (bf16[8,256,256]{2,1,0:T(8,128)(2,1)S(1)}, bf16[8,256,256]{2,1,0:T(8,128)(2,1)S(1)}) custom-call(s32[2]{0:T(128)S(1)} %copy-done.4, s32[3,16]{1,0:T(4,128)S(1)} %copy-done.5, bf16[8,384,256]{2,1,0:T(8,128)(2,1)S(1)} %bitcast.9, bf16[384,4096]{1,0:T(8,128)(2,1)S(1)} %copy-done), custom_call_target="tpu_custom_call" | custom-call | flops 1000000 | bytes 1024 | tf_op jit(solution)/shard_map/kv_gradient/pallas_call | solution.py:161
  134.6 0.1 collective-permute-start.21
  134.7 2.6 %collective-permute-done.21 = bf16[8,256,256]{2,1,0:T(8,128)(2,1)S(1)} collective-permute-done((bf16[8,256,256]{2,1,0:T(8,128)(2,1)S(1)}, bf16[8,256,256]{2,1,0:T(8,128)(2,1)S(1)}, u32[]{:S(2)}, u32[]{:S(2)}) %collective-permute-start.21) | collective-permute-done | bytes 1048608 | tf_op jit(solution)/shard_map/ppermute | solution.py:36
  137.4 1.3 add_convert_fusion
  138.7 3.6 %all-to-all-start.2 = ((bf16[8,256,256]{2,1,0:T(8,128)(2,1)}), bf16[8,256,256]{2,1,0:T(8,128)(2,1)S(1)}, u32[]{:S(2)}, u32[]{:S(2)}) async-start(bf16[8,256,256]{2,1,0:T(8,128)(2,1)} %add_convert_fusion), calls=%async_computation.2 | async-start | bytes 2097152 | tf_op jit(solution)/shard_map/all_to_all | solution.py:362
  142.2 2.7 %convert_reduce_fusion = f32[512,256]{1,0:T(8,128)} fusion(bf16[8,512,256]{2,1,0:T(8,128)(2,1)} %all-to-all-done), kind=kLoop, calls=%fused_computation | loop fusion | flops 1966080 | bytes 2621440 | tf_op jit(solution)/shard_map/reduce_sum | solution.py:394
  144.9 13.0 %all-to-all-done.2 = bf16[8,256,256]{2,1,0:T(8,128)(2,1)S(1)} async-done(((bf16[8,256,256]{2,1,0:T(8,128)(2,1)}), bf16[8,256,256]{2,1,0:T(8,128)(2,1)S(1)}, u32[]{:S(2)}, u32[]{:S(2)}) %all-to-all-start.2) | async-done | bytes 1048608 | tf_op jit(solution)/shard_map/all_to_all | solution.py:362
  158.0 0.1 convert_reduce_fusion.1
  158.2 0.8 copy.15
  158.9 0.8 copy.16
  (64 shorter events, 0.2 us)
Async XLA Ops:
  7.2 49.1 %copy-start.19 = (bf16[384,512]{1,0:T(8,128)(2,1)S(1)}, bf16[384,512]{1,0:T(8,128)(2,1)}, u32[]{:S(2)}) copy-start(bf16[384,512]{1,0:T(8,128)(2,1)} %param.8) | copy-start | bytes 1179652
  7.2 49.1 %all-gather.3.cloned.1.call-start = ((), (), s32[]{:S(2)}) async-start(), calls=%async_computation.3 | async-start | bytes 3538944 | tf_op jit(solution)/shard_map/all_gather | solution.py:375
  7.9 121.7 %all-gather.5.cloned.1.call-start = ((), (), s32[]{:S(2)}) async-start(), calls=%async_computation.4 | async-start | bytes 3932160 | tf_op jit(solution)/shard_map/all_gather | solution.py:386
  9.8 29.5 %copy-start.8 = (bf16[384,256]{1,0:T(8,128)(2,1)}, bf16[384,256]{1,0:T(8,128)(2,1)S(1)}, u32[]{:S(2)}) copy-start(bf16[384,256]{1,0:T(8,128)(2,1)S(1)} %constant_dynamic-update-slice_fusion.rest_0_.rest_8_) | copy-start | bytes 589828
  9.8 8.1 %collective-permute-start.1 = (bf16[384,256]{1,0:T(8,128)(2,1)S(1)}, bf16[384,256]{1,0:T(8,128)(2,1)S(1)}, u32[]{:S(2)}, u32[]{:S(2)}) collective-permute-start(bf16[384,256]{1,0:T(8,128)(2,1)S(1)} %constant_dynamic-update-slice_fusion.rest_0_.rest_8_), channel_id=1, source_target_pairs={{0,64},{8,72},{16,80},{24,88},{32,96},{40,104},{48,112},{56,120},{... | collective-permute-start | bytes 589832 | tf_op jit(solution)/shard_map/ppermute | solution.py:36
  13.0 9.2 %collective-permute-start.2 = (bf16[384,256]{1,0:T(8,128)(2,1)S(1)}, bf16[384,256]{1,0:T(8,128)(2,1)S(1)}, u32[]{:S(2)}, u32[]{:S(2)}) collective-permute-start(bf16[384,256]{1,0:T(8,128)(2,1)S(1)} %constant_dynamic-update-slice_fusion.rest_0_.rest_8_), channel_id=1, source_target_pairs={{0,16},{8,24},{16,32},{24,40},{32,48},{40,56},{48,0},{56,8},{64,80... | collective-permute-start | bytes 589832 | tf_op jit(solution)/shard_map/ppermute | solution.py:36
  14.9 7.3 %collective-permute-start.3 = (bf16[384,256]{1,0:T(8,128)(2,1)S(1)}, bf16[384,256]{1,0:T(8,128)(2,1)S(1)}, u32[]{:S(2)}, u32[]{:S(2)}) collective-permute-start(bf16[384,256]{1,0:T(8,128)(2,1)S(1)} %constant_dynamic-update-slice_fusion.rest_0_.rest_8_), channel_id=1, source_target_pairs={{0,48},{8,56},{16,0},{24,8},{32,16},{40,24},{48,32},{56,40},{64,11... | collective-permute-start | bytes 589832 | tf_op jit(solution)/shard_map/ppermute | solution.py:36
  17.0 7.0 %collective-permute-start.8 = (bf16[384,256]{1,0:T(8,128)(2,1)S(1)}, bf16[384,256]{1,0:T(8,128)(2,1)S(1)}, u32[]{:S(2)}, u32[]{:S(2)}) collective-permute-start(bf16[384,256]{1,0:T(8,128)(2,1)S(1)} %constant_dynamic-update-slice_fusion.rest_0_.rest_8_), channel_id=1, source_target_pairs={{0,8},{8,0},{16,24},{24,16},{32,40},{40,32},{48,56},{56,48},{64,72... | collective-permute-start | bytes 589832 | tf_op jit(solution)/shard_map/ppermute | solution.py:36
  17.9 21.4 %copy-start.9 = (bf16[384,256]{1,0:T(8,128)(2,1)}, bf16[384,256]{1,0:T(8,128)(2,1)S(1)}, u32[]{:S(2)}) copy-start(bf16[384,256]{1,0:T(8,128)(2,1)S(1)} %collective-permute-done.1.rest_1_.rest_9_) | copy-start | bytes 589828
  17.9 7.5 %collective-permute-start.5 = (bf16[384,256]{1,0:T(8,128)(2,1)S(1)}, bf16[384,256]{1,0:T(8,128)(2,1)S(1)}, u32[]{:S(2)}, u32[]{:S(2)}) collective-permute-start(bf16[384,256]{1,0:T(8,128)(2,1)S(1)} %collective-permute-done.1.rest_1_.rest_9_), channel_id=1, source_target_pairs={{0,48},{8,56},{16,0},{24,8},{32,16},{40,24},{48,32},{56,40},{64,11... | collective-permute-start | bytes 589832 | tf_op jit(solution)/shard_map/ppermute | solution.py:36
  22.1 13.4 %collective-permute-start = (bf16[384,512]{1,0:T(8,128)(2,1)}, bf16[384,512]{1,0:T(8,128)(2,1)S(1)}, u32[]{:S(2)}, u32[]{:S(2)}) collective-permute-start(bf16[384,512]{1,0:T(8,128)(2,1)} %rest_0_), channel_id=1, source_target_pairs={{0,8},{8,0},{16,24},{24,16},{32,40},{40,32},{48,56},{56,48},{64,72... | collective-permute-start | bytes 1179656 | tf_op jit(solution)/shard_map/ppermute | solution.py:36
  22.2 17.2 %copy-start.10 = (bf16[384,256]{1,0:T(8,128)(2,1)}, bf16[384,256]{1,0:T(8,128)(2,1)S(1)}, u32[]{:S(2)}) copy-start(bf16[384,256]{1,0:T(8,128)(2,1)S(1)} %collective-permute-done.2.rest_2_.rest_10_) | copy-start | bytes 589828
  22.2 9.0 %collective-permute-start.4 = (bf16[384,256]{1,0:T(8,128)(2,1)S(1)}, bf16[384,256]{1,0:T(8,128)(2,1)S(1)}, u32[]{:S(2)}, u32[]{:S(2)}) collective-permute-start(bf16[384,256]{1,0:T(8,128)(2,1)S(1)} %collective-permute-done.1.rest_1_.rest_9_), channel_id=1, source_target_pairs={{0,16},{8,24},{16,32},{24,40},{32,48},{40,56},{48,0},{56,8},{64,80... | collective-permute-start | bytes 589832 | tf_op jit(solution)/shard_map/ppermute | solution.py:36
  22.3 17.1 %copy-start.11 = (bf16[384,256]{1,0:T(8,128)(2,1)}, bf16[384,256]{1,0:T(8,128)(2,1)S(1)}, u32[]{:S(2)}) copy-start(bf16[384,256]{1,0:T(8,128)(2,1)S(1)} %collective-permute-done.3.rest_3_.rest_11_) | copy-start | bytes 589828
  22.3 12.6 %collective-permute-start.6 = (bf16[384,256]{1,0:T(8,128)(2,1)S(1)}, bf16[384,256]{1,0:T(8,128)(2,1)S(1)}, u32[]{:S(2)}, u32[]{:S(2)}) collective-permute-start(bf16[384,256]{1,0:T(8,128)(2,1)S(1)} %collective-permute-done.2.rest_2_.rest_10_), channel_id=1, source_target_pairs={{0,16},{8,24},{16,32},{24,40},{32,48},{40,56},{48,0},{56,8},{64,80... | collective-permute-start | bytes 589832 | tf_op jit(solution)/shard_map/ppermute | solution.py:36
  24.0 15.3 %copy-start.20 = (bf16[384,256]{1,0:T(8,128)(2,1)}, bf16[384,256]{1,0:T(8,128)(2,1)S(1)}, u32[]{:S(2)}) copy-start(bf16[384,256]{1,0:T(8,128)(2,1)S(1)} %collective-permute-done.8.rest_8_) | copy-start | bytes 589828
  24.0 10.9 %collective-permute-start.9 = (bf16[384,256]{1,0:T(8,128)(2,1)S(1)}, bf16[384,256]{1,0:T(8,128)(2,1)S(1)}, u32[]{:S(2)}, u32[]{:S(2)}) collective-permute-start(bf16[384,256]{1,0:T(8,128)(2,1)S(1)} %collective-permute-done.1.rest_1_.rest_9_), channel_id=1, source_target_pairs={{0,8},{8,0},{16,24},{24,16},{32,40},{40,32},{48,56},{56,48},{64,72... | collective-permute-start | bytes 589832 | tf_op jit(solution)/shard_map/ppermute | solution.py:36
  25.4 13.9 %copy-start.12 = (bf16[384,256]{1,0:T(8,128)(2,1)}, bf16[384,256]{1,0:T(8,128)(2,1)S(1)}, u32[]{:S(2)}) copy-start(bf16[384,256]{1,0:T(8,128)(2,1)S(1)} %collective-permute-done.5.rest_5_.rest_13_) | copy-start | bytes 589828
  25.4 10.0 %collective-permute-start.10 = (bf16[384,256]{1,0:T(8,128)(2,1)S(1)}, bf16[384,256]{1,0:T(8,128)(2,1)S(1)}, u32[]{:S(2)}, u32[]{:S(2)}) collective-permute-start(bf16[384,256]{1,0:T(8,128)(2,1)S(1)} %collective-permute-done.2.rest_2_.rest_10_), channel_id=1, source_target_pairs={{0,8},{8,0},{16,24},{24,16},{32,40},{40,32},{48,56},{56,48},{64,72... | collective-permute-start | bytes 589832 | tf_op jit(solution)/shard_map/ppermute | solution.py:36
  31.1 8.2 %copy-start.13 = (bf16[384,256]{1,0:T(8,128)(2,1)}, bf16[384,256]{1,0:T(8,128)(2,1)S(1)}, u32[]{:S(2)}) copy-start(bf16[384,256]{1,0:T(8,128)(2,1)S(1)} %collective-permute-done.4.rest_4_.rest_12_) | copy-start | bytes 589828
  31.2 6.1 %collective-permute-start.7 = (bf16[384,256]{1,0:T(8,128)(2,1)S(1)}, bf16[384,256]{1,0:T(8,128)(2,1)S(1)}, u32[]{:S(2)}, u32[]{:S(2)}) collective-permute-start(bf16[384,256]{1,0:T(8,128)(2,1)S(1)} %collective-permute-done.5.rest_5_.rest_13_), channel_id=1, source_target_pairs={{0,48},{8,56},{16,0},{24,8},{32,16},{40,24},{48,32},{56,40},{64,11... | collective-permute-start | bytes 589832 | tf_op jit(solution)/shard_map/ppermute | solution.py:36
  34.9 4.5 %copy-start.14 = (bf16[384,256]{1,0:T(8,128)(2,1)}, bf16[384,256]{1,0:T(8,128)(2,1)S(1)}, u32[]{:S(2)}) copy-start(bf16[384,256]{1,0:T(8,128)(2,1)S(1)} %collective-permute-done.6.rest_6_.rest_14_) | copy-start | bytes 589828
  34.9 4.3 %collective-permute-start.11 = (bf16[384,256]{1,0:T(8,128)(2,1)S(1)}, bf16[384,256]{1,0:T(8,128)(2,1)S(1)}, u32[]{:S(2)}, u32[]{:S(2)}) collective-permute-start(bf16[384,256]{1,0:T(8,128)(2,1)S(1)} %collective-permute-done.3.rest_3_.rest_11_), channel_id=1, source_target_pairs={{0,8},{8,0},{16,24},{24,16},{32,40},{40,32},{48,56},{56,48},{64,72... | collective-permute-start | bytes 589832 | tf_op jit(solution)/shard_map/ppermute | solution.py:36
  34.9 4.5 %copy-start.21 = (bf16[384,256]{1,0:T(8,128)(2,1)}, bf16[384,256]{1,0:T(8,128)(2,1)S(1)}, u32[]{:S(2)}) copy-start(bf16[384,256]{1,0:T(8,128)(2,1)S(1)} %collective-permute-done.9.rest_9_) | copy-start | bytes 589828
  34.9 4.3 %collective-permute-start.13 = (bf16[384,256]{1,0:T(8,128)(2,1)S(1)}, bf16[384,256]{1,0:T(8,128)(2,1)S(1)}, u32[]{:S(2)}, u32[]{:S(2)}) collective-permute-start(bf16[384,256]{1,0:T(8,128)(2,1)S(1)} %collective-permute-done.5.rest_5_.rest_13_), channel_id=1, source_target_pairs={{0,8},{8,0},{16,24},{24,16},{32,40},{40,32},{48,56},{56,48},{64,72... | collective-permute-start | bytes 589832 | tf_op jit(solution)/shard_map/ppermute | solution.py:36
  35.4 4.0 %copy-start.22 = (bf16[384,256]{1,0:T(8,128)(2,1)}, bf16[384,256]{1,0:T(8,128)(2,1)S(1)}, u32[]{:S(2)}) copy-start(bf16[384,256]{1,0:T(8,128)(2,1)S(1)} %collective-permute-done.10.rest_10_) | copy-start | bytes 589828
  35.4 3.8 %collective-permute-start.12 = (bf16[384,256]{1,0:T(8,128)(2,1)S(1)}, bf16[384,256]{1,0:T(8,128)(2,1)S(1)}, u32[]{:S(2)}, u32[]{:S(2)}) collective-permute-start(bf16[384,256]{1,0:T(8,128)(2,1)S(1)} %collective-permute-done.4.rest_4_.rest_12_), channel_id=1, source_target_pairs={{0,8},{8,0},{16,24},{24,16},{32,40},{40,32},{48,56},{56,48},{64,72... | collective-permute-start | bytes 589832 | tf_op jit(solution)/shard_map/ppermute | solution.py:36
  35.5 31.6 %copy-start.16 = (bf16[384,512]{1,0:T(8,128)(2,1)}, bf16[384,512]{1,0:T(8,128)(2,1)S(1)}, u32[]{:S(2)}) copy-start(bf16[384,512]{1,0:T(8,128)(2,1)S(1)} %collective-permute-done.rest_1_) | copy-start | bytes 1179652
  35.5 3.8 %collective-permute-start.14 = (bf16[384,256]{1,0:T(8,128)(2,1)S(1)}, bf16[384,256]{1,0:T(8,128)(2,1)}, u32[]{:S(2)}, u32[]{:S(2)}) collective-permute-start(bf16[384,256]{1,0:T(8,128)(2,1)S(1)} %collective-permute-done.6.rest_6_.rest_14_), channel_id=1, source_target_pairs={{0,8},{8,0},{16,24},{24,16},{32,40},{40,32},{48,56},{56,48},{64,72... | collective-permute-start | bytes 589832 | tf_op jit(solution)/shard_map/ppermute | solution.py:36
  37.2 2.2 %copy-start.15 = (bf16[384,256]{1,0:T(8,128)(2,1)}, bf16[384,256]{1,0:T(8,128)(2,1)S(1)}, u32[]{:S(2)}) copy-start(bf16[384,256]{1,0:T(8,128)(2,1)S(1)} %collective-permute-done.7.rest_7_.rest_15_) | copy-start | bytes 589828
  37.2 2.0 %collective-permute-start.15 = (bf16[384,256]{1,0:T(8,128)(2,1)S(1)}, bf16[384,256]{1,0:T(8,128)(2,1)}, u32[]{:S(2)}, u32[]{:S(2)}) collective-permute-start(bf16[384,256]{1,0:T(8,128)(2,1)S(1)} %collective-permute-done.7.rest_7_.rest_15_), channel_id=1, source_target_pairs={{0,8},{8,0},{16,24},{24,16},{32,40},{40,32},{48,56},{56,48},{64,72... | collective-permute-start | bytes 589832 | tf_op jit(solution)/shard_map/ppermute | solution.py:36
  39.2 0.7 copy-start.23
  39.2 0.7 copy-start.24
  39.3 0.8 copy-start.25
  56.3 6.4 %collective-permute-start.17 = (bf16[384,4096]{1,0:T(8,128)(2,1)}, bf16[384,4096]{1,0:T(8,128)(2,1)S(1)}, u32[]{:S(2)}, u32[]{:S(2)}) collective-permute-start(bf16[384,4096]{1,0:T(8,128)(2,1)} %all-gather.3.cloned.1.call-done.grad_own), channel_id=1, source_target_pairs={{0,8},{8,0},{16,24},{24,16},{32,40},{40,32},{48,56},{56,48},{64,72... | collective-permute-start | bytes 9437192 | tf_op jit(solution)/shard_map/ppermute | solution.py:36
  56.4 6.4 %copy-start.1 = (bf16[384,512]{1,0:T(8,128)(2,1)S(1)}, bf16[384,512]{1,0:T(8,128)(2,1)}, u32[]{:S(2)}) copy-start(bf16[384,512]{1,0:T(8,128)(2,1)} %get-tuple-element.17.attn_own.rest_4_) | copy-start | bytes 1179652
  56.4 6.4 %copy-start.3 = (s32[2]{0:T(128)S(1)}, s32[2]{0:T(128)}, u32[]{:S(2)}) copy-start(s32[2]{0:T(128)} %pad_add_fusion.ids) | copy-start | bytes 28
  56.4 6.4 %copy-start.5 = (s32[3,16]{1,0:T(4,128)S(1)}, s32[3,16]{1,0:T(4,128)}, u32[]{:S(2)}) copy-start(s32[3,16]{1,0:T(4,128)} %owners.3) | copy-start | bytes 580
  56.4 6.4 %copy-start.6 = (bf16[384,4096]{1,0:T(8,128)(2,1)S(1)}, bf16[384,4096]{1,0:T(8,128)(2,1)}, u32[]{:S(2)}) copy-start(bf16[384,4096]{1,0:T(8,128)(2,1)} %all-gather.3.cloned.1.call-done.grad_own) | copy-start | bytes 9437188
  56.4 6.3 %collective-permute-start.16 = (bf16[384,512]{1,0:T(8,128)(2,1)}, bf16[384,512]{1,0:T(8,128)(2,1)S(1)}, u32[]{:S(2)}, u32[]{:S(2)}) collective-permute-start(bf16[384,512]{1,0:T(8,128)(2,1)} %get-tuple-element.17.attn_own.rest_4_), channel_id=1, source_target_pairs={{0,8},{8,0},{16,24},{24,16},{32,40},{40,32},{48,56},{56,48},{64,72... | collective-permute-start | bytes 1179656 | tf_op jit(solution)/shard_map/ppermute | solution.py:36
  57.0 11.3 %collective-permute-start.18 = (bf16[384,512]{1,0:T(8,128)(2,1)S(1)}, bf16[384,512]{1,0:T(8,128)(2,1)S(1)}, u32[]{:S(2)}, u32[]{:S(2)}) collective-permute-start(bf16[384,512]{1,0:T(8,128)(2,1)S(1)} %copy-done.19), channel_id=1, source_target_pairs={{0,4},{1,5},{2,6},{3,7},{4,0},{5,1},{6,2},{7,3},{8,12},{9,13},{10,... | collective-permute-start | bytes 1179656 | tf_op jit(solution)/shard_map/ppermute | solution.py:59
  62.6 13.2 %copy-start.17 = (bf16[384,512]{1,0:T(8,128)(2,1)}, bf16[384,512]{1,0:T(8,128)(2,1)S(1)}, u32[]{:S(2)}) copy-start(bf16[384,512]{1,0:T(8,128)(2,1)S(1)} %convolution_convert_fusion.rest_2_) | copy-start | bytes 1179652
  62.7 4.4 %copy-start.2 = (bf16[384,512]{1,0:T(8,128)(2,1)}, bf16[384,512]{1,0:T(8,128)(2,1)S(1)}, u32[]{:S(2)}) copy-start(bf16[384,512]{1,0:T(8,128)(2,1)S(1)} %collective-permute-done.16.attn_other.rest_5_) | copy-start | bytes 1179652
  67.1 8.8 %copy-start.26 = (f32[2,8,768]{2,1,0:T(8,128)S(1)}, f32[2,8,768]{2,1,0:T(8,128)}, u32[]{:S(2)}) copy-start(f32[2,8,768]{2,1,0:T(8,128)} %get-tuple-element.21.rest_6_) | copy-start | bytes 147460
  68.3 0.9 copy-start.7
  69.2 32.7 %all-to-all-start = ((bf16[8,512,256]{2,1,0:T(8,128)(2,1)}), bf16[8,512,256]{2,1,0:T(8,128)(2,1)}, u32[]{:S(2)}, u32[]{:S(2)}) async-start(bf16[8,512,256]{2,1,0:T(8,128)(2,1)} %out_gradient.1), calls=%async_computation | async-start | bytes 4194304 | tf_op jit(solution)/shard_map/all_to_all | solution.py:362
  75.8 1.9 %collective-permute-start.19 = (bf16[384,512]{1,0:T(8,128)(2,1)S(1)}, bf16[384,512]{1,0:T(8,128)(2,1)S(1)}, u32[]{:S(2)}, u32[]{:S(2)}) collective-permute-start(bf16[384,512]{1,0:T(8,128)(2,1)S(1)} %convolution_convert_fusion.rest_2_), channel_id=1, source_target_pairs={{0,8},{8,0},{16,24},{24,16},{32,40},{40,32},{48,56},{56,48},{64,72... | collective-permute-start | bytes 1179656 | tf_op jit(solution)/shard_map/ppermute | solution.py:36
  75.9 53.7 %copy-start.4 = (s32[2]{0:T(128)S(1)}, s32[2]{0:T(128)}, u32[]{:S(2)}) copy-start(s32[2]{0:T(128)} %pad_add_fusion.ids) | copy-start | bytes 28
  75.9 1.8 %collective-permute-start.20 = (f32[2,8,768]{2,1,0:T(8,128)S(1)}, f32[2,8,768]{2,1,0:T(8,128)S(1)}, u32[]{:S(2)}, u32[]{:S(2)}) collective-permute-start(f32[2,8,768]{2,1,0:T(8,128)S(1)} %copy-done.26), channel_id=1, source_target_pairs={{0,8},{8,0},{16,24},{24,16},{32,40},{40,32},{48,56},{56,48},{64,72... | collective-permute-start | bytes 147464 | tf_op jit(solution)/shard_map/ppermute | solution.py:36
  77.7 0.6 copy-start.27
  78.3 0.8 copy-start.18
  129.6 1.9 %copy-start = (bf16[384,4096]{1,0:T(8,128)(2,1)S(1)}, bf16[384,4096]{1,0:T(8,128)(2,1)}, u32[]{:S(2)}) copy-start(bf16[384,4096]{1,0:T(8,128)(2,1)} %all-gather.5.cloned.1.call-done.hidden_ref) | copy-start | bytes 9437188
  134.6 2.7 %collective-permute-start.21 = (bf16[8,256,256]{2,1,0:T(8,128)(2,1)S(1)}, bf16[8,256,256]{2,1,0:T(8,128)(2,1)S(1)}, u32[]{:S(2)}, u32[]{:S(2)}) collective-permute-start(bf16[8,256,256]{2,1,0:T(8,128)(2,1)S(1)} %get-tuple-element.24), channel_id=1, source_target_pairs={{0,8},{8,0},{16,24},{24,16},{32,40},{40,32},{48,56},{56,48},{64,72... | collective-permute-start | bytes 3145736 | tf_op jit(solution)/shard_map/ppermute | solution.py:36
  138.7 19.3 %all-to-all-start.2 = ((bf16[8,256,256]{2,1,0:T(8,128)(2,1)}), bf16[8,256,256]{2,1,0:T(8,128)(2,1)S(1)}, u32[]{:S(2)}, u32[]{:S(2)}) async-start(bf16[8,256,256]{2,1,0:T(8,128)(2,1)} %add_convert_fusion), calls=%async_computation.2 | async-start | bytes 2097152 | tf_op jit(solution)/shard_map/all_to_all | solution.py:362
Sparse Core Ops, SparseCore 0:
  9.7 46.6 all-gather.2
  69.3 39.3 all-gather.4
